TPU v7x, 512 devices: a whole 4x4x16 slice. The times are simulated.
512 devices in a mesh: sx: 64 (over z, y), sy: 8 (over x, core).
Axes of the slice: x: 4, y: 4, z: 16, core: 2. Of those that a mesh axis runs over, the one named last changes fastest.
Arguments:
- frames: bfloat16 [2, 128, 2048, 8], P(None, 'sy', 'sx'), may hold values from -6 to 6
- hidden_init: bfloat16 [128, 2048, 256], P('sy', 'sx'), may hold values from -1 to 1
- cell_init: float32 [128, 2048, 256], P('sy', 'sx'), may hold values from -6 to 6
- conv_weight: bfloat16 [9, 264, 1024], P(None, None, 'sx'), may hold values from -0.125 to 0.125
- gate_offsets_bias: float32 [1024], replicated, may hold values from -3 to 3
- land_mask: int32 [128, 2048], P('sy', 'sx'), may hold values 0 or 1
- projection_coefficients: bfloat16 [256], replicated, may hold values from -0.375 to 0.375
Outputs:
- hidden_out: bfloat16 [128, 2048, 256], P('sy', 'sx')
- cell_out: float32 [128, 2048, 256], P('sy', 'sx')
- predicted_flux: float32 [128, 2048], P('sy', 'sx')
All inputs are finite; a program needn't handle non-finite values. No bound on the sum of `land_mask` on one device may be relied on, other than what follows from the above.
Results may differ from a plain program's by a relative error of at most 0.0046.
Values may be sent and summed in bfloat16 or wider, within the bound.
No kernel may reach another device: no remote copies, remote signals or barrier semaphores. Data moves between devices by JAX's collectives and lax.ppermute only.
A program may use at most 64 MiB of HBM per device.

v0:
```python
import jax
import jax.numpy as jnp
from jax import lax
from jax.sharding import PartitionSpec as P


def padded_2(block, sides, width):
    for axis, dim in sides:
        count = lax.axis_size(axis)
        forward = [(i, i + 1) for i in range(count - 1)]
        backward = [(target, source) for source, target in forward]
        low = lax.ppermute(
            lax.slice_in_dim(block, block.shape[dim] - width, None, axis=dim), axis, forward
        )
        high = lax.ppermute(lax.slice_in_dim(block, 0, width, axis=dim), axis, backward)
        block = jnp.concatenate([low, block, high], axis=dim)
    return block


def make_patch_columns(padded, rows, cols):
    pieces = [padded[a : a + rows, b : b + cols, :] for a in range(3) for b in range(3)]
    return jnp.concatenate(pieces, -1).reshape(rows * cols, -1)


def body(
    frames,
    hidden_init,
    cell_init,
    conv_weight,
    gate_offsets_bias,
    land_mask,
    projection_coefficients,
):
    rows, cols, width = (hidden_init.shape[0], hidden_init.shape[1], hidden_init.shape[2])
    steps = frames.shape[0]
    kept_locations = land_mask.astype(jnp.float32)[:, :, None]
    latent_carry, memory_carry = (hidden_init, cell_init)
    for step in range(steps):
        inputs = jnp.concatenate([frames[step], latent_carry], -1)
        padded = padded_2(inputs, (("sy", 0), ("sx", 1)), 1)
        patches = make_patch_columns(padded, rows, cols)

        def columns(piece, start, patches=patches):
            return jnp.dot(
                patches, piece.reshape(-1, piece.shape[2]), preferred_element_type=jnp.float32
            )

        gates = columns(lax.all_gather(conv_weight, "sx", axis=2, tiled=True), jnp.int32(0))
        gates = gates.reshape(rows, cols, -1) + gate_offsets_bias
        in_gate = jax.nn.sigmoid(gates[..., :width])
        decay_factor = jax.nn.sigmoid(gates[..., width : 2 * width])
        candidate = jnp.tanh(gates[..., 2 * width : 3 * width])
        out_gate = jax.nn.sigmoid(gates[..., 3 * width :])
        memory_carry = decay_factor * memory_carry + in_gate * candidate
        latent_carry = (kept_locations * out_gate * jnp.tanh(memory_carry)).astype(jnp.bfloat16)
    predicted_flux = (
        jnp.dot(latent_carry, projection_coefficients, preferred_element_type=jnp.float32)
        * kept_locations[:, :, 0]
    )
    return (latent_carry, memory_carry, predicted_flux)


def solution(mesh):
    in_specs = (
        P(None, "sy", "sx", None),
        P("sy", "sx", None),
        P("sy", "sx", None),
        P(None, None, "sx"),
        P(),
        P("sy", "sx"),
        P(),
    )
    out_specs = (P("sy", "sx", None), P("sy", "sx", None), P("sy", "sx"))
    return jax.shard_map(body, mesh=mesh, in_specs=in_specs, out_specs=out_specs, check_vma=False)
```

profile of v0, /device:TPU:129, one launch (start us, length us, event | category | flops | bytes accessed | tf_op | source)
XLA Modules:
  0.0 222.8 jit_solution(6742163712033121217)
XLA Ops:
  7.2 0.0 copy-start
  7.2 0.0 all-gather.2.cloned.1.call-start
  7.2 0.7 all-gather.2.cloned.1.call-update
  7.9 0.8 fusion.36
  8.7 0.1 copy.15
  8.8 0.8 pad_maximum_fusion.21
  9.6 3.7 %collective-permute-start = (bf16[1,32,264]{2,1,0:T(8,128)(2,1)S(1)}, bf16[1,32,264]{2,1,0:T(8,128)(2,1)S(1)}, u32[]{:S(2)}, u32[]{:S(2)}) collective-permute-start(bf16[1,32,264]{2,1,0:T(8,128)(2,1)S(1)} %get-tuple-element.33), channel_id=1, source_target_pairs={{0,1},{1,2},{2,3},{3,4},{4,5},{5,6},{6,7},{8,9},{9,10},{10,11},{11... | collective-permute-start | bytes 50696 | tf_op jit(solution)/shard_map/ppermute | solution.py:12
  13.3 1.9 collective-permute-start.1
  15.3 0.7 convert_element_type.9
  16.0 0.1 copy.14
  16.1 0.0 collective-permute-done
  16.1 2.4 %collective-permute-done.1 = bf16[1,32,264]{2,1,0:T(8,128)(2,1)S(1)} collective-permute-done((bf16[1,32,264]{2,1,0:T(8,128)(2,1)S(1)}, bf16[1,32,264]{2,1,0:T(8,128)(2,1)S(1)}, u32[]{:S(2)}, u32[]{:S(2)}) %collective-permute-start.1) | collective-permute-done | bytes 16928 | tf_op jit(solution)/shard_map/ppermute | solution.py:15
  18.5 0.1 pad_maximum_fusion.14
  18.6 4.2 %collective-permute-start.3 = (bf16[18,1,264]{2,1,0:T(2,128)(2,1)S(1)}, bf16[18,1,264]{2,1,0:T(2,128)(2,1)S(1)}, u32[]{:S(2)}, u32[]{:S(2)}) collective-permute-start(bf16[18,1,264]{2,1,0:T(2,128)(2,1)S(1)} %get-tuple-element.25), channel_id=1, source_target_pairs={{8,0},{16,8},{24,16},{32,24},{40,32},{48,40},{56,48},{64,56},{72,6... | collective-permute-start | bytes 28520 | tf_op jit(solution)/shard_map/ppermute | solution.py:15
  22.8 1.9 collective-permute-start.2
  24.7 1.2 pad_maximum_fusion.6
  25.9 0.0 collective-permute-done.3
  25.9 4.8 %collective-permute-done.2 = bf16[18,1,264]{2,1,0:T(2,128)(2,1)S(1)} collective-permute-done((bf16[18,1,264]{2,1,0:T(2,128)(2,1)S(1)}, bf16[18,1,264]{2,1,0:T(2,128)(2,1)S(1)}, u32[]{:S(2)}, u32[]{:S(2)}) %collective-permute-start.2) | collective-permute-done | bytes 9536 | tf_op jit(solution)/shard_map/ppermute | solution.py:12
  30.7 0.5 pad_maximum_fusion
  31.2 1.4 fusion.34
  32.6 4.8 %concatenate.64 = bf16[16,32,2376]{2,1,0:T(8,128)(2,1)S(1)} concatenate(bf16[16,32,264]{2,1,0:T(8,128)(2,1)} %get-tuple-element.37, bf16[16,32,264]{2,1,0:T(8,128)(2,1)} %get-tuple-element.32, bf16[16,32,264]{2,1,0:T(8,128)(2,1)} %get-tuple-element.15, bf16[16,32,264]{2,1,0:T(8,128)(2,1)} %get-tuple-element.38, bf16[16,32,8]{2,1,0:T(8,128)(2,1)S(1)} %bitcast.24, ...), dimensions={2} | concatenate | bytes 4866048 | tf_op jit(solution)/shard_map/concatenate | solution.py:22
  37.4 0.0 copy-start.4
  37.4 120.9 %all-gather.2.cloned.1.call-done = bf16[9,264,1024]{1,2,0:T(8,128)(2,1)} async-done(((bf16[9,264,16]{1,2,0:T(8,128)(2,1)}), bf16[9,264,1024]{1,2,0:T(8,128)(2,1)}) %all-gather.2.cloned.1.call-update) | async-done | bytes 4866064 | tf_op jit(solution)/shard_map/all_gather | solution.py:48
  158.3 8.5 %copy.12 = bf16[9,264,1024]{2,1,0:T(8,128)(2,1)} copy(bf16[9,264,1024]{1,2,0:T(8,128)(2,1)} %all-gather.2.cloned.1.call-done) | data formatting | bytes 9732096 | tf_op jit(solution)/shard_map/all_gather | solution.py:48
  166.8 4.8 %convolution_add_fusion.1 = f32[16,32,1024]{2,1,0:T(8,128)S(1)} fusion(bf16[16,32,2376]{2,1,0:T(8,128)(2,1)S(1)} %concatenate.64, bf16[2376,1024,1]{1,0,2:T(8,128)(2,1)} %bitcast.13, f32[1024]{0:T(1024)S(1)} %copy-done.4), kind=kOutput, calls=%fused_computation.1 | convolution fusion | flops 2491940864 | bytes 9400320 | tf_op jit(solution)/shard_map/dot_general | solution.py:44
  171.6 0.0 copy-done.2
  171.6 0.0 copy-start.5
  171.7 0.6 fusion.28
  172.2 0.1 pad_maximum_fusion.19
  172.3 11.5 %collective-permute-start.4 = (bf16[1,32,264]{2,1,0:T(8,128)(2,1)S(1)}, bf16[1,32,264]{2,1,0:T(8,128)(2,1)S(1)}, u32[]{:S(2)}, u32[]{:S(2)}) collective-permute-start(bf16[1,32,264]{2,1,0:T(8,128)(2,1)S(1)} %get-tuple-element.29), channel_id=1, source_target_pairs={{0,1},{1,2},{2,3},{3,4},{4,5},{5,6},{6,7},{8,9},{9,10},{10,11},{11... | collective-permute-start | bytes 50696 | tf_op jit(solution)/shard_map/ppermute | solution.py:12
  183.8 1.9 collective-permute-start.5
  185.7 0.0 collective-permute-done.4
  185.8 3.2 %collective-permute-done.5 = bf16[1,32,264]{2,1,0:T(8,128)(2,1)S(1)} collective-permute-done((bf16[1,32,264]{2,1,0:T(8,128)(2,1)S(1)}, bf16[1,32,264]{2,1,0:T(8,128)(2,1)S(1)}, u32[]{:S(2)}, u32[]{:S(2)}) %collective-permute-start.5) | collective-permute-done | bytes 16928 | tf_op jit(solution)/shard_map/ppermute | solution.py:15
  188.9 0.1 pad_maximum_fusion.10
  189.1 4.4 %collective-permute-start.7 = (bf16[18,1,264]{2,1,0:T(2,128)(2,1)S(1)}, bf16[18,1,264]{2,1,0:T(2,128)(2,1)S(1)}, u32[]{:S(2)}, u32[]{:S(2)}) collective-permute-start(bf16[18,1,264]{2,1,0:T(2,128)(2,1)S(1)} %get-tuple-element.21), channel_id=1, source_target_pairs={{8,0},{16,8},{24,16},{32,24},{40,32},{48,40},{56,48},{64,56},{72,6... | collective-permute-start | bytes 28520 | tf_op jit(solution)/shard_map/ppermute | solution.py:15
  193.5 1.9 collective-permute-start.6
  195.4 1.2 pad_maximum_fusion.2
  196.7 0.0 collective-permute-done.7
  196.7 4.8 %collective-permute-done.6 = bf16[18,1,264]{2,1,0:T(2,128)(2,1)S(1)} collective-permute-done((bf16[18,1,264]{2,1,0:T(2,128)(2,1)S(1)}, bf16[18,1,264]{2,1,0:T(2,128)(2,1)S(1)}, u32[]{:S(2)}, u32[]{:S(2)}) %collective-permute-start.6) | collective-permute-done | bytes 9536 | tf_op jit(solution)/shard_map/ppermute | solution.py:12
  201.4 0.5 pad_maximum_fusion.1
  201.9 1.1 fusion.32
  203.0 1.1 fusion.33
  204.1 4.9 %concatenate.71 = bf16[16,32,2376]{2,1,0:T(8,128)(2,1)S(1)} concatenate(bf16[16,32,264]{2,1,0:T(8,128)(2,1)} %get-tuple-element.12, bf16[16,32,264]{2,1,0:T(8,128)(2,1)} %get-tuple-element.28, bf16[16,32,264]{2,1,0:T(8,128)(2,1)} %get-tuple-element.9, bf16[16,32,264]{2,1,0:T(8,128)(2,1)} %get-tuple-element.11, bf16[16,32,8]{2,1,0:T(8,128)(2,1)S(1)} %bitcast.19, ...), dimensions={2} | concatenate | bytes 4866048 | tf_op jit(solution)/shard_map/concatenate | solution.py:22
  209.0 4.8 %convolution_add_fusion = f32[16,32,1024]{2,1,0:T(8,128)S(1)} fusion(bf16[16,32,2376]{2,1,0:T(8,128)(2,1)S(1)} %concatenate.71, bf16[2376,1024,1]{1,0,2:T(8,128)(2,1)} %bitcast.14, f32[1024]{0:T(1024)S(1)} %copy-done.4), kind=kOutput, calls=%fused_computation | convolution fusion | flops 2491940864 | bytes 9400320 | tf_op jit(solution)/shard_map/dot_general | solution.py:44
  213.7 0.0 copy-start.3
  213.8 1.4 fusion.29
  215.1 0.3 fusion.37
  215.4 0.6 convert_multiply_fusion
  (8 shorter events, 0.0 us)
Async XLA Ops:
  7.2 11.3 %copy-start = (bf16[16,32,256]{2,1,0:T(8,128)(2,1)S(1)}, bf16[16,32,256]{2,1,0:T(8,128)(2,1)}, u32[]{:S(2)}) copy-start(bf16[16,32,256]{2,1,0:T(8,128)(2,1)} %param.8) | copy-start | bytes 786436
  7.2 151.2 %all-gather.2.cloned.1.call-start = ((), (), s32[]{:S(2)}) async-start(), calls=%async_computation | async-start | bytes 7188480 | tf_op jit(solution)/shard_map/all_gather | solution.py:48
  9.6 6.4 %collective-permute-start = (bf16[1,32,264]{2,1,0:T(8,128)(2,1)S(1)}, bf16[1,32,264]{2,1,0:T(8,128)(2,1)S(1)}, u32[]{:S(2)}, u32[]{:S(2)}) collective-permute-start(bf16[1,32,264]{2,1,0:T(8,128)(2,1)S(1)} %get-tuple-element.33), channel_id=1, source_target_pairs={{0,1},{1,2},{2,3},{3,4},{4,5},{5,6},{6,7},{8,9},{9,10},{10,11},{11... | collective-permute-start | bytes 50696 | tf_op jit(solution)/shard_map/ppermute | solution.py:12
  13.3 5.1 %collective-permute-start.1 = (bf16[1,32,264]{2,1,0:T(8,128)(2,1)S(1)}, bf16[1,32,264]{2,1,0:T(8,128)(2,1)S(1)}, u32[]{:S(2)}, u32[]{:S(2)}) collective-permute-start(bf16[1,32,264]{2,1,0:T(8,128)(2,1)S(1)} %get-tuple-element.34), channel_id=1, source_target_pairs={{1,0},{2,1},{3,2},{4,3},{5,4},{6,5},{7,6},{9,8},{10,9},{11,10},{12... | collective-permute-start | bytes 50696 | tf_op jit(solution)/shard_map/ppermute | solution.py:15
  18.6 7.3 %collective-permute-start.3 = (bf16[18,1,264]{2,1,0:T(2,128)(2,1)S(1)}, bf16[18,1,264]{2,1,0:T(2,128)(2,1)S(1)}, u32[]{:S(2)}, u32[]{:S(2)}) collective-permute-start(bf16[18,1,264]{2,1,0:T(2,128)(2,1)S(1)} %get-tuple-element.25), channel_id=1, source_target_pairs={{8,0},{16,8},{24,16},{32,24},{40,32},{48,40},{56,48},{64,56},{72,6... | collective-permute-start | bytes 28520 | tf_op jit(solution)/shard_map/ppermute | solution.py:15
  22.8 7.9 %collective-permute-start.2 = (bf16[18,1,264]{2,1,0:T(2,128)(2,1)S(1)}, bf16[18,1,264]{2,1,0:T(2,128)(2,1)S(1)}, u32[]{:S(2)}, u32[]{:S(2)}) collective-permute-start(bf16[18,1,264]{2,1,0:T(2,128)(2,1)S(1)} %get-tuple-element.26), channel_id=1, source_target_pairs={{0,8},{8,16},{16,24},{24,32},{32,40},{40,48},{48,56},{56,64},{64,7... | collective-permute-start | bytes 28520 | tf_op jit(solution)/shard_map/ppermute | solution.py:12
  37.4 129.4 %copy-start.4 = (f32[1024]{0:T(1024)S(1)}, f32[1024]{0:T(1024)}, u32[]{:S(2)}) copy-start(f32[1024]{0:T(1024)} %param.11) | copy-start | bytes 12292
  166.8 4.8 %copy-start.2 = (f32[16,32,256]{2,1,0:T(8,128)S(1)}, f32[16,32,256]{2,1,0:T(8,128)}, u32[]{:S(2)}) copy-start(f32[16,32,256]{2,1,0:T(8,128)} %param.9) | copy-start | bytes 1572868
  171.6 14.1 %copy-start.5 = (bf16[256]{0:T(256)(128)(2,1)S(1)}, bf16[256]{0:T(256)(128)(2,1)}, u32[]{:S(2)}) copy-start(bf16[256]{0:T(256)(128)(2,1)} %param.13) | copy-start | bytes 1540
  172.3 13.4 %collective-permute-start.4 = (bf16[1,32,264]{2,1,0:T(8,128)(2,1)S(1)}, bf16[1,32,264]{2,1,0:T(8,128)(2,1)S(1)}, u32[]{:S(2)}, u32[]{:S(2)}) collective-permute-start(bf16[1,32,264]{2,1,0:T(8,128)(2,1)S(1)} %get-tuple-element.29), channel_id=1, source_target_pairs={{0,1},{1,2},{2,3},{3,4},{4,5},{5,6},{6,7},{8,9},{9,10},{10,11},{11... | collective-permute-start | bytes 50696 | tf_op jit(solution)/shard_map/ppermute | solution.py:12
  183.8 5.1 %collective-permute-start.5 = (bf16[1,32,264]{2,1,0:T(8,128)(2,1)S(1)}, bf16[1,32,264]{2,1,0:T(8,128)(2,1)S(1)}, u32[]{:S(2)}, u32[]{:S(2)}) collective-permute-start(bf16[1,32,264]{2,1,0:T(8,128)(2,1)S(1)} %get-tuple-element.30), channel_id=1, source_target_pairs={{1,0},{2,1},{3,2},{4,3},{5,4},{6,5},{7,6},{9,8},{10,9},{11,10},{12... | collective-permute-start | bytes 50696 | tf_op jit(solution)/shard_map/ppermute | solution.py:15
  189.1 7.6 %collective-permute-start.7 = (bf16[18,1,264]{2,1,0:T(2,128)(2,1)S(1)}, bf16[18,1,264]{2,1,0:T(2,128)(2,1)S(1)}, u32[]{:S(2)}, u32[]{:S(2)}) collective-permute-start(bf16[18,1,264]{2,1,0:T(2,128)(2,1)S(1)} %get-tuple-element.21), channel_id=1, source_target_pairs={{8,0},{16,8},{24,16},{32,24},{40,32},{48,40},{56,48},{64,56},{72,6... | collective-permute-start | bytes 28520 | tf_op jit(solution)/shard_map/ppermute | solution.py:15
  193.5 7.9 %collective-permute-start.6 = (bf16[18,1,264]{2,1,0:T(2,128)(2,1)S(1)}, bf16[18,1,264]{2,1,0:T(2,128)(2,1)S(1)}, u32[]{:S(2)}, u32[]{:S(2)}) collective-permute-start(bf16[18,1,264]{2,1,0:T(2,128)(2,1)S(1)} %get-tuple-element.22), channel_id=1, source_target_pairs={{0,8},{8,16},{16,24},{24,32},{32,40},{40,48},{48,56},{56,64},{64,7... | collective-permute-start | bytes 28520 | tf_op jit(solution)/shard_map/ppermute | solution.py:12
  213.7 1.6 copy-start.3
  215.1 0.9 copy-start.1
Sparse Core Ops, SparseCore 0:
  11.0 147.3 all-gather.1
where the time goes:
time: 224 us; the launch traced here: 223 us
  waiting for transfers between devices  137 us (61%)
  starting transfers between devices  31.5 us (14%)
  local copies, waits for them, and re-layouts  22.8 us (10%)
  between operations  14.2 us (6%)
  matrix products  9.85 us (4%)
  other arithmetic  7.71 us (3%)
    all_gather x1, waiting for transfers between devices, body(): lax.all_gather(conv_weight, 'sx', axis=2, tiled=True)  121 us
    ppermute x4, starting transfers between devices, padded_2(): lax.ppermute(lax.slice_in_dim(block, block.shape[dim] - width, None, axis...  19 us
    ppermute x4, starting transfers between devices, padded_2(): lax.ppermute(lax.slice_in_dim(block, 0, width, axis=dim), axis, backward)  12.5 us
    concatenate x2, local copies, waits for them, and re-layouts, make_patch_columns(): return jnp.concatenate(pieces, -1).reshape(rows * cols, -1)  9.66 us
    ppermute x4, waiting for transfers between devices, padded_2(): lax.ppermute(lax.slice_in_dim(block, block.shape[dim] - width, None, axis...  9.59 us
    dot_general x2, matrix products, columns(): jnp.dot(patches, piece.reshape(-1, piece.shape[2]), preferred_element_typ...  9.58 us
    all_gather x1, local copies, waits for them, and re-layouts, body(): lax.all_gather(conv_weight, 'sx', axis=2, tiled=True)  8.47 us
    ppermute x4, waiting for transfers between devices, padded_2(): lax.ppermute(lax.slice_in_dim(block, 0, width, axis=dim), axis, backward)  5.57 us
  transfers between devices with their start and end apart: 9, of which 5 were waited for; matrix products, arithmetic and copies ran while one was open for 5% of the time, Pallas kernels for 0%

commit v1 on v0

v1 whole, which is shorter than its diff:
```python
import jax
import jax.numpy as jnp
from jax import lax
from jax.sharding import Mesh, PartitionSpec as P

KPAD = 2560
HID = 256


def pack_weights(conv_weight):
    taps, cin, cols = conv_weight.shape
    cx = cin - HID
    flipped = jnp.transpose(conv_weight, (2, 0, 1))
    hidden = flipped[:, :, cx:].reshape(cols, taps * HID)
    frame = flipped[:, :, :cx].reshape(cols, taps * cx)
    packed = jnp.concatenate([hidden, frame], axis=1)
    return jnp.pad(packed, ((0, 0), (0, KPAD - packed.shape[1])))


def spread(block, axes):
    count = lax.axis_size(axes)
    copies = jnp.broadcast_to(block[None], (count,) + block.shape)
    return lax.all_to_all(copies, axes, 0, 0)


def shifted(block, axes, step):
    count = lax.axis_size(axes)
    pairs = [(i, i + step) for i in range(count) if 0 <= i + step < count]
    return lax.ppermute(block, axes, pairs)


def widened(block, width):
    for axes, dim in ((("x", "c"), 0), (("z", "y"), 1)):
        size = block.shape[dim]
        low = shifted(lax.slice_in_dim(block, size - width, size, axis=dim), axes, 1)
        high = shifted(lax.slice_in_dim(block, 0, width, axis=dim), axes, -1)
        block = jnp.concatenate([low, block, high], axis=dim)
    return block


def patches_of(hidden, frame):
    rows, cols = hidden.shape[0] - 2, hidden.shape[1] - 2
    pieces = [hidden[a : a + rows, b : b + cols] for a in range(3) for b in range(3)]
    pieces += [frame[a : a + rows, b : b + cols] for a in range(3) for b in range(3)]
    out = jnp.concatenate(pieces, -1)
    out = jnp.pad(out, ((0, 0), (0, 0), (0, KPAD - out.shape[2])))
    return out.reshape(rows * cols, KPAD)


def cell_update(patches, weight, bias, cell, keep):
    rows, cols, width = cell.shape
    gates = lax.dot_general(
        patches, weight, (((1,), (1,)), ((), ())), preferred_element_type=jnp.float32
    )
    gates = gates.reshape(rows, cols, -1) + bias
    in_gate = jax.nn.sigmoid(gates[..., :width])
    decay_factor = jax.nn.sigmoid(gates[..., width : 2 * width])
    candidate = jnp.tanh(gates[..., 2 * width : 3 * width])
    out_gate = jax.nn.sigmoid(gates[..., 3 * width :])
    cell = decay_factor * cell + in_gate * candidate
    return (keep[..., None] * out_gate * jnp.tanh(cell)).astype(jnp.bfloat16), cell


def body(frames, hidden_init, cell_init, conv_weight, bias, land_mask, projection):
    rows, cols, width = hidden_init.shape
    cx = frames.shape[3]
    x, c = lax.axis_index("x"), lax.axis_index("c")
    packed = pack_weights(conv_weight)
    unit = lax.dynamic_slice(packed, (c * 8, x * (KPAD // 4)), (8, KPAD // 4))
    by_z = spread(unit, "z")
    by_z, frames, hidden_init, cell_init, land_mask = lax.optimization_barrier(
        (by_z, frames, hidden_init, cell_init, land_mask)
    )
    by_yx = spread(by_z, ("y", "x"))
    half = by_yx.reshape(4, 4, 16, 8, KPAD // 4)
    other = lax.ppermute(half, "c", [(0, 1), (1, 0)])
    first = jnp.where(c == 0, half, other)
    second = jnp.where(c == 0, other, half)
    weight = jnp.transpose(jnp.stack([first, second]), (3, 1, 0, 4, 2, 5)).reshape(1024, KPAD)

    keep = land_mask.astype(jnp.float32)
    packed_state = jnp.concatenate(
        [
            hidden_init,
            cell_init.astype(jnp.bfloat16),
            frames[0],
            frames[1],
            land_mask.astype(jnp.bfloat16)[..., None],
        ],
        axis=-1,
    )
    wide = widened(packed_state, 2)
    hidden = wide[..., :width]
    frame0 = wide[..., 2 * width : 2 * width + cx]
    frame1 = wide[..., 2 * width + cx : 2 * width + 2 * cx]
    keep_wide = wide[1:-1, 1:-1, 2 * width + 2 * cx].astype(jnp.float32)
    cell_wide = wide[1:-1, 1:-1, width : 2 * width].astype(jnp.float32)
    cell_wide = lax.dynamic_update_slice(cell_wide, cell_init, (1, 1, 0))

    hidden, cell = cell_update(patches_of(hidden, frame0), weight, bias, cell_wide, keep_wide)
    hidden, cell = cell_update(
        patches_of(hidden, frame1[1:-1, 1:-1]), weight, bias, cell[1:-1, 1:-1], keep
    )
    flux = jnp.dot(hidden, projection, preferred_element_type=jnp.float32) * keep
    return hidden, cell, flux


def solution(mesh):
    split = Mesh(mesh.devices.reshape(16, 4, 4, 2), ("z", "y", "x", "c"))
    sx, sy = ("z", "y"), ("x", "c")
    in_specs = (
        P(None, sy, sx, None),
        P(sy, sx, None),
        P(sy, sx, None),
        P(None, None, sx),
        P(),
        P(sy, sx),
        P(),
    )
    out_specs = (P(sy, sx, None), P(sy, sx, None), P(sy, sx))
    return jax.shard_map(body, mesh=split, in_specs=in_specs, out_specs=out_specs, check_vma=False)
```

time: 224 us -> 146 us (0.65)
  waiting for transfers between devices: 137 us -> 8.52 us
  blocking collectives: 0 us -> 60.8 us
  between operations: 14.2 us -> 0.92 us
  starting transfers between devices: 31.5 us -> 18.3 us
  local copies, waits for them, and re-layouts: 22.8 us -> 35.8 us
  other arithmetic: 7.71 us -> 11.1 us
    all_gather x1 -> x0, waiting for transfers between devices: 121 us -> none  [body(): lax.all_gather(conv_weight, 'sx', axis=2, tiled=True)]
    all_to_all x0 -> x2, blocking collectives: none -> 60.8 us  [spread(): return lax.all_to_all(copies, axes, 0, 0)]
    ppermute x8 -> x5, starting transfers between devices: 31.4 us -> 18.3 us  [the longest x4 11.9 us: shifted(): return lax.ppermute(block, axes, pairs)]
    all_gather x1 -> x0, local copies, waits for them, and re-layouts: 8.47 us -> none  [body(): lax.all_gather(conv_weight, 'sx', axis=2, tiled=True)]
    ppermute x8 -> x5, waiting for transfers between devices: 15.2 us -> 8.52 us  [the longest x4 8.52 us: shifted(): return lax.ppermute(block, axes, pairs)]
    unnamed x15 -> x42, local copies, waits for them, and re-layouts: 0.28 us -> 5.92 us
    slice x4 -> x8, local copies, waits for them, and re-layouts: 4.41 us -> 9.18 us  [the longest x3 4.74 us: patches_of(): frame[a:a + rows, b:b + cols]]
    dynamic_update_slice x0 -> x1, local copies, waits for them, and re-layouts: none -> 3.5 us  [body(): cell_wide = lax.dynamic_update_slice(cell_wide, cell_init, (1, 1, 0))]
  transfers between devices with their start and end apart: 9 -> 5, of which waited for: 5 -> 2; matrix products, arithmetic and copies ran while one was open for 5% -> 19% of each run, Pallas kernels for 0% -> 0%
where the time goes in v1:
time: 146 us; the launch traced here: 145 us
  blocking collectives  60.8 us (42%)
  local copies, waits for them, and re-layouts  35.8 us (25%)
  starting transfers between devices  18.3 us (13%)
  other arithmetic  11.1 us (8%)
  matrix products  9.17 us (6%)
  waiting for transfers between devices  8.52 us (6%)
    all_to_all x2, blocking collectives, spread(): return lax.all_to_all(copies, axes, 0, 0)  60.8 us
    ppermute x4, starting transfers between devices, shifted(): return lax.ppermute(block, axes, pairs)  11.9 us
    concatenate x2, local copies, waits for them, and re-layouts, patches_of(): out = jnp.concatenate(pieces, -1)  10.9 us
    dot_general x2, matrix products, cell_update(): lax.dot_general(patches, weight, (((1,), (1,)), ((), ())), preferred_elem...  8.9 us
    ppermute x4, waiting for transfers between devices, shifted(): return lax.ppermute(block, axes, pairs)  8.52 us
    ppermute x1, starting transfers between devices, body(): other = lax.ppermute(half, 'c', [(0, 1), (1, 0)])  6.42 us
    unnamed x42, local copies, waits for them, and re-layouts  5.92 us
    slice x3, local copies, waits for them, and re-layouts, patches_of(): frame[a:a + rows, b:b + cols]  4.74 us
  transfers between devices with their start and end apart: 5, of which 2 were waited for; matrix products, arithmetic and copies ran while one was open for 19% of the time, Pallas kernels for 0%

profile of v1, /device:TPU:129, one launch (start us, length us, event | category | flops | bytes accessed | tf_op | source)
XLA Modules:
  0.0 144.7 jit_solution(9114584831492846016)
XLA Ops:
  0.6 0.8 slice.274
  1.4 1.0 slice_bitcast_fusion.2
  2.4 0.1 copy.21
  2.5 0.1 copy.22
  2.7 23.7 %all_to_all.10 = bf16[16,8,640]{2,1,0:T(8,128)(2,1)S(1)} all-to-all(bf16[16,8,640]{2,1,0:T(8,128)(2,1)S(1)} %broadcast_in_dim.6), channel_id=1, replica_groups=mesh['z'=16,'y'=4,'x'=4,'c'=2] {'z'}, dimensions={0} | all-to-all | bytes 327680 | tf_op jit(solution)/shard_map/all_to_all | solution.py:23
  26.3 0.3 broadcast_in_dim.8
  26.6 37.2 %all_to_all.11 = bf16[16,16,8,640]{3,2,1,0:T(8,128)(2,1)S(1)} all-to-all(bf16[16,16,8,640]{3,2,1,0:T(8,128)(2,1)S(1)} %broadcast_in_dim.8), channel_id=1, replica_groups=mesh['z'=16,'y'=4,'x'=4,'c'=2] {'y','x'}, dimensions={0} | all-to-all | bytes 5242880 | tf_op jit(solution)/shard_map/all_to_all | solution.py:23
  63.8 1.8 %copy.27 = bf16[4,4,16,8,640]{4,3,1,0,2:T(8,128)(2,1)} copy(bf16[4,4,16,8,640]{4,3,2,1,0:T(8,128)(2,1)S(1)} %bitcast.29) | data formatting | bytes 5242880 | tf_op jit(solution)/shard_map/reshape | solution.py:75
  65.7 6.4 %collective-permute-start.4 = (bf16[4,4,16,8,640]{4,3,1,0,2:T(8,128)(2,1)}, bf16[4,4,16,8,640]{4,3,1,0,2:T(8,128)(2,1)}, u32[]{:S(2)}, u32[]{:S(2)}) collective-permute-start(bf16[4,4,16,8,640]{4,3,1,0,2:T(8,128)(2,1)} %copy.27), channel_id=1, source_target_pairs={{0,1},{1,0},{2,3},{3,2},{4,5},{5,4},{6,7},{7,6},{8,9},{9,8},{10,11... | collective-permute-start | bytes 7864328 | tf_op jit(solution)/shard_map/ppermute | solution.py:76
  72.1 0.2 copy.25
  72.3 0.8 copy.23
  73.2 0.7 convert_element_type.27
  73.9 1.6 %slice_bitcast_fusion = (bf16[16,32,8]{2,1,0:T(8,128)(2,1)S(1)}, bf16[16,32,8]{2,1,0:T(8,128)(2,1)}) fusion(bf16[2,16,32,8]{3,2,1,0:T(8,128)(2,1)} %copy.23), kind=kLoop, calls=%fused_computation.54 | loop fusion | bytes 32768 | tf_op jit(solution)/shard_map/squeeze | solution.py:87
  75.5 1.3 concatenate.47
  76.9 0.7 fusion.53
  77.5 2.3 %collective-permute-start = (bf16[2,32,529]{2,1,0:T(8,128)(2,1)}, bf16[2,32,529]{2,1,0:T(8,128)(2,1)S(1)}, u32[]{:S(2)}, u32[]{:S(2)}) collective-permute-start(bf16[2,32,529]{2,1,0:T(8,128)(2,1)} %get-tuple-element.50), channel_id=1, source_target_pairs={{0,1},{1,2},{2,3},{3,4},{4,5},{5,6},{6,7},{8,9},{9,10},{10,11},{11... | collective-permute-start | bytes 203144 | tf_op jit(solution)/shard_map/ppermute | solution.py:29
  79.8 2.1 %collective-permute-start.1 = (bf16[2,32,529]{2,1,0:T(8,128)(2,1)S(1)}, bf16[2,32,529]{2,1,0:T(8,128)(2,1)S(1)}, u32[]{:S(2)}, u32[]{:S(2)}) collective-permute-start(bf16[2,32,529]{2,1,0:T(8,128)(2,1)S(1)} %get-tuple-element.51), channel_id=1, source_target_pairs={{1,0},{2,1},{3,2},{4,3},{5,4},{6,5},{7,6},{9,8},{10,9},{11,10},{12... | collective-permute-start | bytes 203144 | tf_op jit(solution)/shard_map/ppermute | solution.py:29
  81.9 0.6 reshape.36
  82.4 3.1 %collective-permute-done.1 = bf16[2,32,529]{2,1,0:T(8,128)(2,1)S(1)} collective-permute-done((bf16[2,32,529]{2,1,0:T(8,128)(2,1)S(1)}, bf16[2,32,529]{2,1,0:T(8,128)(2,1)S(1)}, u32[]{:S(2)}, u32[]{:S(2)}) %collective-permute-start.1) | collective-permute-done | bytes 67744 | tf_op jit(solution)/shard_map/ppermute | solution.py:29
  85.5 0.1 pad_maximum_fusion.5
  85.6 5.7 %collective-permute-start.3 = (bf16[20,2,529]{2,1,0:T(2,128)(2,1)S(1)}, bf16[20,2,529]{2,1,0:T(2,128)(2,1)S(1)}, u32[]{:S(2)}, u32[]{:S(2)}) collective-permute-start(bf16[20,2,529]{2,1,0:T(2,128)(2,1)S(1)} %get-tuple-element.46), channel_id=1, source_target_pairs={{8,0},{16,8},{24,16},{32,24},{40,32},{48,40},{56,48},{64,56},{72,6... | collective-permute-start | bytes 126968 | tf_op jit(solution)/shard_map/ppermute | solution.py:29
  91.3 1.9 %collective-permute-start.2 = (bf16[20,2,529]{2,1,0:T(2,128)(2,1)S(1)}, bf16[20,2,529]{2,1,0:T(2,128)(2,1)S(1)}, u32[]{:S(2)}, u32[]{:S(2)}) collective-permute-start(bf16[20,2,529]{2,1,0:T(2,128)(2,1)S(1)} %get-tuple-element.47), channel_id=1, source_target_pairs={{0,8},{8,16},{16,24},{24,32},{32,40},{40,48},{48,56},{56,64},{64,7... | collective-permute-start | bytes 126968 | tf_op jit(solution)/shard_map/ppermute | solution.py:29
  93.2 0.8 pad_maximum_fusion.3
  94.1 5.4 %collective-permute-done.2 = bf16[20,2,529]{2,1,0:T(2,128)(2,1)S(1)} collective-permute-done((bf16[20,2,529]{2,1,0:T(2,128)(2,1)S(1)}, bf16[20,2,529]{2,1,0:T(2,128)(2,1)S(1)}, u32[]{:S(2)}, u32[]{:S(2)}) %collective-permute-start.2) | collective-permute-done | bytes 42352 | tf_op jit(solution)/shard_map/ppermute | solution.py:29
  99.5 0.6 pad_maximum_fusion.1
  100.0 1.0 copy-done
  101.0 1.6 %slice_convert_fusion = (f32[18,34,256]{2,1,0:T(8,128)}, bf16[18,34,256]{2,1,0:T(8,128)(2,1)}, bf16[18,34,256]{2,1,0:T(8,128)(2,1)}, bf16[18,34,256]{2,1,0:T(8,128)(2,1)}) fusion(bf16[20,36,529]{2,1,0:T(8,128)(2,1)S(1)} %pad_maximum_fusion.1), kind=kLoop, calls=%fused_computation.50 | loop fusion | flops 156672 | bytes 2820096 | tf_op jit(solution)/shard_map/convert_element_type | solution.py:97
  102.6 3.5 %dynamic_update_slice.3 = f32[18,34,256]{2,1,0:T(8,128)} dynamic-update-slice(f32[18,34,256]{2,1,0:T(8,128)} %get-tuple-element.25, f32[16,32,256]{2,1,0:T(8,128)} %param.9, s32[]{:T(128)} %constant.24.clone.1, s32[]{:T(128)} %constant.24.clone.1, s32[]{:T(128)} %constant.6.clone.1) | dynamic-update-slice | bytes 1048580 | tf_op jit(solution)/shard_map/dynamic_update_slice | solution.py:98
  106.1 0.6 pad_maximum_fusion.2
  106.6 0.6 copy-done.1
  107.3 1.0 fusion.49
  108.3 1.0 fusion.48
  109.3 1.4 fusion.51
  110.7 0.1 copy-done.9
  110.8 7.0 %concatenate.52 = bf16[18,34,2376]{2,1,0:T(8,128)(2,1)} concatenate(bf16[18,34,256]{2,1,0:T(8,128)(2,1)} %get-tuple-element.71, bf16[18,34,256]{2,1,0:T(8,128)(2,1)} %get-tuple-element.28, bf16[18,34,256]{2,1,0:T(8,128)(2,1)} %get-tuple-element.40, bf16[18,34,256]{2,1,0:T(8,128)(2,1)} %get-tuple-element.72, bf16[18,34,256]{2,1,0:T(8,128)(2,1)S(1)} %copy-done.9, ...), dimensions={2} | concatenate | bytes 5816448 | tf_op jit(solution)/shard_map/concatenate | solution.py:45
  117.9 1.2 convert_reduce_fusion
  119.1 2.7 %fusion.46 = (bf16[16,32,8]{2,1,0:T(8,128)(2,1)}, bf16[16,32,8]{2,1,0:T(8,128)(2,1)}, bf16[16,32,8]{2,1,0:T(8,128)(2,1)}, bf16[16,32,8]{2,1,0:T(8,128)(2,1)}, bf...) fusion(bf16[20,34,529]{2,1,0:T(8,128)(2,1)} %copy-done.2, bf16[20,34,529]{2,1,0:T(8,128)(2,1)} %copy-done.3), kind=kLoop, calls=%fused_computation.70 | loop fusion | bytes 98304 | tf_op jit(solution)/shard_map/slice | solution.py:44
  121.8 2.2 %select_bitcast_fusion.1 = (bf16[1,4,4,16,8,640]{5,4,2,0,1,3:T(8,128)(2,1)S(1)}, bf16[1,4,4,16,8,640]{5,4,2,0,1,3:T(8,128)(2,1)S(1)}) fusion(bf16[4,4,16,8,640]{4,3,1,0,2:T(8,128)(2,1)} %collective-permute-done.4, pred[]{:T(512)S(6)} %eq.4, bf16[4,4,16,8,640]{4,3,2,1,0:T(8,128)(2,1)S(1)} %bitcast.30), kind=kLoop, calls=%fused_computation.6 | loop fusion | flops 2621440 | bytes 10485761 | tf_op jit(solution)/shard_map/stack | solution.py:79
  124.0 0.5 pad_maximum_fusion
  124.6 2.6 %copy-done.5 = bf16[18,34,2376]{2,1,0:T(8,128)(2,1)S(1)} copy-done((bf16[18,34,2376]{2,1,0:T(8,128)(2,1)S(1)}, bf16[18,34,2376]{2,1,0:T(8,128)(2,1)}, u32[]{:S(2)}) %copy-start.5) | copy-done | bytes 2908248
  127.1 4.0 %fusion.4 = f32[18,34,1024]{2,1,0:T(8,128)S(1)} fusion(bf16[1024,2560,1]{1,0,2:T(8,128)(2,1)S(1)} %bitcast.31, bf16[18,34,2376]{2,1,0:T(8,128)(2,1)S(1)} %copy-done.5, f32[1024]{0:T(1024)S(1)} %copy-done.18), kind=kOutput, calls=%fused_computation.7 | convolution fusion | flops 3209269248 | bytes 10661952 | tf_op jit(solution)/shard_map/dot_general | solution.py:52
  131.2 0.8 fusion.24
  132.0 1.6 %fusion.54 = (bf16[16,32,256]{2,1,0:T(8,128)(2,1)}, bf16[16,32,256]{2,1,0:T(8,128)(2,1)}, bf16[16,32,256]{2,1,0:T(8,128)(2,1)}, bf16[16,32,256]{2,1,0:T(8,128)(2...) fusion(bf16[18,34,256]{2,1,0:T(8,128)(2,1)S(1)} %get-tuple-elem, ...), kind=kLoop, calls=%fused_computation.78 | loop fusion | bytes 4718592 | tf_op jit(solution)/shard_map/slice | solution.py:43
  133.6 3.9 %concatenate.55 = bf16[16,32,2376]{2,1,0:T(8,128)(2,1)S(1)} concatenate(bf16[16,32,256]{2,1,0:T(8,128)(2,1)} %get-tuple-element.60, bf16[16,32,256]{2,1,0:T(8,128)(2,1)} %get-tuple-element.59, bf16[16,32,256]{2,1,0:T(8,128)(2,1)} %get-tuple-element.58, bf16[16,32,256]{2,1,0:T(8,128)(2,1)} %get-tuple-element.57, bf16[16,32,256]{2,1,0:T(8,128)(2,1)} %get-tuple-element.56, ...), dimensions={2} | concatenate | bytes 4866048 | tf_op jit(solution)/shard_map/concatenate | solution.py:45
  137.5 4.9 %fusion.7 = f32[16,32,1024]{2,1,0:T(8,128)S(1)} fusion(bf16[1024,2560,1]{1,0,2:T(8,128)(2,1)} %bitcast.32, bf16[16,32,2376]{2,1,0:T(8,128)(2,1)S(1)} %concatenate.55, f32[1024]{0:T(1024)S(1)} %copy-done.18), kind=kOutput, calls=%fused_computation.8 | convolution fusion | flops 2684878848 | bytes 9777152 | tf_op jit(solution)/shard_map/dot_general | solution.py:52
  142.4 1.4 fusion.38
  143.8 0.3 fusion.56
  144.0 0.6 convert_multiply_fusion
  (43 shorter events, 0.2 us)
Async XLA Ops:
  63.8 8.3 %copy-start.15 = (s32[16,32]{1,0:T(8,128)S(1)}, s32[16,32]{1,0:T(8,128)}, u32[]{:S(2)}) copy-start(s32[16,32]{1,0:T(8,128)} %param.12) | copy-start | bytes 6148
  63.8 8.5 %copy-start.14 = (bf16[2,16,32,8]{2,3,1,0:T(8,128)(2,1)S(1)}, bf16[2,16,32,8]{2,3,1,0:T(8,128)(2,1)}, u32[]{:S(2)}) copy-start(bf16[2,16,32,8]{2,3,1,0:T(8,128)(2,1)} %param.7) | copy-start | bytes 49156
  63.8 9.4 %copy-start.7 = (f32[16,32,256]{2,1,0:T(8,128)S(1)}, f32[16,32,256]{2,1,0:T(8,128)}, u32[]{:S(2)}) copy-start(f32[16,32,256]{2,1,0:T(8,128)} %param.9) | copy-start | bytes 1572868
  65.7 16.2 %copy-start.19 = (bf16[256]{0:T(256)(128)(2,1)S(1)}, bf16[256]{0:T(256)(128)(2,1)}, u32[]{:S(2)}) copy-start(bf16[256]{0:T(256)(128)(2,1)} %param.13) | copy-start | bytes 1540
  65.7 56.1 %collective-permute-start.4 = (bf16[4,4,16,8,640]{4,3,1,0,2:T(8,128)(2,1)}, bf16[4,4,16,8,640]{4,3,1,0,2:T(8,128)(2,1)}, u32[]{:S(2)}, u32[]{:S(2)}) collective-permute-start(bf16[4,4,16,8,640]{4,3,1,0,2:T(8,128)(2,1)} %copy.27), channel_id=1, source_target_pairs={{0,1},{1,0},{2,3},{3,2},{4,5},{5,4},{6,7},{7,6},{8,9},{9,8},{10,11... | collective-permute-start | bytes 7864328 | tf_op jit(solution)/shard_map/ppermute | solution.py:76
  75.5 2.0 %copy-start.10 = (bf16[16,32,8]{2,1,0:T(8,128)(2,1)}, bf16[16,32,8]{2,1,0:T(8,128)(2,1)S(1)}, u32[]{:S(2)}) copy-start(bf16[16,32,8]{2,1,0:T(8,128)(2,1)S(1)} %get-tuple-element.61) | copy-start | bytes 24580
  77.5 4.9 %collective-permute-start = (bf16[2,32,529]{2,1,0:T(8,128)(2,1)}, bf16[2,32,529]{2,1,0:T(8,128)(2,1)S(1)}, u32[]{:S(2)}, u32[]{:S(2)}) collective-permute-start(bf16[2,32,529]{2,1,0:T(8,128)(2,1)} %get-tuple-element.50), channel_id=1, source_target_pairs={{0,1},{1,2},{2,3},{3,4},{4,5},{5,6},{6,7},{8,9},{9,10},{10,11},{11... | collective-permute-start | bytes 203144 | tf_op jit(solution)/shard_map/ppermute | solution.py:29
  79.8 5.8 %collective-permute-start.1 = (bf16[2,32,529]{2,1,0:T(8,128)(2,1)S(1)}, bf16[2,32,529]{2,1,0:T(8,128)(2,1)S(1)}, u32[]{:S(2)}, u32[]{:S(2)}) collective-permute-start(bf16[2,32,529]{2,1,0:T(8,128)(2,1)S(1)} %get-tuple-element.51), channel_id=1, source_target_pairs={{1,0},{2,1},{3,2},{4,3},{5,4},{6,5},{7,6},{9,8},{10,9},{11,10},{12... | collective-permute-start | bytes 203144 | tf_op jit(solution)/shard_map/ppermute | solution.py:29
  85.6 8.4 %collective-permute-start.3 = (bf16[20,2,529]{2,1,0:T(2,128)(2,1)S(1)}, bf16[20,2,529]{2,1,0:T(2,128)(2,1)S(1)}, u32[]{:S(2)}, u32[]{:S(2)}) collective-permute-start(bf16[20,2,529]{2,1,0:T(2,128)(2,1)S(1)} %get-tuple-element.46), channel_id=1, source_target_pairs={{8,0},{16,8},{24,16},{32,24},{40,32},{48,40},{56,48},{64,56},{72,6... | collective-permute-start | bytes 126968 | tf_op jit(solution)/shard_map/ppermute | solution.py:29
  91.3 8.2 %collective-permute-start.2 = (bf16[20,2,529]{2,1,0:T(2,128)(2,1)S(1)}, bf16[20,2,529]{2,1,0:T(2,128)(2,1)S(1)}, u32[]{:S(2)}, u32[]{:S(2)}) collective-permute-start(bf16[20,2,529]{2,1,0:T(2,128)(2,1)S(1)} %get-tuple-element.47), channel_id=1, source_target_pairs={{0,8},{8,16},{16,24},{24,32},{32,40},{40,48},{48,56},{56,64},{64,7... | collective-permute-start | bytes 126968 | tf_op jit(solution)/shard_map/ppermute | solution.py:29
  100.0 1.0 copy-start
  106.1 1.2 copy-start.1
  107.3 3.4 %copy-start.2 = (bf16[20,34,529]{2,1,0:T(8,128)(2,1)}, bf16[20,34,529]{2,1,0:T(8,128)(2,1)S(1)}, u32[]{:S(2)}) copy-start(bf16[20,34,529]{2,1,0:T(8,128)(2,1)S(1)} %get-tuple-element.44) | copy-start | bytes 2158324
  107.3 3.4 %copy-start.3 = (bf16[20,34,529]{2,1,0:T(8,128)(2,1)}, bf16[20,34,529]{2,1,0:T(8,128)(2,1)S(1)}, u32[]{:S(2)}) copy-start(bf16[20,34,529]{2,1,0:T(8,128)(2,1)S(1)} %get-tuple-element.45) | copy-start | bytes 2158324
  109.3 1.4 copy-start.8
  109.3 1.5 %copy-start.9 = (bf16[18,34,256]{2,1,0:T(8,128)(2,1)S(1)}, bf16[18,34,256]{2,1,0:T(8,128)(2,1)}, u32[]{:S(2)}) copy-start(bf16[18,34,256]{2,1,0:T(8,128)(2,1)} %get-tuple-element.27) | copy-start | bytes 940036
  124.0 3.2 %copy-start.5 = (bf16[18,34,2376]{2,1,0:T(8,128)(2,1)S(1)}, bf16[18,34,2376]{2,1,0:T(8,128)(2,1)}, u32[]{:S(2)}) copy-start(bf16[18,34,2376]{2,1,0:T(8,128)(2,1)} %concatenate.52) | copy-start | bytes 8724676
  124.0 3.1 %copy-start.18 = (f32[1024]{0:T(1024)S(1)}, f32[1024]{0:T(1024)}, u32[]{:S(2)}) copy-start(f32[1024]{0:T(1024)} %param.11) | copy-start | bytes 12292
  124.6 6.6 %copy-start.4 = (bf16[2,4,4,16,8,640]{5,4,2,0,1,3:T(8,128)(2,1)}, bf16[2,4,4,16,8,640]{5,4,2,0,1,3:T(8,128)(2,1)S(1)}, u32[]{:S(2)}) copy-start(bf16[2,4,4,16,8,640]{5,4,2,0,1,3:T(8,128)(2,1)S(1)} %pad_maximum_fusion) | copy-start | bytes 15728644
  127.1 4.0 %copy-start.6 = (f32[18,34,256]{2,1,0:T(8,128)S(1)}, f32[18,34,256]{2,1,0:T(8,128)}, u32[]{:S(2)}) copy-start(f32[18,34,256]{2,1,0:T(8,128)} %dynamic_update_slice.3) | copy-start | bytes 1880068
  132.0 1.6 %copy-start.11 = (bf16[16,32,8]{2,1,0:T(8,128)(2,1)S(1)}, bf16[16,32,8]{2,1,0:T(8,128)(2,1)}, u32[]{:S(2)}) copy-start(bf16[16,32,8]{2,1,0:T(8,128)(2,1)} %copy-done.10) | copy-start | bytes 24580
  132.0 1.6 %copy-start.13 = (bf16[16,32,8]{2,1,0:T(8,128)(2,1)S(1)}, bf16[16,32,8]{2,1,0:T(8,128)(2,1)}, u32[]{:S(2)}) copy-start(bf16[16,32,8]{2,1,0:T(8,128)(2,1)} %get-tuple-element.48) | copy-start | bytes 24580
  142.4 1.4 copy-start.17
  142.4 1.6 %copy-start.16 = (s32[16,32]{1,0:T(8,128)S(1)}, s32[16,32]{1,0:T(8,128)}, u32[]{:S(2)}) copy-start(s32[16,32]{1,0:T(8,128)} %param.12) | copy-start | bytes 6148
  143.8 0.9 copy-start.12

commit v2 on v1

v2 whole, which is shorter than its diff:
```python
import jax
import jax.numpy as jnp
from jax import lax
from jax.experimental import pallas as pl
from jax.experimental.pallas import tpu as pltpu
from jax.sharding import Mesh, PartitionSpec as P

KPAD = 2560
HID = 256
F32 = jnp.float32
BF16 = jnp.bfloat16
NT = (((1,), (1,)), ((), ()))
NN = (((1,), (0,)), ((), ()))
VMEM = pl.BlockSpec(memory_space=pltpu.VMEM)
SMEM = pl.BlockSpec(memory_space=pltpu.SMEM)
PARAMS = pltpu.CompilerParams(vmem_limit_bytes=48 * 1024 * 1024)


def pack_weights(conv_weight):
    taps, cin, cols = conv_weight.shape
    cx = cin - HID
    flipped = jnp.transpose(conv_weight, (2, 0, 1))
    hidden = flipped[:, :, cx:].reshape(cols, taps * HID)
    frame = flipped[:, :, :cx].reshape(cols, taps * cx)
    packed = jnp.concatenate([hidden, frame], axis=1)
    return jnp.pad(packed, ((0, 0), (0, KPAD - packed.shape[1])))


def spread(block, axes):
    count = lax.axis_size(axes)
    copies = jnp.broadcast_to(block[None], (count,) + block.shape)
    return lax.all_to_all(copies, axes, 0, 0)


def shifted(block, axes, step):
    count = lax.axis_size(axes)
    pairs = [(i, i + step) for i in range(count) if 0 <= i + step < count]
    return lax.ppermute(block, axes, pairs)


def widened(block, width):
    for axes, dim in ((("x", "c"), 0), (("z", "y"), 1)):
        size = block.shape[dim]
        low = shifted(lax.slice_in_dim(block, size - width, size, axis=dim), axes, 1)
        high = shifted(lax.slice_in_dim(block, 0, width, axis=dim), axes, -1)
        block = jnp.concatenate([low, block, high], axis=dim)
    return block


def taps_of(source, rows, cols):
    return [source[a : a + rows, b : b + cols] for a in range(3) for b in range(3)]


def patches_of(hidden, frame):
    rows, cols = frame.shape[0] - 2, frame.shape[1] - 2
    pieces = [] if hidden is None else taps_of(hidden, rows, cols)
    pieces += taps_of(frame, rows, cols)
    out = jnp.concatenate(pieces, -1)
    width = -(-out.shape[2] // 256) * 256
    out = jnp.pad(out, ((0, 0), (0, 0), (0, width - out.shape[2])))
    return out.reshape(rows * cols, width)


def ringed(core, left, right):
    pad = ((0, 6), (0, 0))
    return jnp.concatenate([core, jnp.pad(left, pad), jnp.pad(right, pad)], axis=0)


def chooser(half, shape, channel_axis):
    place = lax.broadcasted_iota(jnp.int32, shape, 1 - channel_axis)
    natural = lax.broadcasted_iota(jnp.int32, shape, channel_axis)
    y = lax.shift_right_logical(place, 5)
    zz = lax.shift_right_logical(place, 3) & 3
    wanted = zz * 64 + y * 16 + half * 8 + (place & 7)
    return jnp.where(natural == wanted, 1.0, 0.0).astype(BF16)


def parts_of(value):
    high = value.astype(BF16)
    rest = value - high.astype(F32)
    middle = rest.astype(BF16)
    return high, middle, (rest - middle.astype(F32)).astype(BF16)


def moved(value, choice):
    dots = [lax.dot_general(p, choice, NN, preferred_element_type=F32) for p in parts_of(value)]
    return dots[0] + (dots[1] + dots[2])


def half_step(patches, weight_ref, bias, cell, keep):
    gates = []
    for pair in range(2):
        rhs = jnp.concatenate(
            [
                jnp.concatenate(
                    [
                        weight_ref[y * 4 + x, q * 32 : (q + 1) * 32, :]
                        for q in (2 * pair, 2 * pair + 1)
                        for y in range(4)
                    ],
                    axis=0,
                )
                for x in range(4)
            ],
            axis=1,
        )
        both = lax.dot_general(patches, rhs, NT, preferred_element_type=F32)
        gates.append(both[:, :128] + bias[2 * pair][None])
        gates.append(both[:, 128:] + bias[2 * pair + 1][None])
    sig = lambda v: 0.5 * jnp.tanh(0.5 * v) + 0.5
    cell = sig(gates[1]) * cell + sig(gates[0]) * jnp.tanh(gates[2])
    hidden = (keep * sig(gates[3]) * jnp.tanh(cell)).astype(BF16)
    return hidden, cell


def first_kernel(half_ref, patches_ref, weight_ref, bias_ref, cell_ref, keep_ref, hid_out, cell_out):
    choice = chooser(half_ref[0], (HID, 128), 0)
    cell = moved(cell_ref[...], choice)
    hidden, cell = half_step(patches_ref[...], weight_ref, bias_ref[...], cell, keep_ref[...])
    hid_out[...] = hidden
    cell_out[...] = cell


def first_step(half, patches, weight, bias, cell, keep):
    count = patches.shape[0]
    return pl.pallas_call(
        first_kernel,
        out_shape=(
            jax.ShapeDtypeStruct((count, 128), BF16),
            jax.ShapeDtypeStruct((count, 128), F32),
        ),
        in_specs=[SMEM] + [VMEM] * 5,
        out_specs=(VMEM, VMEM),
        compiler_params=PARAMS,
        cost_estimate=pl.CostEstimate(
            flops=2 * count * KPAD * 512, bytes_accessed=6_000_000, transcendentals=count * 640
        ),
    )(half, patches, weight, bias, cell, keep)


def second_kernel(
    half_ref,
    hid0_ref,
    hid1_ref,
    cell0_ref,
    cell1_ref,
    frame_ref,
    weight0_ref,
    weight1_ref,
    bias_ref,
    keep_ref,
    keep2_ref,
    proj_ref,
    hid_out,
    cell_out,
    flux_out,
    wide,
    patches,
):
    choices = [chooser(half_ref[i], (128, HID), 1) for i in range(2)]
    natural = lax.dot_general(
        hid0_ref[...], choices[0], NN, preferred_element_type=F32
    ) + lax.dot_general(hid1_ref[...], choices[1], NN, preferred_element_type=F32)
    wide[:, 8:40, :] = natural[:576].reshape(18, 32, HID)
    for row in range(18):
        wide[row, 7:8, :] = natural[576 + row : 577 + row]
        wide[row, 40:41, :] = natural[600 + row : 601 + row]
    for b in range(3):
        moved_rows = wide[:, 7 + b : 39 + b, :].astype(BF16)
        for a in range(3):
            t = 3 * a + b
            patches[:, t * HID : (t + 1) * HID] = moved_rows[a : a + 16].reshape(512, HID)
    patches[:, 9 * HID :] = frame_ref[...]
    hid, cell = None, None
    for i, (weight_ref, cell_ref) in enumerate(((weight0_ref, cell0_ref), (weight1_ref, cell1_ref))):
        new_hid, new_cell = half_step(
            patches[...], weight_ref, bias_ref[i], cell_ref[32:544, :], keep_ref[...]
        )
        one = lax.dot_general(new_hid, choices[i], NN, preferred_element_type=F32)
        two = moved(new_cell, choices[i])
        hid = one if hid is None else hid + one
        cell = two if cell is None else cell + two
    hid = hid.astype(BF16)
    hid_out[...] = hid
    cell_out[...] = cell
    flux = lax.dot_general(proj_ref[...], hid, NT, preferred_element_type=F32)
    for row in range(16):
        flux_out[row : row + 1, :] = flux[0:1, row * 32 : (row + 1) * 32] * keep2_ref[row : row + 1, :]


def second_step(halves, hids, cells, frame, weights, bias, keep, keep2, proj):
    return pl.pallas_call(
        second_kernel,
        out_shape=(
            jax.ShapeDtypeStruct((512, HID), BF16),
            jax.ShapeDtypeStruct((512, HID), F32),
            jax.ShapeDtypeStruct((16, 32), F32),
        ),
        in_specs=[SMEM] + [VMEM] * 11,
        out_specs=(VMEM, VMEM, VMEM),
        scratch_shapes=[pltpu.VMEM((18, 48, HID), F32), pltpu.VMEM((512, KPAD), BF16)],
        compiler_params=PARAMS,
        cost_estimate=pl.CostEstimate(
            flops=2 * 512 * KPAD * 1024, bytes_accessed=8_000_000, transcendentals=512 * 1280
        ),
    )(halves, *hids, *cells, frame, *weights, bias, keep, keep2, proj)


def compute(halves, own, other, wide, cell_init, land_mask, bias, projection, cx):
    rows, cols = land_mask.shape
    width = HID
    keep = land_mask.astype(F32)
    hidden = wide[..., :width]
    frame0 = wide[..., 2 * width : 2 * width + cx]
    frame1 = wide[..., 2 * width + cx : 2 * width + 2 * cx]
    keep_wide = wide[1:-1, 1:-1, 2 * width + 2 * cx :].astype(F32)
    cell_wide = wide[1:-1, 1:-1, width : 2 * width].astype(F32)
    middle = jnp.concatenate([cell_wide[:1, 1:-1], cell_init, cell_wide[-1:, 1:-1]], axis=0)
    cell1 = ringed(middle.reshape(-1, width), cell_wide[:, 0], cell_wide[:, -1])
    keep1 = ringed(keep_wide[:, 1:-1].reshape(-1, 1), keep_wide[:, 0], keep_wide[:, -1])
    patches1 = ringed(
        patches_of(hidden[:, 1:-1], frame0[:, 1:-1]),
        patches_of(hidden[:, :3], frame0[:, :3]),
        patches_of(hidden[:, -3:], frame0[:, -3:]),
    )
    frame2 = patches_of(None, frame1[1:-1, 1:-1])

    by_half = jnp.transpose(bias.reshape(4, 4, 4, 2, 8), (3, 0, 2, 1, 4)).reshape(2, 4, 128)
    bias2 = jnp.stack([by_half[halves[0]], by_half[halves[1]]])
    hid0, cell0 = first_step(halves[:1], patches1, own, bias2[0], cell1, keep1)
    hid1, cell1 = first_step(halves[1:], patches1, other, bias2[1], cell1, keep1)
    proj = jnp.broadcast_to(projection[None], (16, width))
    hidden, cell, flux = second_step(
        halves, (hid0, hid1), (cell0, cell1), frame2, (own, other), bias2,
        keep.reshape(-1, 1), keep, proj,
    )
    return hidden.reshape(rows, cols, width), cell.reshape(rows, cols, width), flux


def body(frames, hidden_init, cell_init, conv_weight, bias, land_mask, projection):
    cx = frames.shape[3]
    x, c = lax.axis_index("x"), lax.axis_index("c")
    packed = pack_weights(conv_weight)
    unit = lax.dynamic_slice(packed, (c * 8, x * (KPAD // 4)), (8, KPAD // 4))
    by_z = spread(unit, "z").reshape(128, KPAD // 4)
    own = spread(by_z, ("y", "x"))
    other = lax.ppermute(own, "c", [(0, 1), (1, 0)])
    packed_state = jnp.concatenate(
        [
            hidden_init,
            cell_init.astype(BF16),
            frames[0],
            frames[1],
            land_mask.astype(BF16)[..., None],
        ],
        axis=-1,
    )
    wide = widened(packed_state, 2)
    halves = jnp.stack([c, 1 - c]).astype(jnp.int32)
    return compute(halves, own, other, wide, cell_init, land_mask, bias, projection, cx)


def solution(mesh):
    split = Mesh(mesh.devices.reshape(16, 4, 4, 2), ("z", "y", "x", "c"))
    sx, sy = ("z", "y"), ("x", "c")
    in_specs = (
        P(None, sy, sx, None),
        P(sy, sx, None),
        P(sy, sx, None),
        P(None, None, sx),
        P(),
        P(sy, sx),
        P(),
    )
    out_specs = (P(sy, sx, None), P(sy, sx, None), P(sy, sx))
    return jax.shard_map(body, mesh=split, in_specs=in_specs, out_specs=out_specs, check_vma=False)
```

time: 146 us -> 154 us (1.055)
  the two profiles are of different devices: /device:TPU:129 before, /device:TPU:37 now
where the time goes in v2:
time: 154 us; the launch traced here: 152 us
  local copies, waits for them, and re-layouts  44.7 us (29%)
  starting transfers between devices  42 us (27%)
  waiting for transfers between devices  30.9 us (20%)
  other arithmetic  18 us (12%)
  Pallas kernels  15.8 us (10%)
    ppermute x4, waiting for transfers between devices, shifted(): return lax.ppermute(block, axes, pairs)  22.7 us
    all_to_all x2, starting transfers between devices, spread(): return lax.all_to_all(copies, axes, 0, 0)  21.7 us
    ppermute x4, starting transfers between devices, shifted(): return lax.ppermute(block, axes, pairs)  14.9 us
    concatenate x4, local copies, waits for them, and re-layouts, patches_of(): out = jnp.concatenate(pieces, -1)  12.4 us
    slice x9, local copies, waits for them, and re-layouts, taps_of(): return [source[a:a + rows, b:b + cols] for a in range(3) for b in range(3)]  9.89 us
    pallas_call x2, Pallas kernels, first_step(): pl.pallas_call(first_kernel, out_shape=(jax.ShapeDtypeStruct((count, 128)...  8.95 us
    all_to_all x2, waiting for transfers between devices, spread(): return lax.all_to_all(copies, axes, 0, 0)  8.17 us
    unnamed x29, local copies, waits for them, and re-layouts  7.76 us
  transfers between devices with their start and end apart: 7, of which 2 were waited for; matrix products, arithmetic and copies ran while one was open for 38% of the time, Pallas kernels for 3%

profile of v2, /device:TPU:37, one launch (start us, length us, event | category | flops | bytes accessed | tf_op | source)
XLA Modules:
  0.0 152.4 jit_solution(6052629553881820282)
XLA Ops:
  0.6 0.8 slice.544
  1.4 1.0 slice_bitcast_fusion
  2.6 0.7 broadcast_in_dim.11
  3.3 14.7 %all-to-all-start = ((bf16[16,8,640]{2,1,0:T(8,128)(2,1)}), bf16[16,8,640]{2,1,0:T(8,128)(2,1)S(1)}, u32[]{:S(2)}, u32[]{:S(2)}) async-start(bf16[16,8,640]{2,1,0:T(8,128)(2,1)} %broadcast_in_dim.11), calls=%async_computation | async-start | bytes 327680 | tf_op jit(solution)/shard_map/all_to_all | solution.py:32
  18.0 0.8 fusion.31
  18.9 0.8 fusion.36
  20.1 1.1 copy.43
  21.2 1.3 copy.63
  22.5 1.1 concatenate.80
  23.6 8.2 %all-to-all-done = bf16[16,8,640]{2,1,0:T(8,128)(2,1)S(1)} async-done(((bf16[16,8,640]{2,1,0:T(8,128)(2,1)}), bf16[16,8,640]{2,1,0:T(8,128)(2,1)S(1)}, u32[]{:S(2)}, u32[]{:S(2)}) %all-to-all-start) | async-done | bytes 163872 | tf_op jit(solution)/shard_map/all_to_all | solution.py:32
  31.8 1.8 %broadcast_in_dim.25 = bf16[16,128,640]{2,1,0:T(8,128)(2,1)} broadcast(bf16[128,640]{1,0:T(8,128)(2,1)S(1)} %bitcast.39), dimensions={1,2} | broadcast | bytes 2785280 | tf_op jit(solution)/shard_map/broadcast_in_dim | solution.py:31
  33.5 7.0 %all-to-all-start.1 = ((bf16[16,128,640]{2,1,0:T(8,128)(2,1)}), bf16[16,128,640]{2,1,0:T(8,128)(2,1)S(1)}, u32[]{:S(2)}, u32[]{:S(2)}) async-start(bf16[16,128,640]{2,1,0:T(8,128)(2,1)} %broadcast_in_dim.25), calls=%async_computation.1 | async-start | bytes 5242880 | tf_op jit(solution)/shard_map/all_to_all | solution.py:32
  40.6 1.2 fusion.30
  41.8 4.8 %collective-permute-start.1 = (bf16[2,32,529]{2,0,1:T(2,128)(2,1)S(1)}, bf16[2,32,529]{2,0,1:T(2,128)(2,1)S(1)}, u32[]{:S(2)}, u32[]{:S(2)}) collective-permute-start(bf16[2,32,529]{2,0,1:T(2,128)(2,1)S(1)} %get-tuple-element.63), channel_id=1, source_target_pairs={{1,0},{2,1},{3,2},{4,3},{5,4},{6,5},{7,6},{9,8},{10,9},{11,10},{12... | collective-permute-start | bytes 203144 | tf_op jit(solution)/shard_map/ppermute | solution.py:38
  46.5 2.7 %collective-permute-start = (bf16[2,32,529]{2,0,1:T(2,128)(2,1)S(1)}, bf16[2,32,529]{2,0,1:T(2,128)(2,1)S(1)}, u32[]{:S(2)}, u32[]{:S(2)}) collective-permute-start(bf16[2,32,529]{2,0,1:T(2,128)(2,1)S(1)} %get-tuple-element.64), channel_id=1, source_target_pairs={{0,1},{1,2},{2,3},{3,4},{4,5},{5,6},{6,7},{8,9},{9,10},{10,11},{11... | collective-permute-start | bytes 203144 | tf_op jit(solution)/shard_map/ppermute | solution.py:38
  49.9 22.7 %collective-permute-done.1 = bf16[2,32,529]{2,0,1:T(2,128)(2,1)S(1)} collective-permute-done((bf16[2,32,529]{2,0,1:T(2,128)(2,1)S(1)}, bf16[2,32,529]{2,0,1:T(2,128)(2,1)S(1)}, u32[]{:S(2)}, u32[]{:S(2)}) %collective-permute-start.1) | collective-permute-done | bytes 67744 | tf_op jit(solution)/shard_map/ppermute | solution.py:38
  72.6 0.9 pad_maximum_fusion.10
  73.6 2.5 %collective-permute-start.2 = (bf16[20,2,529]{2,0,1:T(8,128)(2,1)S(1)}, bf16[20,2,529]{2,0,1:T(8,128)(2,1)S(1)}, u32[]{:S(2)}, u32[]{:S(2)}) collective-permute-start(bf16[20,2,529]{2,0,1:T(8,128)(2,1)S(1)} %get-tuple-element.47), channel_id=1, source_target_pairs={{0,8},{8,16},{16,24},{24,32},{32,40},{40,48},{48,56},{56,64},{64,7... | collective-permute-start | bytes 126968 | tf_op jit(solution)/shard_map/ppermute | solution.py:38
  76.1 4.9 %collective-permute-start.3 = (bf16[20,2,529]{2,0,1:T(8,128)(2,1)S(1)}, bf16[20,2,529]{2,0,1:T(8,128)(2,1)S(1)}, u32[]{:S(2)}, u32[]{:S(2)}) collective-permute-start(bf16[20,2,529]{2,0,1:T(8,128)(2,1)S(1)} %get-tuple-element.48), channel_id=1, source_target_pairs={{8,0},{16,8},{24,16},{32,24},{40,32},{48,40},{56,48},{64,56},{72,6... | collective-permute-start | bytes 126968 | tf_op jit(solution)/shard_map/ppermute | solution.py:38
  81.0 1.4 pad_maximum_fusion.18
  82.4 1.9 %pad_maximum_fusion.7 = (bf16[16,32,8]{2,0,1:T(8,128)(2,1)S(1)}, bf16[16,32,8]{2,0,1:T(8,128)(2,1)}) fusion(bf16[2,32,529]{2,0,1:T(2,128)(2,1)S(1)} %collective-permute-done.1, bf16[16,32,529]{2,0,1:T(8,128)(2,1)} %concatenate.80, bf16[2,32,529]{2,0,1:T(2,128)(2,1)S(1)} %collective-permute-done), kind=kLoop, calls=%fused_computation.52 | loop fusion | flops 32768 | bytes 693504 | tf_op jit(solution)/shard_map/concatenate | solution.py:46
  84.3 1.9 %fusion.9 = (bf16[18,32,8]{2,0,1:T(8,128)(2,1)}, bf16[18,32,8]{2,0,1:T(8,128)(2,1)}) fusion(bf16[16,32,529]{2,0,1:T(8,128)(2,1)} %concatenate.80, bf16[2,32,529]{2,0,1:T(2,128)(2,1)S(1)} %collective-permute-done.1, bf16[2,32,529]{2,0,1:T(2,128)(2,1)S(1)} %collective-permute-done), kind=kLoop, calls=%fused_computation.50 | loop fusion | flops 36864 | bytes 695552 | tf_op jit(solution)/shard_map/concatenate | solution.py:46
  86.2 2.1 %fusion.6 = (bf16[18,32,256]{2,0,1:T(8,128)(2,1)}, bf16[18,32,256]{2,0,1:T(8,128)(2,1)}) fusion(bf16[16,32,529]{2,0,1:T(8,128)(2,1)} %concatenate.80, bf16[2,32,529]{2,0,1:T(2,128)(2,1)S(1)} %collective-permute-done.1, bf16[2,32,529]{2,0,1:T(2,128)(2,1)S(1)} %collective-permute-done), kind=kLoop, calls=%fused_computation.43 | loop fusion | flops 1179648 | bytes 1266944 | tf_op jit(solution)/shard_map/concatenate | solution.py:46
  89.5 0.7 slice.497
  90.2 0.9 slice.486
  91.2 1.0 fusion.8
  92.7 1.2 fusion.24
  93.9 1.1 fusion.26
  95.0 1.8 %fusion.28 = (bf16[18,32,256]{2,0,1:T(8,128)(2,1)}, bf16[18,32,256]{2,0,1:T(8,128)(2,1)}, bf16[18,32,256]{2,0,1:T(8,128)(2,1)}, bf16[18,32,256]{2,0,1:T(8,128)(2...) fusion(bf16[20,34,529]{2,0,1:T(8,128)(2,1)S(1)} %get-tuple-element.43, ...), kind=kLoop, calls=%fused_computation.100 | loop fusion | bytes 3538944 | tf_op jit(solution)/shard_map/slice | solution.py:51
  96.8 5.5 %collective-permute-start.4 = (bf16[16,128,640]{2,1,0:T(8,128)(2,1)S(1)}, bf16[16,128,640]{2,1,0:T(8,128)(2,1)}, u32[]{:S(2)}, u32[]{:S(2)}) collective-permute-start(bf16[16,128,640]{2,1,0:T(8,128)(2,1)S(1)} %all-to-all-done.1.weight_ref.weight0_ref), channel_id=1, source_target_pairs={{0,1},{1,0},{2,3},{3,2},{4,5},{5,4},{6,7},{7,6},{8,9},{9,8},{10,11... | collective-permute-start | bytes 7864328 | tf_op jit(solution)/shard_map/ppermute | solution.py:247
  103.6 1.8 %slice.545 = f32[18,32,1]{2,0,1:T(8,128)} slice(f32[18,34,1]{2,0,1:T(8,128)} %fusion.8), slice={[0:18], [1:33], [0:1]} | slice | bytes 4608 | tf_op jit(solution)/shard_map/slice | solution.py:220
  105.4 1.2 copy.52
  107.1 2.1 %concatenate.95 = bf16[16,32,72]{2,0,1:T(8,128)(2,1)} concatenate(bf16[16,32,8]{2,0,1:T(8,128)(2,1)} %get-tuple-element.95, bf16[16,32,8]{2,0,1:T(8,128)(2,1)} %get-tuple-element.57, bf16[16,32,8]{2,0,1:T(8,128)(2,1)} %get-tuple-element.21, bf16[16,32,8]{2,0,1:T(8,128)(2,1)} %get-tuple-element.96, bf16[16,32,8]{2,0,1:T(8,128)(2,1)S(1)} %bitcast.38, ...), dimensions={2} | concatenate | bytes 147456 | tf_op jit(solution)/shard_map/concatenate | solution.py:58
  109.3 1.6 %copy.60 = bf16[16,32,72]{2,1,0:T(8,128)(2,1)} copy(bf16[16,32,72]{2,0,1:T(8,128)(2,1)} %concatenate.95) | data formatting | bytes 147456
  110.9 7.1 %concatenate.86 = bf16[18,32,2376]{2,0,1:T(8,128)(2,1)} concatenate(bf16[18,32,256]{2,0,1:T(8,128)(2,1)} %get-tuple-element.101, bf16[18,32,256]{2,0,1:T(8,128)(2,1)} %get-tuple-element.61, bf16[18,32,256]{2,0,1:T(8,128)(2,1)} %get-tuple-element.33, bf16[18,32,256]{2,0,1:T(8,128)(2,1)} %get-tuple-element.102, bf16[18,32,256]{2,0,1:T(8,128)(2,1)} %slice.486, ...), dimensions={2} | concatenate | bytes 5474304 | tf_op jit(solution)/shard_map/concatenate | solution.py:58
  117.9 2.4 %copy.59 = bf16[18,32,2376]{2,1,0:T(8,128)(2,1)S(1)} copy(bf16[18,32,2376]{2,0,1:T(8,128)(2,1)} %concatenate.86) | data formatting | bytes 5474304
  120.4 2.0 %pad.40.clone = bf16[18,32,2560]{2,1,0:T(8,128)(2,1)} pad(bf16[18,32,2376]{2,1,0:T(8,128)(2,1)S(1)} %copy.59, bf16[]{:T(256)} %constant.8.clone.1), padding=0_0x0_0x0_184 | pad | bytes 5686274 | tf_op jit(solution)/shard_map/jit(_pad)/pad | solution.py:60
  124.3 1.6 %concatenate.87 = bf16[18,1,2376]{2,0,1:T(8,128)(2,1)} concatenate(bf16[18,1,256]{2,0,1:T(8,128)(2,1)} %get-tuple-element.78, bf16[18,1,256]{2,0,1:T(8,128)(2,1)} %get-tuple-element.77, bf16[18,1,256]{2,0,1:T(8,128)(2,1)} %get-tuple-element.49, bf16[18,1,256]{2,0,1:T(8,128)(2,1)} %get-tuple-element.76, bf16[18,1,256]{2,0,1:T(8,128)(2,1)} %get-tuple-element.75, ...), dimensions={2} | concatenate | bytes 171072 | tf_op jit(solution)/shard_map/concatenate | solution.py:58
  126.0 1.5 fusion.34
  127.4 1.5 fusion.35
  128.9 1.6 %concatenate.88 = bf16[18,1,2376]{2,0,1:T(8,128)(2,1)} concatenate(bf16[18,1,256]{2,0,1:T(8,128)(2,1)} %get-tuple-element.62, bf16[18,1,256]{2,0,1:T(8,128)(2,1)} %get-tuple-element.90, bf16[18,1,256]{2,0,1:T(8,128)(2,1)S(1)} %get-tuple-element.89, bf16[18,1,256]{2,0,1:T(8,128)(2,1)} %get-tuple-element.41, bf16[18,1,256]{2,0,1:T(8,128)(2,1)S(1)} %get-tuple-element.88, ...), dimensions={2} | concatenate | bytes 171072 | tf_op jit(solution)/shard_map/concatenate | solution.py:58
  130.5 1.1 pad_maximum_fusion.2
  131.6 0.8 select_maximum_fusion.cell_ref
  132.4 1.0 pad_bitcast_fusion
  133.4 3.2 %fusion.4.patches_ref = bf16[624,2560]{1,0:T(8,128)(2,1)} fusion(bf16[18,2560]{1,0:T(8,128)(2,1)S(1)} %get-tuple-element.104, bf16[18,2560]{1,0:T(8,128)(2,1)S(1)} %get-tuple-element.105, bf16[576,2560]{1,0:T(8,128)(2,1)} %bitcast.35), kind=kLoop, calls=%fused_computation.7 | loop fusion | flops 19169280 | bytes 6328320 | tf_op jit(solution)/shard_map/concatenate | solution.py:66
  136.6 4.1 %shard_map.94 = (bf16[624,128]{1,0:T(8,128)(2,1)S(1)}, f32[624,128]{1,0:T(8,128)S(1)}) custom-call(s32[1]{0:T(128)} %bitcast.half_ref, bf16[624,2560]{1,0:T(8,128)(2,1)} %fusion.4.patches_ref, bf16[16,128,640]{2,1,0:T(8,128)(2,1)S(1)} %all-to-all-done.1.weight_ref.weight0_ref, f32[4,128]{1,0:T(4,128)S(1)} %bitcast.34, ...), custom_call_target="tpu_custom_call" | custom-call | flops 1635778560 | bytes 6000000 | tf_op jit(solution)/shard_map/pallas_call | solution.py:126
  140.7 4.9 %shard_map.95 = (bf16[624,128]{1,0:T(8,128)(2,1)S(1)}, f32[624,128]{1,0:T(8,128)S(1)}) custom-call(s32[1]{0:T(128)} %bitcast.1.half_ref, bf16[624,2560]{1,0:T(8,128)(2,1)} %fusion.4.patches_ref, bf16[16,128,640]{2,1,0:T(8,128)(2,1)} %collective-permute-done.4.weight_ref.weight1_ref, f32[4,128]{1,0:T(4,128)S(1)} %bitcast.33, ...), custom_call_target="tpu_custom_call" | custom-call | flops 1635778560 | bytes 6000000 | tf_op jit(solution)/shard_map/pallas_call | solution.py:126
  145.6 6.8 %shard_map.96 = (bf16[512,256]{1,0:T(8,128)(2,1)}, f32[512,256]{1,0:T(8,128)}, f32[16,32]{1,0:T(8,128)}) custom-call(s32[2]{0:T(128)S(1)} %pad_add_fusion.half_ref, bf16[624,128]{1,0:T(8,128)(2,1)S(1)} %get-tuple-element.10.hid0_ref, bf16[624,128]{1,0:T(8,128)(2,1)S(1)} %get-tuple-element.11.hid1_ref, f32[624,128]{1,0:T(8,128)S(1)} %get-tuple-element.12.cell0_ref, ...), custom_call_target="tpu_custom_call" | custom-call | flops 2684354560 | bytes 8000000 | tf_op jit(solution)/shard_map/pallas_call | solution.py:192
  (56 shorter events, 7.0 us)
Async XLA Ops:
  3.3 28.4 %all-to-all-start = ((bf16[16,8,640]{2,1,0:T(8,128)(2,1)}), bf16[16,8,640]{2,1,0:T(8,128)(2,1)S(1)}, u32[]{:S(2)}, u32[]{:S(2)}) async-start(bf16[16,8,640]{2,1,0:T(8,128)(2,1)} %broadcast_in_dim.11), calls=%async_computation | async-start | bytes 327680 | tf_op jit(solution)/shard_map/all_to_all | solution.py:32
  33.5 15.7 %copy-start.9 = (f32[1024]{0:T(1024)S(1)}, f32[1024]{0:T(1024)}, u32[]{:S(2)}) copy-start(f32[1024]{0:T(1024)} %param.11) | copy-start | bytes 12292
  33.5 63.2 %all-to-all-start.1 = ((bf16[16,128,640]{2,1,0:T(8,128)(2,1)}), bf16[16,128,640]{2,1,0:T(8,128)(2,1)S(1)}, u32[]{:S(2)}, u32[]{:S(2)}) async-start(bf16[16,128,640]{2,1,0:T(8,128)(2,1)} %broadcast_in_dim.25), calls=%async_computation.1 | async-start | bytes 5242880 | tf_op jit(solution)/shard_map/all_to_all | solution.py:32
  41.8 30.9 %collective-permute-start.1 = (bf16[2,32,529]{2,0,1:T(2,128)(2,1)S(1)}, bf16[2,32,529]{2,0,1:T(2,128)(2,1)S(1)}, u32[]{:S(2)}, u32[]{:S(2)}) collective-permute-start(bf16[2,32,529]{2,0,1:T(2,128)(2,1)S(1)} %get-tuple-element.63), channel_id=1, source_target_pairs={{1,0},{2,1},{3,2},{4,3},{5,4},{6,5},{7,6},{9,8},{10,9},{11,10},{12... | collective-permute-start | bytes 203144 | tf_op jit(solution)/shard_map/ppermute | solution.py:38
  46.5 26.1 %collective-permute-start = (bf16[2,32,529]{2,0,1:T(2,128)(2,1)S(1)}, bf16[2,32,529]{2,0,1:T(2,128)(2,1)S(1)}, u32[]{:S(2)}, u32[]{:S(2)}) collective-permute-start(bf16[2,32,529]{2,0,1:T(2,128)(2,1)S(1)} %get-tuple-element.64), channel_id=1, source_target_pairs={{0,1},{1,2},{2,3},{3,4},{4,5},{5,6},{6,7},{8,9},{9,10},{10,11},{11... | collective-permute-start | bytes 203144 | tf_op jit(solution)/shard_map/ppermute | solution.py:38
  49.9 38.4 %copy-start = (bf16[16,32,529]{2,0,1:T(8,128)(2,1)S(1)}, bf16[16,32,529]{2,0,1:T(8,128)(2,1)}, u32[]{:S(2)}) copy-start(bf16[16,32,529]{2,0,1:T(8,128)(2,1)} %concatenate.80) | copy-start | bytes 1625092
  72.6 34.0 %copy-start.2 = (bf16[2,32,529]{2,0,1:T(2,128)(2,1)}, bf16[2,32,529]{2,0,1:T(2,128)(2,1)S(1)}, u32[]{:S(2)}) copy-start(bf16[2,32,529]{2,0,1:T(2,128)(2,1)S(1)} %collective-permute-done.1) | copy-start | bytes 203140
  72.6 34.0 %copy-start.4 = (bf16[2,32,529]{2,0,1:T(2,128)(2,1)}, bf16[2,32,529]{2,0,1:T(2,128)(2,1)S(1)}, u32[]{:S(2)}) copy-start(bf16[2,32,529]{2,0,1:T(2,128)(2,1)S(1)} %collective-permute-done) | copy-start | bytes 203140
  73.6 17.6 %collective-permute-start.2 = (bf16[20,2,529]{2,0,1:T(8,128)(2,1)S(1)}, bf16[20,2,529]{2,0,1:T(8,128)(2,1)S(1)}, u32[]{:S(2)}, u32[]{:S(2)}) collective-permute-start(bf16[20,2,529]{2,0,1:T(8,128)(2,1)S(1)} %get-tuple-element.47), channel_id=1, source_target_pairs={{0,8},{8,16},{16,24},{24,32},{32,40},{40,48},{48,56},{56,64},{64,7... | collective-permute-start | bytes 126968 | tf_op jit(solution)/shard_map/ppermute | solution.py:38
  76.1 15.0 %collective-permute-start.3 = (bf16[20,2,529]{2,0,1:T(8,128)(2,1)S(1)}, bf16[20,2,529]{2,0,1:T(8,128)(2,1)S(1)}, u32[]{:S(2)}, u32[]{:S(2)}) collective-permute-start(bf16[20,2,529]{2,0,1:T(8,128)(2,1)S(1)} %get-tuple-element.48), channel_id=1, source_target_pairs={{8,0},{16,8},{24,16},{32,24},{40,32},{48,40},{56,48},{64,56},{72,6... | collective-permute-start | bytes 126968 | tf_op jit(solution)/shard_map/ppermute | solution.py:38
  91.1 15.5 %copy-start.6 = (bf16[20,2,529]{2,0,1:T(8,128)(2,1)}, bf16[20,2,529]{2,0,1:T(8,128)(2,1)S(1)}, u32[]{:S(2)}) copy-start(bf16[20,2,529]{2,0,1:T(8,128)(2,1)S(1)} %collective-permute-done.3) | copy-start | bytes 126964
  96.8 43.9 %collective-permute-start.4 = (bf16[16,128,640]{2,1,0:T(8,128)(2,1)S(1)}, bf16[16,128,640]{2,1,0:T(8,128)(2,1)}, u32[]{:S(2)}, u32[]{:S(2)}) collective-permute-start(bf16[16,128,640]{2,1,0:T(8,128)(2,1)S(1)} %all-to-all-done.1.weight_ref.weight0_ref), channel_id=1, source_target_pairs={{0,1},{1,0},{2,3},{3,2},{4,5},{5,4},{6,7},{7,6},{8,9},{9,8},{10,11... | collective-permute-start | bytes 7864328 | tf_op jit(solution)/shard_map/ppermute | solution.py:247
  117.9 2.4 %copy-start.8 = (bf16[16,32,72]{2,1,0:T(8,128)(2,1)S(1)}, bf16[16,32,72]{2,1,0:T(8,128)(2,1)}, u32[]{:S(2)}) copy-start(bf16[16,32,72]{2,1,0:T(8,128)(2,1)} %copy.60) | copy-start | bytes 221188
  120.4 2.7 %copy-start.1 = (bf16[16,32,529]{2,0,1:T(8,128)(2,1)S(1)}, bf16[16,32,529]{2,0,1:T(8,128)(2,1)}, u32[]{:S(2)}) copy-start(bf16[16,32,529]{2,0,1:T(8,128)(2,1)} %concatenate.80) | copy-start | bytes 1625092
  120.4 2.6 %copy-start.3 = (bf16[2,32,529]{2,0,1:T(2,128)(2,1)S(1)}, bf16[2,32,529]{2,0,1:T(2,128)(2,1)}, u32[]{:S(2)}) copy-start(bf16[2,32,529]{2,0,1:T(2,128)(2,1)} %copy-done.2) | copy-start | bytes 203140
  120.4 2.6 %copy-start.5 = (bf16[2,32,529]{2,0,1:T(2,128)(2,1)S(1)}, bf16[2,32,529]{2,0,1:T(2,128)(2,1)}, u32[]{:S(2)}) copy-start(bf16[2,32,529]{2,0,1:T(2,128)(2,1)} %copy-done.4) | copy-start | bytes 203140
  120.4 2.6 %copy-start.7 = (bf16[20,2,529]{2,0,1:T(8,128)(2,1)S(1)}, bf16[20,2,529]{2,0,1:T(8,128)(2,1)}, u32[]{:S(2)}) copy-start(bf16[20,2,529]{2,0,1:T(8,128)(2,1)} %copy-done.6) | copy-start | bytes 126964
  140.7 4.9 %copy-start.10 = (bf16[256]{0:T(256)(128)(2,1)S(1)}, bf16[256]{0:T(256)(128)(2,1)}, u32[]{:S(2)}) copy-start(bf16[256]{0:T(256)(128)(2,1)} %param.13) | copy-start | bytes 1540

commit v3 on v2

--- a/solution.py
+++ b/solution.py
@@ -1,3 +1,5 @@
+import functools
+
 import jax
 import jax.numpy as jnp
 from jax import lax
@@ -7,13 +9,15 @@
 
 KPAD = 2560
 HID = 256
+AUX = 128
+PACK = 2 * HID + AUX
 F32 = jnp.float32
 BF16 = jnp.bfloat16
 NT = (((1,), (1,)), ((), ()))
 NN = (((1,), (0,)), ((), ()))
 VMEM = pl.BlockSpec(memory_space=pltpu.VMEM)
 SMEM = pl.BlockSpec(memory_space=pltpu.SMEM)
-PARAMS = pltpu.CompilerParams(vmem_limit_bytes=48 * 1024 * 1024)
+PARAMS = pltpu.CompilerParams(vmem_limit_bytes=16 * 1024 * 1024)
 
 
 def pack_weights(conv_weight):
@@ -38,32 +42,142 @@
     return lax.ppermute(block, axes, pairs)
 
 
-def widened(block, width):
-    for axes, dim in ((("x", "c"), 0), (("z", "y"), 1)):
-        size = block.shape[dim]
-        low = shifted(lax.slice_in_dim(block, size - width, size, axis=dim), axes, 1)
-        high = shifted(lax.slice_in_dim(block, 0, width, axis=dim), axes, -1)
-        block = jnp.concatenate([low, block, high], axis=dim)
-    return block
-
-
-def taps_of(source, rows, cols):
-    return [source[a : a + rows, b : b + cols] for a in range(3) for b in range(3)]
-
-
-def patches_of(hidden, frame):
-    rows, cols = frame.shape[0] - 2, frame.shape[1] - 2
-    pieces = [] if hidden is None else taps_of(hidden, rows, cols)
-    pieces += taps_of(frame, rows, cols)
-    out = jnp.concatenate(pieces, -1)
-    width = -(-out.shape[2] // 256) * 256
-    out = jnp.pad(out, ((0, 0), (0, 0), (0, width - out.shape[2])))
-    return out.reshape(rows * cols, width)
-
-
-def ringed(core, left, right):
-    pad = ((0, 6), (0, 0))
-    return jnp.concatenate([core, jnp.pad(left, pad), jnp.pad(right, pad)], axis=0)
+def ends_kernel(hidden_ref, cell_ref, aux_ref, last_out, first_out):
+    for out, start in ((last_out, 14), (first_out, 0)):
+        for j in range(2):
+            rows = slice(j * 32, (j + 1) * 32)
+            out[rows, :HID] = hidden_ref[start + j]
+            out[rows, HID : 2 * HID] = cell_ref[start + j].astype(BF16)
+            out[rows, 2 * HID :] = aux_ref[start + j]
+
+
+def ends_of(hidden, cell, aux):
+    return pl.pallas_call(
+        ends_kernel,
+        out_shape=(jax.ShapeDtypeStruct((64, PACK), BF16),) * 2,
+        in_specs=[VMEM] * 3,
+        out_specs=(VMEM, VMEM),
+        compiler_params=PARAMS,
+        cost_estimate=pl.CostEstimate(flops=0, bytes_accessed=1_000_000, transcendentals=0),
+    )(hidden, cell, aux)
+
+
+def sides_kernel(hidden_ref, cell_ref, aux_ref, low_ref, high_ref, last_out, first_out, last, first):
+    for out, scratch, start, at in ((last_out, last, 16, 14), (first_out, first, 0, 0)):
+        cols = slice(start, start + 16)
+        for r in range(20):
+            into = slice(2 * r, 2 * r + 2)
+            if r < 2 or r >= 18:
+                ref, j = (low_ref, r) if r < 2 else (high_ref, r - 18)
+                block = ref[j * 32 + start : j * 32 + start + 16, :].astype(F32)
+                scratch[into, :] = block[at : at + 2]
+            else:
+                scratch[into, :HID] = hidden_ref[r - 2, cols, :].astype(F32)[at : at + 2]
+                scratch[into, HID : 2 * HID] = cell_ref[r - 2, cols, :][at : at + 2]
+                scratch[into, 2 * HID :] = aux_ref[r - 2, cols, :].astype(F32)[at : at + 2]
+        scratch[40:, :] = jnp.zeros((8, PACK), F32)
+        out[...] = scratch[...].astype(BF16)
+
+
+def sides_of(hidden, cell, aux, low, high):
+    return pl.pallas_call(
+        sides_kernel,
+        out_shape=(jax.ShapeDtypeStruct((48, PACK), BF16),) * 2,
+        in_specs=[VMEM] * 5,
+        out_specs=(VMEM, VMEM),
+        scratch_shapes=[pltpu.VMEM((48, PACK), F32)] * 2,
+        compiler_params=PARAMS,
+        cost_estimate=pl.CostEstimate(flops=0, bytes_accessed=1_000_000, transcendentals=0),
+    )(hidden, cell, aux, low, high)
+
+
+def placer(tap, first, cx):
+    source = lax.broadcasted_iota(jnp.int32, (AUX, AUX), 0)
+    target = lax.broadcasted_iota(jnp.int32, (AUX, AUX), 1)
+    hit = (target - source == tap * cx - first) & (source >= first) & (source < first + cx)
+    return jnp.where(hit, 1.0, 0.0).astype(BF16)
+
+
+def prep_kernel(
+    cx,
+    hidden_ref,
+    cell_ref,
+    aux_ref,
+    low_ref,
+    high_ref,
+    left_ref,
+    right_ref,
+    patches_out,
+    frame_out,
+    cell_out,
+    keep_out,
+    wide,
+):
+    wide[2:18, 8:40, :HID] = hidden_ref[...].astype(F32)
+    wide[2:18, 8:40, HID:] = aux_ref[...].astype(F32)
+    for ref, row in ((low_ref, 0), (high_ref, 18)):
+        both = ref[...].astype(F32).reshape(2, 32, PACK)
+        wide[row : row + 2, 8:40, :HID] = both[:, :, :HID]
+        wide[row : row + 2, 8:40, HID:] = both[:, :, 2 * HID :]
+    cell_out[:32, :] = low_ref[32:, HID : 2 * HID].astype(F32)
+    cell_out[32:544, :] = cell_ref[...].reshape(512, HID)
+    cell_out[544:576, :] = high_ref[:32, HID : 2 * HID].astype(F32)
+    cell_out[576:, :] = jnp.zeros((48, HID), F32)
+    for ref, col, near, base in ((left_ref, 6, 1, 575), (right_ref, 40, 0, 599)):
+        rows = ref[...].astype(F32)
+        for r in range(20):
+            pair = rows[2 * r : 2 * r + 2]
+            wide[r, col : col + 2, :HID] = pair[:, :HID]
+            wide[r, col : col + 2, HID:] = pair[:, 2 * HID :]
+            if 1 <= r < 19:
+                cell_out[base + r : base + r + 1, :] = pair[near : near + 1, HID : 2 * HID]
+
+    def border(b, a):
+        pad = jnp.zeros((6, HID + AUX), F32)
+        left = wide[a : a + 18, 6 + b, :]
+        right = wide[a : a + 18, 39 + b, :]
+        return jnp.concatenate([left, pad, right, pad], axis=0).astype(BF16)
+
+    first = jnp.zeros((624, AUX), F32)
+    second = jnp.zeros((512, AUX), F32)
+    for b in range(3):
+        cols = wide[:, 7 + b : 39 + b, :].astype(BF16)
+        for a in range(3):
+            t = 3 * a + b
+            core = cols[a : a + 18].reshape(576, HID + AUX)
+            edge = border(b, a)
+            patches_out[:576, t * HID : (t + 1) * HID] = core[:, :HID]
+            patches_out[576:, t * HID : (t + 1) * HID] = edge[:, :HID]
+            aux = jnp.concatenate([core[:, HID:], edge[:, HID:]], axis=0)
+            first = first + lax.dot_general(aux, placer(t, 0, cx), NN, preferred_element_type=F32)
+            second = second + lax.dot_general(
+                aux[32:544], placer(t, cx, cx), NN, preferred_element_type=F32
+            )
+            if t == 4:
+                source = lax.broadcasted_iota(jnp.int32, (AUX, AUX), 0)
+                copy = jnp.where(source == 2 * cx, 1.0, 0.0).astype(BF16)
+                keep_out[...] = lax.dot_general(aux, copy, NN, preferred_element_type=F32)
+    patches_out[:, 9 * HID : 9 * HID + AUX] = first.astype(BF16)
+    patches_out[:, 9 * HID + AUX :] = jnp.zeros((624, AUX), BF16)
+    frame_out[:, :AUX] = second.astype(BF16)
+    frame_out[:, AUX:] = jnp.zeros((512, AUX), BF16)
+
+
+def prepared(cx, hidden, cell, aux, low, high, left, right):
+    return pl.pallas_call(
+        functools.partial(prep_kernel, cx),
+        out_shape=(
+            jax.ShapeDtypeStruct((624, KPAD), BF16),
+            jax.ShapeDtypeStruct((512, HID), BF16),
+            jax.ShapeDtypeStruct((624, HID), F32),
+            jax.ShapeDtypeStruct((624, 128), F32),
+        ),
+        in_specs=[VMEM] * 7,
+        out_specs=(VMEM,) * 4,
+        scratch_shapes=[pltpu.VMEM((20, 48, HID + AUX), F32)],
+        compiler_params=PARAMS,
+        cost_estimate=pl.CostEstimate(flops=0, bytes_accessed=12_000_000, transcendentals=0),
+    )(hidden, cell, aux, low, high, left, right)
 
 
 def chooser(half, shape, channel_axis):
@@ -174,7 +288,7 @@
     hid, cell = None, None
     for i, (weight_ref, cell_ref) in enumerate(((weight0_ref, cell0_ref), (weight1_ref, cell1_ref))):
         new_hid, new_cell = half_step(
-            patches[...], weight_ref, bias_ref[i], cell_ref[32:544, :], keep_ref[...]
+            patches[...], weight_ref, bias_ref[i], cell_ref[32:544, :], keep_ref[32:544, :]
         )
         one = lax.dot_general(new_hid, choices[i], NN, preferred_element_type=F32)
         two = moved(new_cell, choices[i])
@@ -206,35 +320,26 @@
     )(halves, *hids, *cells, frame, *weights, bias, keep, keep2, proj)
 
 
-def compute(halves, own, other, wide, cell_init, land_mask, bias, projection, cx):
+def compute(halves, own, other, prep, land_mask, bias, projection):
     rows, cols = land_mask.shape
-    width = HID
-    keep = land_mask.astype(F32)
-    hidden = wide[..., :width]
-    frame0 = wide[..., 2 * width : 2 * width + cx]
-    frame1 = wide[..., 2 * width + cx : 2 * width + 2 * cx]
-    keep_wide = wide[1:-1, 1:-1, 2 * width + 2 * cx :].astype(F32)
-    cell_wide = wide[1:-1, 1:-1, width : 2 * width].astype(F32)
-    middle = jnp.concatenate([cell_wide[:1, 1:-1], cell_init, cell_wide[-1:, 1:-1]], axis=0)
-    cell1 = ringed(middle.reshape(-1, width), cell_wide[:, 0], cell_wide[:, -1])
-    keep1 = ringed(keep_wide[:, 1:-1].reshape(-1, 1), keep_wide[:, 0], keep_wide[:, -1])
-    patches1 = ringed(
-        patches_of(hidden[:, 1:-1], frame0[:, 1:-1]),
-        patches_of(hidden[:, :3], frame0[:, :3]),
-        patches_of(hidden[:, -3:], frame0[:, -3:]),
-    )
-    frame2 = patches_of(None, frame1[1:-1, 1:-1])
-
+    patches1, frame2, cell1, keep1 = prep
     by_half = jnp.transpose(bias.reshape(4, 4, 4, 2, 8), (3, 0, 2, 1, 4)).reshape(2, 4, 128)
     bias2 = jnp.stack([by_half[halves[0]], by_half[halves[1]]])
     hid0, cell0 = first_step(halves[:1], patches1, own, bias2[0], cell1, keep1)
     hid1, cell1 = first_step(halves[1:], patches1, other, bias2[1], cell1, keep1)
-    proj = jnp.broadcast_to(projection[None], (16, width))
+    proj = jnp.broadcast_to(projection[None], (16, HID))
     hidden, cell, flux = second_step(
         halves, (hid0, hid1), (cell0, cell1), frame2, (own, other), bias2,
-        keep.reshape(-1, 1), keep, proj,
+        keep1, land_mask.astype(F32), proj,
     )
-    return hidden.reshape(rows, cols, width), cell.reshape(rows, cols, width), flux
+    return hidden.reshape(rows, cols, HID), cell.reshape(rows, cols, HID), flux
+
+
+def aux_of(frames, land_mask):
+    rows, cols = land_mask.shape
+    both = jnp.transpose(frames, (1, 2, 0, 3)).reshape(rows, cols, -1)
+    aux = jnp.concatenate([both, land_mask.astype(BF16)[..., None]], axis=-1)
+    return jnp.pad(aux, ((0, 0), (0, 0), (0, AUX - aux.shape[2])))
 
 
 def body(frames, hidden_init, cell_init, conv_weight, bias, land_mask, projection):
@@ -243,21 +348,22 @@
     packed = pack_weights(conv_weight)
     unit = lax.dynamic_slice(packed, (c * 8, x * (KPAD // 4)), (8, KPAD // 4))
     by_z = spread(unit, "z").reshape(128, KPAD // 4)
+
+    state = (hidden_init, cell_init, aux_of(frames, land_mask))
+    last, first = ends_of(*state)
+    low = shifted(last, ("x", "c"), 1)
+    high = shifted(first, ("x", "c"), -1)
+    by_z, low, high = lax.optimization_barrier((by_z, low, high))
+
     own = spread(by_z, ("y", "x"))
+    last, first = sides_of(*state, low, high)
+    left = shifted(last, ("z", "y"), 1)
+    right = shifted(first, ("z", "y"), -1)
+    prep = prepared(cx, *state, low, high, left, right)
+    own, prep = lax.optimization_barrier((own, prep))
     other = lax.ppermute(own, "c", [(0, 1), (1, 0)])
-    packed_state = jnp.concatenate(
-        [
-            hidden_init,
-            cell_init.astype(BF16),
-            frames[0],
-            frames[1],
-            land_mask.astype(BF16)[..., None],
-        ],
-        axis=-1,
-    )
-    wide = widened(packed_state, 2)
     halves = jnp.stack([c, 1 - c]).astype(jnp.int32)
-    return compute(halves, own, other, wide, cell_init, land_mask, bias, projection, cx)
+    return compute(halves, own, other, prep, land_mask, bias, projection)
 
 
 def solution(mesh):

time: 154 us -> 102 us (0.66)
  the two profiles are of different devices: /device:TPU:37 before, /device:TPU:129 now
where the time goes in v3:
time: 102 us
  starting transfers between devices  37.4 us (37%)
  waiting for transfers between devices  30 us (29%)
  Pallas kernels  17.2 us (17%)
  local copies, waits for them, and re-layouts  15.1 us (15%)
  other arithmetic  1.02 us (1%)
    all_to_all x2, starting transfers between devices, spread(): return lax.all_to_all(copies, axes, 0, 0)  19.9 us
    ppermute x4, waiting for transfers between devices, shifted(): return lax.ppermute(block, axes, pairs)  15.6 us
    ppermute x4, starting transfers between devices, shifted(): return lax.ppermute(block, axes, pairs)  14.8 us
    all_to_all x2, waiting for transfers between devices, spread(): return lax.all_to_all(copies, axes, 0, 0)  14.4 us
    unnamed x38, local copies, waits for them, and re-layouts  11 us
    pallas_call x2, Pallas kernels, first_step(): pl.pallas_call(first_kernel, out_shape=(jax.ShapeDtypeStruct((count, 128)...  7.89 us
    pallas_call x1, Pallas kernels, second_step(): pl.pallas_call(second_kernel, out_shape=(jax.ShapeDtypeStruct((512, HID),...  7.63 us
    ppermute x1, starting transfers between devices, body(): other = lax.ppermute(own, 'c', [(0, 1), (1, 0)])  2.71 us
  transfers between devices with their start and end apart: 7, of which 3 were waited for; matrix products, arithmetic and copies ran while one was open for 2% of the time, Pallas kernels for 5%

profile of v3, /device:TPU:129, one launch (start us, length us, event | category | flops | bytes accessed | tf_op | source)
XLA Modules:
  0.0 101.6 jit_solution(10077691430535107658)
XLA Ops:
  0.6 1.0 slice_bitcast_fusion
  1.6 0.8 slice.9
  2.4 0.1 copy.12
  2.5 0.1 copy.13
  2.6 0.7 broadcast_in_dim.8
  3.3 13.3 %all-to-all-start = ((bf16[16,8,640]{2,1,0:T(8,128)(2,1)}), bf16[16,8,640]{2,1,0:T(8,128)(2,1)S(1)}, u32[]{:S(2)}, u32[]{:S(2)}) async-start(bf16[16,8,640]{2,1,0:T(8,128)(2,1)} %broadcast_in_dim.8), calls=%async_computation | async-start | bytes 327680 | tf_op jit(solution)/shard_map/all_to_all | solution.py:36
  16.6 0.8 fusion.6
  17.4 0.2 copy.16
  17.6 0.9 copy.20
  18.4 0.1 copy.15
  18.6 0.1 fusion.2.aux_ref
  18.7 0.0 copy-start
  18.7 1.0 %copy-done = f32[16,32,256]{2,1,0:T(8,128)S(1)} copy-done((f32[16,32,256]{2,1,0:T(8,128)S(1)}, f32[16,32,256]{2,1,0:T(8,128)}, u32[]{:S(2)}) %copy-start) | copy-done | bytes 524312
  19.7 0.9 copy-done.5
  20.7 4.2 %collective-permute-start = (bf16[64,640]{1,0:T(8,128)(2,1)S(1)}, bf16[64,640]{1,0:T(8,128)(2,1)S(1)}, u32[]{:S(2)}, u32[]{:S(2)}) collective-permute-start(bf16[64,640]{1,0:T(8,128)(2,1)S(1)} %get-tuple-element.26), channel_id=1, source_target_pairs={{0,1},{1,2},{2,3},{3,4},{4,5},{5,6},{6,7},{8,9},{9,10},{10,11},{11... | collective-permute-start | bytes 245768 | tf_op jit(solution)/shard_map/ppermute | solution.py:42
  24.9 1.9 %collective-permute-start.1 = (bf16[64,640]{1,0:T(8,128)(2,1)S(1)}, bf16[64,640]{1,0:T(8,128)(2,1)S(1)}, u32[]{:S(2)}, u32[]{:S(2)}) collective-permute-start(bf16[64,640]{1,0:T(8,128)(2,1)S(1)} %get-tuple-element.27), channel_id=1, source_target_pairs={{1,0},{2,1},{3,2},{4,3},{5,4},{6,5},{7,6},{9,8},{10,9},{11,10},{12... | collective-permute-start | bytes 245768 | tf_op jit(solution)/shard_map/ppermute | solution.py:42
  26.9 0.0 collective-permute-done.low_ref
  26.9 3.8 %collective-permute-done.1.high_ref = bf16[64,640]{1,0:T(8,128)(2,1)S(1)} collective-permute-done((bf16[64,640]{1,0:T(8,128)(2,1)S(1)}, bf16[64,640]{1,0:T(8,128)(2,1)S(1)}, u32[]{:S(2)}, u32[]{:S(2)}) %collective-permute-start.1) | collective-permute-done | bytes 81952 | tf_op jit(solution)/shard_map/ppermute | solution.py:42
  30.7 0.0 all-to-all-done
  30.7 1.8 %broadcast_in_dim.10 = bf16[16,128,640]{2,1,0:T(8,128)(2,1)} broadcast(bf16[128,640]{1,0:T(8,128)(2,1)S(1)} %bitcast.22), dimensions={1,2} | broadcast | bytes 2785280 | tf_op jit(solution)/shard_map/broadcast_in_dim | solution.py:35
  32.6 6.6 %all-to-all-start.1 = ((bf16[16,128,640]{2,1,0:T(8,128)(2,1)}), bf16[16,128,640]{2,1,0:T(8,128)(2,1)}, u32[]{:S(2)}, u32[]{:S(2)}) async-start(bf16[16,128,640]{2,1,0:T(8,128)(2,1)} %broadcast_in_dim.10), calls=%async_computation.1 | async-start | bytes 5242880 | tf_op jit(solution)/shard_map/all_to_all | solution.py:36
  39.2 0.0 copy-done.7
  39.3 0.1 shard_map.95
  39.3 3.2 %collective-permute-start.2 = (bf16[48,640]{1,0:T(8,128)(2,1)S(1)}, bf16[48,640]{1,0:T(8,128)(2,1)S(1)}, u32[]{:S(2)}, u32[]{:S(2)}) collective-permute-start(bf16[48,640]{1,0:T(8,128)(2,1)S(1)} %get-tuple-element.31), channel_id=1, source_target_pairs={{0,8},{8,16},{16,24},{24,32},{32,40},{40,48},{48,56},{56,64},{64,7... | collective-permute-start | bytes 184328 | tf_op jit(solution)/shard_map/ppermute | solution.py:42
  42.6 5.4 %collective-permute-start.3 = (bf16[48,640]{1,0:T(8,128)(2,1)S(1)}, bf16[48,640]{1,0:T(8,128)(2,1)S(1)}, u32[]{:S(2)}, u32[]{:S(2)}) collective-permute-start(bf16[48,640]{1,0:T(8,128)(2,1)S(1)} %get-tuple-element.32), channel_id=1, source_target_pairs={{8,0},{16,8},{24,16},{32,24},{40,32},{48,40},{56,48},{64,56},{72,6... | collective-permute-start | bytes 184328 | tf_op jit(solution)/shard_map/ppermute | solution.py:42
  48.0 11.8 %collective-permute-done.2.left_ref = bf16[48,640]{1,0:T(8,128)(2,1)S(1)} collective-permute-done((bf16[48,640]{1,0:T(8,128)(2,1)S(1)}, bf16[48,640]{1,0:T(8,128)(2,1)S(1)}, u32[]{:S(2)}, u32[]{:S(2)}) %collective-permute-start.2) | collective-permute-done | bytes 61472 | tf_op jit(solution)/shard_map/ppermute | solution.py:42
  59.7 0.0 collective-permute-done.3.right_ref
  59.7 1.0 %copy-done.2 = f32[16,32,256]{2,1,0:T(8,128)S(1)} copy-done((f32[16,32,256]{2,1,0:T(8,128)S(1)}, f32[16,32,256]{2,1,0:T(8,128)}, u32[]{:S(2)}) %copy-start.2) | copy-done | bytes 524312
  60.8 0.9 copy-done.8
  61.7 0.9 copy-done.13
  62.6 1.6 %shard_map.96 = (bf16[624,2560]{1,0:T(8,128)(2,1)S(1)}, bf16[512,256]{1,0:T(8,128)(2,1)S(1)}, f32[624,256]{1,0:T(8,128)S(1)}, f32[624,128]{1,0:T(8,128)S(1)}) custom-call(bf16[16,32,256]{2,1,0:T(8,128)(2,1)S(1)} %copy-done.6, f32[16,32,256]{2,1,0:T(8,128)S(1)} %copy-done.2, bf16[16,32,128]{2,1,0:T(8,128)(2,1)S(1)} %copy-done.8, ...), custom_call_target="tpu_custom_call" | custom-call | bytes 12000000 | tf_op jit(solution)/shard_map/pallas_call | solution.py:167
  64.1 0.8 copy-done.3
  65.0 0.7 copy-done.9
  65.7 0.7 copy-done.14
  66.4 14.4 %all-to-all-done.1.weight_ref.weight0_ref = bf16[16,128,640]{2,1,0:T(8,128)(2,1)} async-done(((bf16[16,128,640]{2,1,0:T(8,128)(2,1)}), bf16[16,128,640]{2,1,0:T(8,128)(2,1)}, u32[]{:S(2)}, u32[]{:S(2)}) %all-to-all-start.1) | async-done | bytes 2621472 | tf_op jit(solution)/shard_map/all_to_all | solution.py:36
  80.8 2.7 %collective-permute-start.4 = (bf16[16,128,640]{2,1,0:T(8,128)(2,1)}, bf16[16,128,640]{2,1,0:T(8,128)(2,1)}, u32[]{:S(2)}, u32[]{:S(2)}) collective-permute-start(bf16[16,128,640]{2,1,0:T(8,128)(2,1)} %all-to-all-done.1.weight_ref.weight0_ref), channel_id=1, source_target_pairs={{0,1},{1,0},{2,3},{3,2},{4,5},{5,4},{6,7},{7,6},{8,9},{9,8},{10,11... | collective-permute-start | bytes 7864328 | tf_op jit(solution)/shard_map/ppermute | solution.py:364
  83.5 0.1 reshape.37
  83.7 0.1 reshape.38
  83.8 0.1 pad_add_fusion.half_ref
  83.9 1.1 %copy-done.4 = f32[624,256]{1,0:T(8,128)S(1)} copy-done((f32[624,256]{1,0:T(8,128)S(1)}, f32[624,256]{1,0:T(8,128)}, u32[]{:S(2)}) %copy-start.4) | copy-done | bytes 639000
  85.0 1.0 copy-done.10
  85.9 3.9 %shard_map.97 = (bf16[624,128]{1,0:T(8,128)(2,1)S(1)}, f32[624,128]{1,0:T(8,128)S(1)}) custom-call(s32[1]{0:T(128)} %bitcast.half_ref, bf16[624,2560]{1,0:T(8,128)(2,1)S(1)} %get-tuple-element.37.patches_ref, bf16[16,128,640]{2,1,0:T(8,128)(2,1)} %all-to-all-done.1.weight_ref.weight0_ref, f32[4,128]{1,0:T(4,128)S(1)} %bitcast.21, f32[624,256]{1,0:T(8,128)S(1)} %copy-done.4, ...), custom_call_target="tpu_custom_call" | custom-call | flops 1635778560 | bytes 6000000 | tf_op jit(solution)/shard_map/pallas_call | solution.py:240
  89.9 0.0 collective-permute-done.4.weight_ref.weight1_ref
  89.9 0.0 copy-start.17
  89.9 0.0 copy-start.11
  89.9 0.0 copy-start.15
  89.9 4.0 %shard_map.98 = (bf16[624,128]{1,0:T(8,128)(2,1)S(1)}, f32[624,128]{1,0:T(8,128)S(1)}) custom-call(s32[1]{0:T(128)} %bitcast.1.half_ref, bf16[624,2560]{1,0:T(8,128)(2,1)S(1)} %get-tuple-element.37.patches_ref, bf16[16,128,640]{2,1,0:T(8,128)(2,1)} %collective-permute-done.4.weight_ref.weight1_ref, f32[4,128]{1,0:T(4,128)S(1)} %bitcast.20, ...), custom_call_target="tpu_custom_call" | custom-call | flops 1635778560 | bytes 6000000 | tf_op jit(solution)/shard_map/pallas_call | solution.py:240
  93.9 7.6 %shard_map.99 = (bf16[512,256]{1,0:T(8,128)(2,1)}, f32[512,256]{1,0:T(8,128)}, f32[16,32]{1,0:T(8,128)}) custom-call(s32[2]{0:T(128)S(1)} %pad_add_fusion.half_ref, bf16[624,128]{1,0:T(8,128)(2,1)S(1)} %get-tuple-element.41.hid0_ref, bf16[624,128]{1,0:T(8,128)(2,1)S(1)} %get-tuple-element.42.hid1_ref, f32[624,128]{1,0:T(8,128)S(1)} %get-tuple-element.43.cell0_ref, ...), custom_call_target="tpu_custom_call" | custom-call | flops 2684354560 | bytes 8000000 | tf_op jit(solution)/shard_map/pallas_call | solution.py:306
  (28 shorter events, 0.1 us)
Async XLA Ops:
  3.3 27.4 %all-to-all-start = ((bf16[16,8,640]{2,1,0:T(8,128)(2,1)}), bf16[16,8,640]{2,1,0:T(8,128)(2,1)S(1)}, u32[]{:S(2)}, u32[]{:S(2)}) async-start(bf16[16,8,640]{2,1,0:T(8,128)(2,1)} %broadcast_in_dim.8), calls=%async_computation | async-start | bytes 327680 | tf_op jit(solution)/shard_map/all_to_all | solution.py:36
  18.7 1.0 %copy-start = (f32[16,32,256]{2,1,0:T(8,128)S(1)}, f32[16,32,256]{2,1,0:T(8,128)}, u32[]{:S(2)}) copy-start(f32[16,32,256]{2,1,0:T(8,128)} %cell_ref.5) | copy-start | bytes 1572868
  19.7 0.9 copy-start.5
  20.7 18.5 %copy-start.7 = (bf16[16,32,128]{2,1,0:T(8,128)(2,1)}, bf16[16,32,128]{2,1,0:T(8,128)(2,1)S(1)}, u32[]{:S(2)}) copy-start(bf16[16,32,128]{2,1,0:T(8,128)(2,1)S(1)} %fusion.2.aux_ref) | copy-start | bytes 393220
  20.7 6.2 %collective-permute-start = (bf16[64,640]{1,0:T(8,128)(2,1)S(1)}, bf16[64,640]{1,0:T(8,128)(2,1)S(1)}, u32[]{:S(2)}, u32[]{:S(2)}) collective-permute-start(bf16[64,640]{1,0:T(8,128)(2,1)S(1)} %get-tuple-element.26), channel_id=1, source_target_pairs={{0,1},{1,2},{2,3},{3,4},{4,5},{5,6},{6,7},{8,9},{9,10},{10,11},{11... | collective-permute-start | bytes 245768 | tf_op jit(solution)/shard_map/ppermute | solution.py:42
  24.9 5.8 %collective-permute-start.1 = (bf16[64,640]{1,0:T(8,128)(2,1)S(1)}, bf16[64,640]{1,0:T(8,128)(2,1)S(1)}, u32[]{:S(2)}, u32[]{:S(2)}) collective-permute-start(bf16[64,640]{1,0:T(8,128)(2,1)S(1)} %get-tuple-element.27), channel_id=1, source_target_pairs={{1,0},{2,1},{3,2},{4,3},{5,4},{6,5},{7,6},{9,8},{10,9},{11,10},{12... | collective-permute-start | bytes 245768 | tf_op jit(solution)/shard_map/ppermute | solution.py:42
  30.7 8.5 %copy-start.12 = (bf16[64,640]{1,0:T(8,128)(2,1)}, bf16[64,640]{1,0:T(8,128)(2,1)S(1)}, u32[]{:S(2)}) copy-start(bf16[64,640]{1,0:T(8,128)(2,1)S(1)} %collective-permute-done.1.high_ref) | copy-start | bytes 245764
  32.6 6.7 %copy-start.1 = (f32[16,32,256]{2,1,0:T(8,128)S(1)}, f32[16,32,256]{2,1,0:T(8,128)}, u32[]{:S(2)}) copy-start(f32[16,32,256]{2,1,0:T(8,128)} %cell_ref.5) | copy-start | bytes 1572868
  32.6 6.7 %copy-start.6 = (bf16[16,32,256]{2,1,0:T(8,128)(2,1)S(1)}, bf16[16,32,256]{2,1,0:T(8,128)(2,1)}, u32[]{:S(2)}) copy-start(bf16[16,32,256]{2,1,0:T(8,128)(2,1)} %hidden_ref.5) | copy-start | bytes 786436
  32.6 50.9 %copy-start.16 = (f32[1024]{0:T(1024)S(1)}, f32[1024]{0:T(1024)}, u32[]{:S(2)}) copy-start(f32[1024]{0:T(1024)} %param.11) | copy-start | bytes 12292
  32.6 48.2 %all-to-all-start.1 = ((bf16[16,128,640]{2,1,0:T(8,128)(2,1)}), bf16[16,128,640]{2,1,0:T(8,128)(2,1)}, u32[]{:S(2)}, u32[]{:S(2)}) async-start(bf16[16,128,640]{2,1,0:T(8,128)(2,1)} %broadcast_in_dim.10), calls=%async_computation.1 | async-start | bytes 5242880 | tf_op jit(solution)/shard_map/all_to_all | solution.py:36
  39.3 20.4 %collective-permute-start.2 = (bf16[48,640]{1,0:T(8,128)(2,1)S(1)}, bf16[48,640]{1,0:T(8,128)(2,1)S(1)}, u32[]{:S(2)}, u32[]{:S(2)}) collective-permute-start(bf16[48,640]{1,0:T(8,128)(2,1)S(1)} %get-tuple-element.31), channel_id=1, source_target_pairs={{0,8},{8,16},{16,24},{24,32},{32,40},{40,48},{48,56},{56,64},{64,7... | collective-permute-start | bytes 184328 | tf_op jit(solution)/shard_map/ppermute | solution.py:42
  42.6 17.2 %collective-permute-start.3 = (bf16[48,640]{1,0:T(8,128)(2,1)S(1)}, bf16[48,640]{1,0:T(8,128)(2,1)S(1)}, u32[]{:S(2)}, u32[]{:S(2)}) collective-permute-start(bf16[48,640]{1,0:T(8,128)(2,1)S(1)} %get-tuple-element.32), channel_id=1, source_target_pairs={{8,0},{16,8},{24,16},{32,24},{40,32},{48,40},{56,48},{64,56},{72,6... | collective-permute-start | bytes 184328 | tf_op jit(solution)/shard_map/ppermute | solution.py:42
  59.7 1.0 %copy-start.2 = (f32[16,32,256]{2,1,0:T(8,128)S(1)}, f32[16,32,256]{2,1,0:T(8,128)}, u32[]{:S(2)}) copy-start(f32[16,32,256]{2,1,0:T(8,128)} %cell_ref.5) | copy-start | bytes 1572868
  60.8 0.9 copy-start.8
  61.7 0.9 copy-start.13
  64.1 0.8 copy-start.3
  65.0 0.7 copy-start.9
  65.7 0.7 copy-start.14
  80.8 9.1 %collective-permute-start.4 = (bf16[16,128,640]{2,1,0:T(8,128)(2,1)}, bf16[16,128,640]{2,1,0:T(8,128)(2,1)}, u32[]{:S(2)}, u32[]{:S(2)}) collective-permute-start(bf16[16,128,640]{2,1,0:T(8,128)(2,1)} %all-to-all-done.1.weight_ref.weight0_ref), channel_id=1, source_target_pairs={{0,1},{1,0},{2,3},{3,2},{4,5},{5,4},{6,7},{7,6},{8,9},{9,8},{10,11... | collective-permute-start | bytes 7864328 | tf_op jit(solution)/shard_map/ppermute | solution.py:364
  83.9 1.1 %copy-start.4 = (f32[624,256]{1,0:T(8,128)S(1)}, f32[624,256]{1,0:T(8,128)}, u32[]{:S(2)}) copy-start(f32[624,256]{1,0:T(8,128)} %copy-done.3) | copy-start | bytes 1916932
  85.0 1.0 copy-start.10
  89.9 4.0 %copy-start.17 = (bf16[256]{0:T(256)(128)(2,1)S(1)}, bf16[256]{0:T(256)(128)(2,1)}, u32[]{:S(2)}) copy-start(bf16[256]{0:T(256)(128)(2,1)} %param.13) | copy-start | bytes 1540
  89.9 4.0 %copy-start.11 = (f32[624,128]{1,0:T(8,128)S(1)}, f32[624,128]{1,0:T(8,128)}, u32[]{:S(2)}) copy-start(f32[624,128]{1,0:T(8,128)} %copy-done.9) | copy-start | bytes 958468
  89.9 4.0 %copy-start.15 = (bf16[512,256]{1,0:T(8,128)(2,1)S(1)}, bf16[512,256]{1,0:T(8,128)(2,1)}, u32[]{:S(2)}) copy-start(bf16[512,256]{1,0:T(8,128)(2,1)} %copy-done.14) | copy-start | bytes 786436

commit v4 on v3

--- a/solution.py
+++ b/solution.py
@@ -8,6 +8,7 @@
 from jax.sharding import Mesh, PartitionSpec as P
 
 KPAD = 2560
+CHUNK = KPAD // 4
 HID = 256
 AUX = 128
 PACK = 2 * HID + AUX
@@ -34,6 +35,11 @@
     count = lax.axis_size(axes)
     copies = jnp.broadcast_to(block[None], (count,) + block.shape)
     return lax.all_to_all(copies, axes, 0, 0)
+
+
+def turned(block, axis, step):
+    count = lax.axis_size(axis)
+    return lax.ppermute(block, axis, [(i, (i + step) % count) for i in range(count)])
 
 
 def shifted(block, axes, step):
@@ -96,6 +102,13 @@
     target = lax.broadcasted_iota(jnp.int32, (AUX, AUX), 1)
     hit = (target - source == tap * cx - first) & (source >= first) & (source < first + cx)
     return jnp.where(hit, 1.0, 0.0).astype(BF16)
+
+
+def put(ref, rows, lane, value):
+    for i in range(value.shape[1] // 128):
+        group = lane // 128 + i
+        at = group % 5 * 128
+        ref[group // 5, rows, at : at + 128] = value[:, i * 128 : (i + 1) * 128]
 
 
 def prep_kernel(
@@ -146,8 +159,8 @@
             t = 3 * a + b
             core = cols[a : a + 18].reshape(576, HID + AUX)
             edge = border(b, a)
-            patches_out[:576, t * HID : (t + 1) * HID] = core[:, :HID]
-            patches_out[576:, t * HID : (t + 1) * HID] = edge[:, :HID]
+            put(patches_out, slice(0, 576), t * HID, core[:, :HID])
+            put(patches_out, slice(576, 624), t * HID, edge[:, :HID])
             aux = jnp.concatenate([core[:, HID:], edge[:, HID:]], axis=0)
             first = first + lax.dot_general(aux, placer(t, 0, cx), NN, preferred_element_type=F32)
             second = second + lax.dot_general(
@@ -157,8 +170,8 @@
                 source = lax.broadcasted_iota(jnp.int32, (AUX, AUX), 0)
                 copy = jnp.where(source == 2 * cx, 1.0, 0.0).astype(BF16)
                 keep_out[...] = lax.dot_general(aux, copy, NN, preferred_element_type=F32)
-    patches_out[:, 9 * HID : 9 * HID + AUX] = first.astype(BF16)
-    patches_out[:, 9 * HID + AUX :] = jnp.zeros((624, AUX), BF16)
+    put(patches_out, slice(0, 624), 9 * HID, first.astype(BF16))
+    put(patches_out, slice(0, 624), 9 * HID + AUX, jnp.zeros((624, AUX), BF16))
     frame_out[:, :AUX] = second.astype(BF16)
     frame_out[:, AUX:] = jnp.zeros((512, AUX), BF16)
 
@@ -167,7 +180,7 @@
     return pl.pallas_call(
         functools.partial(prep_kernel, cx),
         out_shape=(
-            jax.ShapeDtypeStruct((624, KPAD), BF16),
+            jax.ShapeDtypeStruct((4, 624, CHUNK), BF16),
             jax.ShapeDtypeStruct((512, HID), BF16),
             jax.ShapeDtypeStruct((624, HID), F32),
             jax.ShapeDtypeStruct((624, 128), F32),
@@ -176,7 +189,7 @@
         out_specs=(VMEM,) * 4,
         scratch_shapes=[pltpu.VMEM((20, 48, HID + AUX), F32)],
         compiler_params=PARAMS,
-        cost_estimate=pl.CostEstimate(flops=0, bytes_accessed=12_000_000, transcendentals=0),
+        cost_estimate=pl.CostEstimate(flops=0, bytes_accessed=100_000, transcendentals=0),
     )(hidden, cell, aux, low, high, left, right)
 
 
@@ -201,68 +214,72 @@
     return dots[0] + (dots[1] + dots[2])
 
 
-def half_step(patches, weight_ref, bias, cell, keep):
-    gates = []
-    for pair in range(2):
-        rhs = jnp.concatenate(
-            [
-                jnp.concatenate(
-                    [
-                        weight_ref[y * 4 + x, q * 32 : (q + 1) * 32, :]
-                        for q in (2 * pair, 2 * pair + 1)
-                        for y in range(4)
-                    ],
-                    axis=0,
-                )
-                for x in range(4)
-            ],
-            axis=1,
-        )
-        both = lax.dot_general(patches, rhs, NT, preferred_element_type=F32)
-        gates.append(both[:, :128] + bias[2 * pair][None])
-        gates.append(both[:, 128:] + bias[2 * pair + 1][None])
-    sig = lambda v: 0.5 * jnp.tanh(0.5 * v) + 0.5
-    cell = sig(gates[1]) * cell + sig(gates[0]) * jnp.tanh(gates[2])
-    hidden = (keep * sig(gates[3]) * jnp.tanh(cell)).astype(BF16)
-    return hidden, cell
-
-
-def first_kernel(half_ref, patches_ref, weight_ref, bias_ref, cell_ref, keep_ref, hid_out, cell_out):
-    choice = chooser(half_ref[0], (HID, 128), 0)
-    cell = moved(cell_ref[...], choice)
-    hidden, cell = half_step(patches_ref[...], weight_ref, bias_ref[...], cell, keep_ref[...])
-    hid_out[...] = hidden
-    cell_out[...] = cell
-
-
-def first_step(half, patches, weight, bias, cell, keep):
-    count = patches.shape[0]
+def product(patches, weight_ref, pair):
+    rhs = jnp.concatenate(
+        [
+            weight_ref[y, q * 32 : (q + 1) * 32, :]
+            for q in (2 * pair, 2 * pair + 1)
+            for y in range(4)
+        ],
+        axis=0,
+    )
+    return lax.dot_general(patches, rhs, NT, preferred_element_type=F32)
+
+
+def sigmoid(value):
+    return 0.5 * jnp.tanh(0.5 * value) + 0.5
+
+
+def updated(sums, bias, cell, keep):
+    in_gate = sigmoid(sums[0][:, :128] + bias[0][None])
+    decay_factor = sigmoid(sums[0][:, 128:] + bias[1][None])
+    candidate = jnp.tanh(sums[1][:, :128] + bias[2][None])
+    out_gate = sigmoid(sums[1][:, 128:] + bias[3][None])
+    cell = decay_factor * cell + in_gate * candidate
+    return (keep * out_gate * jnp.tanh(cell)).astype(BF16), cell
+
+
+def partial_kernel(slot, more, ids_ref, patches_ref, own_ref, other_ref, *refs):
+    total = refs[-1]
+    patches = patches_ref[ids_ref[slot]]
+    for i, weight_ref in enumerate((own_ref, other_ref)):
+        for pair in range(2):
+            value = product(patches, weight_ref, pair)
+            if more:
+                value = value + refs[0][i, pair]
+            total[i, pair] = value
+
+
+def partial(slot, ids, patches, own, other, *before):
+    count = patches.shape[1]
     return pl.pallas_call(
-        first_kernel,
-        out_shape=(
-            jax.ShapeDtypeStruct((count, 128), BF16),
-            jax.ShapeDtypeStruct((count, 128), F32),
-        ),
-        in_specs=[SMEM] + [VMEM] * 5,
-        out_specs=(VMEM, VMEM),
+        functools.partial(partial_kernel, slot, len(before) > 0),
+        out_shape=jax.ShapeDtypeStruct((2, 2, count, HID), F32),
+        in_specs=[SMEM] + [VMEM] * (3 + len(before)),
+        out_specs=VMEM,
+        input_output_aliases={4: 0} if before else {},
         compiler_params=PARAMS,
-        cost_estimate=pl.CostEstimate(
-            flops=2 * count * KPAD * 512, bytes_accessed=6_000_000, transcendentals=count * 640
-        ),
-    )(half, patches, weight, bias, cell, keep)
-
-
-def second_kernel(
+        cost_estimate=pl.CostEstimate(flops=0, bytes_accessed=100_000, transcendentals=0),
+    )(ids, patches, own, other, *before)
+
+
+def final_kernel(
+    ids_ref,
     half_ref,
-    hid0_ref,
-    hid1_ref,
-    cell0_ref,
-    cell1_ref,
+    patches_ref,
+    total_ref,
+    own0,
+    own1,
+    own2,
+    own3,
+    other0,
+    other1,
+    other2,
+    other3,
+    bias_ref,
+    cell_ref,
+    keep_ref,
     frame_ref,
-    weight0_ref,
-    weight1_ref,
-    bias_ref,
-    keep_ref,
     keep2_ref,
     proj_ref,
     hid_out,
@@ -271,10 +288,22 @@
     wide,
     patches,
 ):
+    weights = ((own0, own1, own2, own3), (other0, other1, other2, other3))
     choices = [chooser(half_ref[i], (128, HID), 1) for i in range(2)]
-    natural = lax.dot_general(
-        hid0_ref[...], choices[0], NN, preferred_element_type=F32
-    ) + lax.dot_general(hid1_ref[...], choices[1], NN, preferred_element_type=F32)
+    natural, cells = None, []
+    for i in range(2):
+        sums = []
+        for pair in range(2):
+            value = total_ref[i, pair]
+            for slot in (1, 2, 3):
+                value = value + product(patches_ref[ids_ref[slot]], weights[i][slot], pair)
+            sums.append(value)
+        cell = moved(cell_ref[...], chooser(half_ref[i], (HID, 128), 0))
+        hid, cell = updated(sums, bias_ref[i], cell, keep_ref[...])
+        cells.append(cell[32:544])
+        one = lax.dot_general(hid, choices[i], NN, preferred_element_type=F32)
+        natural = one if natural is None else natural + one
+
     wide[:, 8:40, :] = natural[:576].reshape(18, 32, HID)
     for row in range(18):
         wide[row, 7:8, :] = natural[576 + row : 577 + row]
@@ -282,14 +311,19 @@
     for b in range(3):
         moved_rows = wide[:, 7 + b : 39 + b, :].astype(BF16)
         for a in range(3):
-            t = 3 * a + b
-            patches[:, t * HID : (t + 1) * HID] = moved_rows[a : a + 16].reshape(512, HID)
-    patches[:, 9 * HID :] = frame_ref[...]
+            put(patches, slice(0, 512), (3 * a + b) * HID, moved_rows[a : a + 16].reshape(512, HID))
+    put(patches, slice(0, 512), 9 * HID, frame_ref[...])
+
     hid, cell = None, None
-    for i, (weight_ref, cell_ref) in enumerate(((weight0_ref, cell0_ref), (weight1_ref, cell1_ref))):
-        new_hid, new_cell = half_step(
-            patches[...], weight_ref, bias_ref[i], cell_ref[32:544, :], keep_ref[32:544, :]
-        )
+    for i in range(2):
+        sums = []
+        for pair in range(2):
+            value = None
+            for slot in range(4):
+                part = product(patches[ids_ref[slot]], weights[i][slot], pair)
+                value = part if value is None else value + part
+            sums.append(value)
+        new_hid, new_cell = updated(sums, bias_ref[i], cells[i], keep_ref[32:544, :])
         one = lax.dot_general(new_hid, choices[i], NN, preferred_element_type=F32)
         two = moved(new_cell, choices[i])
         hid = one if hid is None else hid + one
@@ -302,37 +336,42 @@
         flux_out[row : row + 1, :] = flux[0:1, row * 32 : (row + 1) * 32] * keep2_ref[row : row + 1, :]
 
 
-def second_step(halves, hids, cells, frame, weights, bias, keep, keep2, proj):
+def finished(ids, halves, patches, total, own, other, bias, cell, keep, frame, keep2, proj):
     return pl.pallas_call(
-        second_kernel,
+        final_kernel,
         out_shape=(
             jax.ShapeDtypeStruct((512, HID), BF16),
             jax.ShapeDtypeStruct((512, HID), F32),
             jax.ShapeDtypeStruct((16, 32), F32),
         ),
-        in_specs=[SMEM] + [VMEM] * 11,
+        in_specs=[SMEM] * 2 + [VMEM] * 16,
         out_specs=(VMEM, VMEM, VMEM),
-        scratch_shapes=[pltpu.VMEM((18, 48, HID), F32), pltpu.VMEM((512, KPAD), BF16)],
+        scratch_shapes=[pltpu.VMEM((18, 48, HID), F32), pltpu.VMEM((4, 512, CHUNK), BF16)],
         compiler_params=PARAMS,
         cost_estimate=pl.CostEstimate(
-            flops=2 * 512 * KPAD * 1024, bytes_accessed=8_000_000, transcendentals=512 * 1280
+            flops=2 * 824 * KPAD * 1024, bytes_accessed=14_000_000, transcendentals=1136 * 1280
         ),
-    )(halves, *hids, *cells, frame, *weights, bias, keep, keep2, proj)
-
-
-def compute(halves, own, other, prep, land_mask, bias, projection):
+    )(ids, halves, patches, total, *own, *other, bias, cell, keep, frame, keep2, proj)
+
+
+def compute(ids, halves, own, swapped, prep, land_mask, bias2, proj):
     rows, cols = land_mask.shape
     patches1, frame2, cell1, keep1 = prep
-    by_half = jnp.transpose(bias.reshape(4, 4, 4, 2, 8), (3, 0, 2, 1, 4)).reshape(2, 4, 128)
-    bias2 = jnp.stack([by_half[halves[0]], by_half[halves[1]]])
-    hid0, cell0 = first_step(halves[:1], patches1, own, bias2[0], cell1, keep1)
-    hid1, cell1 = first_step(halves[1:], patches1, other, bias2[1], cell1, keep1)
-    proj = jnp.broadcast_to(projection[None], (16, HID))
-    hidden, cell, flux = second_step(
-        halves, (hid0, hid1), (cell0, cell1), frame2, (own, other), bias2,
-        keep1, land_mask.astype(F32), proj,
+    other = [swapped(0, own[0])]
+    total = partial(0, ids, patches1, own[0], other[0])
+    later, total = lax.optimization_barrier((own[1:], total))
+    own = own[:1] + later
+    other += [swapped(slot, own[slot]) for slot in (1, 2, 3)]
+    hidden, cell, flux = finished(
+        ids, halves, patches1, total, own, other, bias2, cell1, keep1, frame2,
+        land_mask.astype(F32), proj,
     )
     return hidden.reshape(rows, cols, HID), cell.reshape(rows, cols, HID), flux
+
+
+def bias_of(bias, c):
+    by_half = jnp.transpose(bias.reshape(4, 4, 4, 2, 8), (3, 0, 2, 1, 4)).reshape(2, 4, 128)
+    return jnp.where(c == 0, by_half, by_half[::-1])
 
 
 def aux_of(frames, land_mask):
@@ -353,17 +392,24 @@
     last, first = ends_of(*state)
     low = shifted(last, ("x", "c"), 1)
     high = shifted(first, ("x", "c"), -1)
-    by_z, low, high = lax.optimization_barrier((by_z, low, high))
-
-    own = spread(by_z, ("y", "x"))
+    halves = jnp.stack([c, 1 - c]).astype(jnp.int32)
+    ids = jnp.stack([x, (x + 2) % 4, (x + 1) % 4, (x + 3) % 4]).astype(jnp.int32)
+    proj = jnp.broadcast_to(projection[None], (16, HID))
+    bias2 = bias_of(bias, c)
+    by_z, low, high, halves, ids, proj, bias2 = lax.optimization_barrier(
+        (by_z, low, high, halves, ids, proj, bias2)
+    )
+
+    by_y = spread(by_z, "y")
     last, first = sides_of(*state, low, high)
     left = shifted(last, ("z", "y"), 1)
     right = shifted(first, ("z", "y"), -1)
+    by_y, left, right = lax.optimization_barrier((by_y, left, right))
+
+    own = [by_y] + [turned(by_y, "x", step) for step in (2, -1, 1)]
     prep = prepared(cx, *state, low, high, left, right)
-    own, prep = lax.optimization_barrier((own, prep))
-    other = lax.ppermute(own, "c", [(0, 1), (1, 0)])
-    halves = jnp.stack([c, 1 - c]).astype(jnp.int32)
-    return compute(halves, own, other, prep, land_mask, bias, projection)
+    swapped = lambda slot, piece: turned(piece, "c", 1)
+    return compute(ids, halves, own, swapped, prep, land_mask, bias2, proj)
 
 
 def solution(mesh):

time: 102 us -> 109 us (1.069)
  the two profiles are of different devices: /device:TPU:129 before, /device:TPU:27 now
where the time goes in v4:
time: 109 us; the launch traced here: 108 us
  starting transfers between devices  51.6 us (47%)
  waiting for transfers between devices  33.2 us (30%)
  Pallas kernels  13.9 us (13%)
  local copies, waits for them, and re-layouts  7.73 us (7%)
  other arithmetic  1.09 us (1%)
    ppermute x7, waiting for transfers between devices, turned(): lax.ppermute(block, axis, [(i, (i + step) % count) for i in range(count)])  24.9 us
    ppermute x7, starting transfers between devices, turned(): lax.ppermute(block, axis, [(i, (i + step) % count) for i in range(count)])  21.4 us
    all_to_all x2, starting transfers between devices, spread(): return lax.all_to_all(copies, axes, 0, 0)  19 us
    ppermute x4, starting transfers between devices, shifted(): return lax.ppermute(block, axes, pairs)  11.2 us
    pallas_call x1, Pallas kernels, finished(): pl.pallas_call(final_kernel, out_shape=(jax.ShapeDtypeStruct((512, HID),...  10.4 us
    ppermute x4, waiting for transfers between devices, shifted(): return lax.ppermute(block, axes, pairs)  8.28 us
    unnamed x12, local copies, waits for them, and re-layouts  3.84 us
  transfers between devices with their start and end apart: 13, of which 7 were waited for; matrix products, arithmetic and copies ran while one was open for 3% of the time, Pallas kernels for 3%

profile of v4, /device:TPU:27, one launch (start us, length us, event | category | flops | bytes accessed | tf_op | source)
XLA Modules:
  0.0 108.5 jit_solution(16828880779631248895)
XLA Ops:
  0.6 0.0 copy-start.1
  0.6 0.0 copy-start.3
  0.7 0.8 slice.9
  1.5 1.0 slice_bitcast_fusion
  2.5 0.1 copy.12
  2.6 0.1 copy.13
  2.7 0.7 broadcast_in_dim.8
  3.4 14.9 %all-to-all-start = ((bf16[16,8,640]{2,1,0:T(8,128)(2,1)}), bf16[16,8,640]{2,1,0:T(8,128)(2,1)S(1)}, u32[]{:S(2)}, u32[]{:S(2)}) async-start(bf16[16,8,640]{2,1,0:T(8,128)(2,1)} %broadcast_in_dim.8), calls=%async_computation | async-start | bytes 327680 | tf_op jit(solution)/shard_map/all_to_all | solution.py:37
  18.3 0.8 fusion.6
  19.1 0.9 copy.20
  20.0 0.1 copy.15
  20.1 0.2 copy.16
  20.3 0.1 fusion.2.aux_ref
  20.4 0.0 copy-start
  20.4 1.0 copy-done
  21.5 0.9 copy-done.2
  22.4 4.0 %collective-permute-start = (bf16[64,640]{1,0:T(8,128)(2,1)S(1)}, bf16[64,640]{1,0:T(8,128)(2,1)S(1)}, u32[]{:S(2)}, u32[]{:S(2)}) collective-permute-start(bf16[64,640]{1,0:T(8,128)(2,1)S(1)} %get-tuple-element.28), channel_id=1, source_target_pairs={{0,1},{1,2},{2,3},{3,4},{4,5},{5,6},{6,7},{8,9},{9,10},{10,11},{11... | collective-permute-start | bytes 245768 | tf_op jit(solution)/shard_map/ppermute | solution.py:48
  26.4 1.9 %collective-permute-start.1 = (bf16[64,640]{1,0:T(8,128)(2,1)S(1)}, bf16[64,640]{1,0:T(8,128)(2,1)S(1)}, u32[]{:S(2)}, u32[]{:S(2)}) collective-permute-start(bf16[64,640]{1,0:T(8,128)(2,1)S(1)} %get-tuple-element.29), channel_id=1, source_target_pairs={{1,0},{2,1},{3,2},{4,3},{5,4},{6,5},{7,6},{9,8},{10,9},{11,10},{12... | collective-permute-start | bytes 245768 | tf_op jit(solution)/shard_map/ppermute | solution.py:48
  28.4 0.8 reshape.37
  29.2 0.1 reshape.38
  29.4 0.1 pad_add_fusion.half_ref
  29.4 0.1 pad_add_fusion.1.ids_ref
  29.5 0.0 collective-permute-done.low_ref
  29.5 2.9 %collective-permute-done.1.high_ref = bf16[64,640]{1,0:T(8,128)(2,1)S(1)} collective-permute-done((bf16[64,640]{1,0:T(8,128)(2,1)S(1)}, bf16[64,640]{1,0:T(8,128)(2,1)S(1)}, u32[]{:S(2)}, u32[]{:S(2)}) %collective-permute-start.1) | collective-permute-done | bytes 81952 | tf_op jit(solution)/shard_map/ppermute | solution.py:48
  32.5 0.0 all-to-all-done
  32.5 0.9 broadcast_in_dim.11
  33.4 4.1 %all-to-all-start.1 = ((bf16[4,128,640]{2,1,0:T(8,128)(2,1)}), bf16[4,128,640]{2,1,0:T(8,128)(2,1)S(1)}, u32[]{:S(2)}, u32[]{:S(2)}) async-start(bf16[4,128,640]{2,1,0:T(8,128)(2,1)} %broadcast_in_dim.11), calls=%async_computation.1 | async-start | bytes 1310720 | tf_op jit(solution)/shard_map/all_to_all | solution.py:37
  37.5 0.1 shard_map.95
  37.6 3.3 %collective-permute-start.2 = (bf16[48,640]{1,0:T(8,128)(2,1)S(1)}, bf16[48,640]{1,0:T(8,128)(2,1)S(1)}, u32[]{:S(2)}, u32[]{:S(2)}) collective-permute-start(bf16[48,640]{1,0:T(8,128)(2,1)S(1)} %get-tuple-element.35), channel_id=1, source_target_pairs={{0,8},{8,16},{16,24},{24,32},{32,40},{40,48},{48,56},{56,64},{64,7... | collective-permute-start | bytes 184328 | tf_op jit(solution)/shard_map/ppermute | solution.py:48
  40.9 2.0 %collective-permute-start.3 = (bf16[48,640]{1,0:T(8,128)(2,1)S(1)}, bf16[48,640]{1,0:T(8,128)(2,1)S(1)}, u32[]{:S(2)}, u32[]{:S(2)}) collective-permute-start(bf16[48,640]{1,0:T(8,128)(2,1)S(1)} %get-tuple-element.36), channel_id=1, source_target_pairs={{8,0},{16,8},{24,16},{32,24},{40,32},{48,40},{56,48},{64,56},{72,6... | collective-permute-start | bytes 184328 | tf_op jit(solution)/shard_map/ppermute | solution.py:48
  42.9 1.7 %collective-permute-done.2.left_ref = bf16[48,640]{1,0:T(8,128)(2,1)S(1)} collective-permute-done((bf16[48,640]{1,0:T(8,128)(2,1)S(1)}, bf16[48,640]{1,0:T(8,128)(2,1)S(1)}, u32[]{:S(2)}, u32[]{:S(2)}) %collective-permute-start.2) | collective-permute-done | bytes 61472 | tf_op jit(solution)/shard_map/ppermute | solution.py:48
  44.6 3.6 %collective-permute-done.3.right_ref = bf16[48,640]{1,0:T(8,128)(2,1)S(1)} collective-permute-done((bf16[48,640]{1,0:T(8,128)(2,1)S(1)}, bf16[48,640]{1,0:T(8,128)(2,1)S(1)}, u32[]{:S(2)}, u32[]{:S(2)}) %collective-permute-start.3) | collective-permute-done | bytes 61472 | tf_op jit(solution)/shard_map/ppermute | solution.py:48
  48.2 0.0 all-to-all-done.1.own_ref.own0
  48.2 5.0 %collective-permute-start.7 = (bf16[4,128,640]{2,1,0:T(8,128)(2,1)S(1)}, bf16[4,128,640]{2,1,0:T(8,128)(2,1)S(1)}, u32[]{:S(2)}, u32[]{:S(2)}) collective-permute-start(bf16[4,128,640]{2,1,0:T(8,128)(2,1)S(1)} %all-to-all-done.1.own_ref.own0), channel_id=1, source_target_pairs={{0,1},{1,0},{2,3},{3,2},{4,5},{5,4},{6,7},{7,6},{8,9},{9,8},{10,11... | collective-permute-start | bytes 1966088 | tf_op jit(solution)/shard_map/ppermute | solution.py:42
  53.3 3.1 %collective-permute-start.6 = (bf16[4,128,640]{2,1,0:T(8,128)(2,1)S(1)}, bf16[4,128,640]{2,1,0:T(8,128)(2,1)S(1)}, u32[]{:S(2)}, u32[]{:S(2)}) collective-permute-start(bf16[4,128,640]{2,1,0:T(8,128)(2,1)S(1)} %all-to-all-done.1.own_ref.own0), channel_id=1, source_target_pairs={{0,2},{2,4},{4,6},{6,0},{1,3},{3,5},{5,7},{7,1},{8,10},{10,12},{12... | collective-permute-start | bytes 1966088 | tf_op jit(solution)/shard_map/ppermute | solution.py:42
  56.4 2.2 %collective-permute-start.5 = (bf16[4,128,640]{2,1,0:T(8,128)(2,1)S(1)}, bf16[4,128,640]{2,1,0:T(8,128)(2,1)S(1)}, u32[]{:S(2)}, u32[]{:S(2)}) collective-permute-start(bf16[4,128,640]{2,1,0:T(8,128)(2,1)S(1)} %all-to-all-done.1.own_ref.own0), channel_id=1, source_target_pairs={{0,6},{2,0},{4,2},{6,4},{1,7},{3,1},{5,3},{7,5},{8,14},{10,8},{12,... | collective-permute-start | bytes 1966088 | tf_op jit(solution)/shard_map/ppermute | solution.py:42
  58.6 3.8 %collective-permute-start.4 = (bf16[4,128,640]{2,1,0:T(8,128)(2,1)S(1)}, bf16[4,128,640]{2,1,0:T(8,128)(2,1)S(1)}, u32[]{:S(2)}, u32[]{:S(2)}) collective-permute-start(bf16[4,128,640]{2,1,0:T(8,128)(2,1)S(1)} %all-to-all-done.1.own_ref.own0), channel_id=1, source_target_pairs={{0,4},{2,6},{4,0},{6,2},{1,5},{3,7},{5,1},{7,3},{8,12},{10,14},{12... | collective-permute-start | bytes 1966088 | tf_op jit(solution)/shard_map/ppermute | solution.py:42
  62.3 1.7 %shard_map.96 = (bf16[4,624,640]{2,1,0:T(8,128)(2,1)S(1)}, bf16[512,256]{1,0:T(8,128)(2,1)S(1)}, f32[624,256]{1,0:T(8,128)S(1)}, f32[624,128]{1,0:T(8,128)S(1)}) custom-call(bf16[16,32,256]{2,1,0:T(8,128)(2,1)S(1)} %copy-done.3, f32[16,32,256]{2,1,0:T(8,128)S(1)} %copy-done.1, bf16[16,32,128]{2,1,0:T(8,128)(2,1)S(1)} %fusion.2.aux_ref, ...), custom_call_target="tpu_custom_call" | custom-call | bytes 100000 | tf_op jit(solution)/shard_map/pallas_call | solution.py:180
  64.0 1.7 %shard_map.97.total_ref = f32[2,2,624,256]{3,2,1,0:T(8,128)S(1)} custom-call(s32[4]{0:T(128)S(1)} %pad_add_fusion.1.ids_ref, bf16[4,624,640]{2,1,0:T(8,128)(2,1)S(1)} %get-tuple-element.39.patches_ref, bf16[4,128,640]{2,1,0:T(8,128)(2,1)S(1)} %all-to-all-done.1.own_ref.own0, bf16[4,128,640]{2,1,0:T(8,128)(2,1)S(1)} %collective-permute-done.7.other_ref.other0), custom_call_target="tpu_custom_call" | custom-call | bytes 100000 | tf_op jit(solution)/shard_map/pallas_call | solution.py:255
  65.8 5.7 %collective-permute-done.6.own3 = bf16[4,128,640]{2,1,0:T(8,128)(2,1)S(1)} collective-permute-done((bf16[4,128,640]{2,1,0:T(8,128)(2,1)S(1)}, bf16[4,128,640]{2,1,0:T(8,128)(2,1)S(1)}, u32[]{:S(2)}, u32[]{:S(2)}) %collective-permute-start.6) | collective-permute-done | bytes 655392 | tf_op jit(solution)/shard_map/ppermute | solution.py:42
  71.5 2.8 %collective-permute-done.5.own2 = bf16[4,128,640]{2,1,0:T(8,128)(2,1)S(1)} collective-permute-done((bf16[4,128,640]{2,1,0:T(8,128)(2,1)S(1)}, bf16[4,128,640]{2,1,0:T(8,128)(2,1)S(1)}, u32[]{:S(2)}, u32[]{:S(2)}) %collective-permute-start.5) | collective-permute-done | bytes 655392 | tf_op jit(solution)/shard_map/ppermute | solution.py:42
  74.3 14.7 %collective-permute-done.4.own1 = bf16[4,128,640]{2,1,0:T(8,128)(2,1)S(1)} collective-permute-done((bf16[4,128,640]{2,1,0:T(8,128)(2,1)S(1)}, bf16[4,128,640]{2,1,0:T(8,128)(2,1)S(1)}, u32[]{:S(2)}, u32[]{:S(2)}) %collective-permute-start.4) | collective-permute-done | bytes 655392 | tf_op jit(solution)/shard_map/ppermute | solution.py:42
  89.0 3.0 %collective-permute-start.8 = (bf16[4,128,640]{2,1,0:T(8,128)(2,1)S(1)}, bf16[4,128,640]{2,1,0:T(8,128)(2,1)S(1)}, u32[]{:S(2)}, u32[]{:S(2)}) collective-permute-start(bf16[4,128,640]{2,1,0:T(8,128)(2,1)S(1)} %collective-permute-done.4.own1), channel_id=1, source_target_pairs={{0,1},{1,0},{2,3},{3,2},{4,5},{5,4},{6,7},{7,6},{8,9},{9,8},{10,11... | collective-permute-start | bytes 1966088 | tf_op jit(solution)/shard_map/ppermute | solution.py:42
  92.0 1.9 %collective-permute-start.9 = (bf16[4,128,640]{2,1,0:T(8,128)(2,1)S(1)}, bf16[4,128,640]{2,1,0:T(8,128)(2,1)S(1)}, u32[]{:S(2)}, u32[]{:S(2)}) collective-permute-start(bf16[4,128,640]{2,1,0:T(8,128)(2,1)S(1)} %collective-permute-done.5.own2), channel_id=1, source_target_pairs={{0,1},{1,0},{2,3},{3,2},{4,5},{5,4},{6,7},{7,6},{8,9},{9,8},{10,11... | collective-permute-start | bytes 1966088 | tf_op jit(solution)/shard_map/ppermute | solution.py:42
  93.9 2.4 %collective-permute-start.10 = (bf16[4,128,640]{2,1,0:T(8,128)(2,1)S(1)}, bf16[4,128,640]{2,1,0:T(8,128)(2,1)S(1)}, u32[]{:S(2)}, u32[]{:S(2)}) collective-permute-start(bf16[4,128,640]{2,1,0:T(8,128)(2,1)S(1)} %collective-permute-done.6.own3), channel_id=1, source_target_pairs={{0,1},{1,0},{2,3},{3,2},{4,5},{5,4},{6,7},{7,6},{8,9},{9,8},{10,11... | collective-permute-start | bytes 1966088 | tf_op jit(solution)/shard_map/ppermute | solution.py:42
  96.3 0.0 collective-permute-done.8.other1
  96.4 1.7 %collective-permute-done.10.other3 = bf16[4,128,640]{2,1,0:T(8,128)(2,1)S(1)} collective-permute-done((bf16[4,128,640]{2,1,0:T(8,128)(2,1)S(1)}, bf16[4,128,640]{2,1,0:T(8,128)(2,1)S(1)}, u32[]{:S(2)}, u32[]{:S(2)}) %collective-permute-start.10) | collective-permute-done | bytes 655392 | tf_op jit(solution)/shard_map/ppermute | solution.py:42
  98.1 10.4 %shard_map.98 = (bf16[512,256]{1,0:T(8,128)(2,1)}, f32[512,256]{1,0:T(8,128)}, f32[16,32]{1,0:T(8,128)}) custom-call(s32[4]{0:T(128)S(1)} %pad_add_fusion.1.ids_ref, s32[2]{0:T(128)S(1)} %pad_add_fusion.half_ref, bf16[4,624,640]{2,1,0:T(8,128)(2,1)S(1)} %get-tuple-element.39.patches_ref, f32[2,2,624,256]{3,2,1,0:T(8,128)S(1)} %shard_map.97.total_ref, ...), custom_call_target="tpu_custom_call" | custom-call | flops 4320133120 | bytes 14000000 | tf_op jit(solution)/shard_map/pallas_call | solution.py:340
  (13 shorter events, 0.1 us)
Async XLA Ops:
  0.6 36.9 %copy-start.1 = (f32[16,32,256]{2,1,0:T(8,128)S(1)}, f32[16,32,256]{2,1,0:T(8,128)}, u32[]{:S(2)}) copy-start(f32[16,32,256]{2,1,0:T(8,128)} %cell_ref.5) | copy-start | bytes 1572868
  0.6 36.9 %copy-start.3 = (bf16[16,32,256]{2,1,0:T(8,128)(2,1)S(1)}, bf16[16,32,256]{2,1,0:T(8,128)(2,1)}, u32[]{:S(2)}) copy-start(bf16[16,32,256]{2,1,0:T(8,128)(2,1)} %hidden_ref.5) | copy-start | bytes 786436
  0.7 31.8 %copy-start.4 = (bf16[256]{0:T(256)(128)(2,1)S(1)}, bf16[256]{0:T(256)(128)(2,1)}, u32[]{:S(2)}) copy-start(bf16[256]{0:T(256)(128)(2,1)} %param.13) | copy-start | bytes 1540
  3.4 29.1 %all-to-all-start = ((bf16[16,8,640]{2,1,0:T(8,128)(2,1)}), bf16[16,8,640]{2,1,0:T(8,128)(2,1)S(1)}, u32[]{:S(2)}, u32[]{:S(2)}) async-start(bf16[16,8,640]{2,1,0:T(8,128)(2,1)} %broadcast_in_dim.8), calls=%async_computation | async-start | bytes 327680 | tf_op jit(solution)/shard_map/all_to_all | solution.py:37
  20.4 1.0 copy-start
  21.5 0.9 copy-start.2
  22.4 7.1 %collective-permute-start = (bf16[64,640]{1,0:T(8,128)(2,1)S(1)}, bf16[64,640]{1,0:T(8,128)(2,1)S(1)}, u32[]{:S(2)}, u32[]{:S(2)}) collective-permute-start(bf16[64,640]{1,0:T(8,128)(2,1)S(1)} %get-tuple-element.28), channel_id=1, source_target_pairs={{0,1},{1,2},{2,3},{3,4},{4,5},{5,6},{6,7},{8,9},{9,10},{10,11},{11... | collective-permute-start | bytes 245768 | tf_op jit(solution)/shard_map/ppermute | solution.py:48
  26.4 6.1 %collective-permute-start.1 = (bf16[64,640]{1,0:T(8,128)(2,1)S(1)}, bf16[64,640]{1,0:T(8,128)(2,1)S(1)}, u32[]{:S(2)}, u32[]{:S(2)}) collective-permute-start(bf16[64,640]{1,0:T(8,128)(2,1)S(1)} %get-tuple-element.29), channel_id=1, source_target_pairs={{1,0},{2,1},{3,2},{4,3},{5,4},{6,5},{7,6},{9,8},{10,9},{11,10},{12... | collective-permute-start | bytes 245768 | tf_op jit(solution)/shard_map/ppermute | solution.py:48
  33.4 14.9 %all-to-all-start.1 = ((bf16[4,128,640]{2,1,0:T(8,128)(2,1)}), bf16[4,128,640]{2,1,0:T(8,128)(2,1)S(1)}, u32[]{:S(2)}, u32[]{:S(2)}) async-start(bf16[4,128,640]{2,1,0:T(8,128)(2,1)} %broadcast_in_dim.11), calls=%async_computation.1 | async-start | bytes 1310720 | tf_op jit(solution)/shard_map/all_to_all | solution.py:37
  37.6 7.0 %collective-permute-start.2 = (bf16[48,640]{1,0:T(8,128)(2,1)S(1)}, bf16[48,640]{1,0:T(8,128)(2,1)S(1)}, u32[]{:S(2)}, u32[]{:S(2)}) collective-permute-start(bf16[48,640]{1,0:T(8,128)(2,1)S(1)} %get-tuple-element.35), channel_id=1, source_target_pairs={{0,8},{8,16},{16,24},{24,32},{32,40},{40,48},{48,56},{56,64},{64,7... | collective-permute-start | bytes 184328 | tf_op jit(solution)/shard_map/ppermute | solution.py:48
  40.9 7.4 %collective-permute-start.3 = (bf16[48,640]{1,0:T(8,128)(2,1)S(1)}, bf16[48,640]{1,0:T(8,128)(2,1)S(1)}, u32[]{:S(2)}, u32[]{:S(2)}) collective-permute-start(bf16[48,640]{1,0:T(8,128)(2,1)S(1)} %get-tuple-element.36), channel_id=1, source_target_pairs={{8,0},{16,8},{24,16},{32,24},{40,32},{48,40},{56,48},{64,56},{72,6... | collective-permute-start | bytes 184328 | tf_op jit(solution)/shard_map/ppermute | solution.py:48
  48.2 15.8 %collective-permute-start.7 = (bf16[4,128,640]{2,1,0:T(8,128)(2,1)S(1)}, bf16[4,128,640]{2,1,0:T(8,128)(2,1)S(1)}, u32[]{:S(2)}, u32[]{:S(2)}) collective-permute-start(bf16[4,128,640]{2,1,0:T(8,128)(2,1)S(1)} %all-to-all-done.1.own_ref.own0), channel_id=1, source_target_pairs={{0,1},{1,0},{2,3},{3,2},{4,5},{5,4},{6,7},{7,6},{8,9},{9,8},{10,11... | collective-permute-start | bytes 1966088 | tf_op jit(solution)/shard_map/ppermute | solution.py:42
  53.3 18.2 %collective-permute-start.6 = (bf16[4,128,640]{2,1,0:T(8,128)(2,1)S(1)}, bf16[4,128,640]{2,1,0:T(8,128)(2,1)S(1)}, u32[]{:S(2)}, u32[]{:S(2)}) collective-permute-start(bf16[4,128,640]{2,1,0:T(8,128)(2,1)S(1)} %all-to-all-done.1.own_ref.own0), channel_id=1, source_target_pairs={{0,2},{2,4},{4,6},{6,0},{1,3},{3,5},{5,7},{7,1},{8,10},{10,12},{12... | collective-permute-start | bytes 1966088 | tf_op jit(solution)/shard_map/ppermute | solution.py:42
  56.4 17.9 %collective-permute-start.5 = (bf16[4,128,640]{2,1,0:T(8,128)(2,1)S(1)}, bf16[4,128,640]{2,1,0:T(8,128)(2,1)S(1)}, u32[]{:S(2)}, u32[]{:S(2)}) collective-permute-start(bf16[4,128,640]{2,1,0:T(8,128)(2,1)S(1)} %all-to-all-done.1.own_ref.own0), channel_id=1, source_target_pairs={{0,6},{2,0},{4,2},{6,4},{1,7},{3,1},{5,3},{7,5},{8,14},{10,8},{12,... | collective-permute-start | bytes 1966088 | tf_op jit(solution)/shard_map/ppermute | solution.py:42
  58.6 30.4 %collective-permute-start.4 = (bf16[4,128,640]{2,1,0:T(8,128)(2,1)S(1)}, bf16[4,128,640]{2,1,0:T(8,128)(2,1)S(1)}, u32[]{:S(2)}, u32[]{:S(2)}) collective-permute-start(bf16[4,128,640]{2,1,0:T(8,128)(2,1)S(1)} %all-to-all-done.1.own_ref.own0), channel_id=1, source_target_pairs={{0,4},{2,6},{4,0},{6,2},{1,5},{3,7},{5,1},{7,3},{8,12},{10,14},{12... | collective-permute-start | bytes 1966088 | tf_op jit(solution)/shard_map/ppermute | solution.py:42
  89.0 7.4 %collective-permute-start.8 = (bf16[4,128,640]{2,1,0:T(8,128)(2,1)S(1)}, bf16[4,128,640]{2,1,0:T(8,128)(2,1)S(1)}, u32[]{:S(2)}, u32[]{:S(2)}) collective-permute-start(bf16[4,128,640]{2,1,0:T(8,128)(2,1)S(1)} %collective-permute-done.4.own1), channel_id=1, source_target_pairs={{0,1},{1,0},{2,3},{3,2},{4,5},{5,4},{6,7},{7,6},{8,9},{9,8},{10,11... | collective-permute-start | bytes 1966088 | tf_op jit(solution)/shard_map/ppermute | solution.py:42
  92.0 4.4 %collective-permute-start.9 = (bf16[4,128,640]{2,1,0:T(8,128)(2,1)S(1)}, bf16[4,128,640]{2,1,0:T(8,128)(2,1)S(1)}, u32[]{:S(2)}, u32[]{:S(2)}) collective-permute-start(bf16[4,128,640]{2,1,0:T(8,128)(2,1)S(1)} %collective-permute-done.5.own2), channel_id=1, source_target_pairs={{0,1},{1,0},{2,3},{3,2},{4,5},{5,4},{6,7},{7,6},{8,9},{9,8},{10,11... | collective-permute-start | bytes 1966088 | tf_op jit(solution)/shard_map/ppermute | solution.py:42
  93.9 4.1 %collective-permute-start.10 = (bf16[4,128,640]{2,1,0:T(8,128)(2,1)S(1)}, bf16[4,128,640]{2,1,0:T(8,128)(2,1)S(1)}, u32[]{:S(2)}, u32[]{:S(2)}) collective-permute-start(bf16[4,128,640]{2,1,0:T(8,128)(2,1)S(1)} %collective-permute-done.6.own3), channel_id=1, source_target_pairs={{0,1},{1,0},{2,3},{3,2},{4,5},{5,4},{6,7},{7,6},{8,9},{9,8},{10,11... | collective-permute-start | bytes 1966088 | tf_op jit(solution)/shard_map/ppermute | solution.py:42

commit v5 on v4

--- a/solution.py
+++ b/solution.py
@@ -214,10 +214,10 @@
     return dots[0] + (dots[1] + dots[2])
 
 
-def product(patches, weight_ref, pair):
+def product(patches, weight_ref, pair, chunk=0):
     rhs = jnp.concatenate(
         [
-            weight_ref[y, q * 32 : (q + 1) * 32, :]
+            weight_ref[chunk * 4 + y, q * 32 : (q + 1) * 32, :]
             for q in (2 * pair, 2 * pair + 1)
             for y in range(4)
         ],
@@ -239,28 +239,56 @@
     return (keep * out_gate * jnp.tanh(cell)).astype(BF16), cell
 
 
-def partial_kernel(slot, more, ids_ref, patches_ref, own_ref, other_ref, *refs):
-    total = refs[-1]
-    patches = patches_ref[ids_ref[slot]]
+def partial_kernel(ids_ref, patches_ref, own_ref, other_ref, total):
+    patches = patches_ref[ids_ref[0]]
     for i, weight_ref in enumerate((own_ref, other_ref)):
         for pair in range(2):
-            value = product(patches, weight_ref, pair)
-            if more:
-                value = value + refs[0][i, pair]
-            total[i, pair] = value
-
-
-def partial(slot, ids, patches, own, other, *before):
+            total[i, pair] = product(patches, weight_ref, pair)
+
+
+def partial(ids, patches, own, other):
     count = patches.shape[1]
     return pl.pallas_call(
-        functools.partial(partial_kernel, slot, len(before) > 0),
+        partial_kernel,
         out_shape=jax.ShapeDtypeStruct((2, 2, count, HID), F32),
-        in_specs=[SMEM] + [VMEM] * (3 + len(before)),
+        in_specs=[SMEM] + [VMEM] * 3,
         out_specs=VMEM,
-        input_output_aliases={4: 0} if before else {},
         compiler_params=PARAMS,
         cost_estimate=pl.CostEstimate(flops=0, bytes_accessed=100_000, transcendentals=0),
-    )(ids, patches, own, other, *before)
+    )(ids, patches, own, other)
+
+
+def first_half(i, half, ids_ref, patches_ref, total_ref, rest_ref, bias_ref, cell_ref, keep_ref):
+    sums = []
+    for pair in range(2):
+        value = total_ref[i, pair]
+        for slot in (1, 2, 3):
+            value = value + product(patches_ref[ids_ref[slot]], rest_ref, pair, slot - 1)
+        sums.append(value)
+    cell = moved(cell_ref[...], chooser(half, (HID, 128), 0))
+    return updated(sums, bias_ref[i], cell, keep_ref[...])
+
+
+def own_kernel(ids_ref, half_ref, *refs):
+    *ins, hid_out, cell_out = refs
+    hid_out[...], cell_out[...] = first_half(0, half_ref[0], ids_ref, *ins)
+
+
+def own_half(ids, halves, patches, total, rest, bias, cell, keep):
+    count = patches.shape[1]
+    return pl.pallas_call(
+        own_kernel,
+        out_shape=(
+            jax.ShapeDtypeStruct((count, 128), BF16),
+            jax.ShapeDtypeStruct((count, 128), F32),
+        ),
+        in_specs=[SMEM] * 2 + [VMEM] * 6,
+        out_specs=(VMEM, VMEM),
+        compiler_params=PARAMS,
+        cost_estimate=pl.CostEstimate(
+            flops=2 * count * KPAD * 512, bytes_accessed=6_000_000, transcendentals=count * 640
+        ),
+    )(ids, halves, patches, total, rest, bias, cell, keep)
 
 
 def final_kernel(
@@ -269,16 +297,14 @@
     patches_ref,
     total_ref,
     own0,
-    own1,
-    own2,
-    own3,
+    own_rest,
     other0,
-    other1,
-    other2,
-    other3,
+    other_rest,
     bias_ref,
     cell_ref,
     keep_ref,
+    hid0_ref,
+    cell0_ref,
     frame_ref,
     keep2_ref,
     proj_ref,
@@ -288,21 +314,14 @@
     wide,
     patches,
 ):
-    weights = ((own0, own1, own2, own3), (other0, other1, other2, other3))
     choices = [chooser(half_ref[i], (128, HID), 1) for i in range(2)]
-    natural, cells = None, []
-    for i in range(2):
-        sums = []
-        for pair in range(2):
-            value = total_ref[i, pair]
-            for slot in (1, 2, 3):
-                value = value + product(patches_ref[ids_ref[slot]], weights[i][slot], pair)
-            sums.append(value)
-        cell = moved(cell_ref[...], chooser(half_ref[i], (HID, 128), 0))
-        hid, cell = updated(sums, bias_ref[i], cell, keep_ref[...])
-        cells.append(cell[32:544])
-        one = lax.dot_general(hid, choices[i], NN, preferred_element_type=F32)
-        natural = one if natural is None else natural + one
+    hid, cell = first_half(
+        1, half_ref[1], ids_ref, patches_ref, total_ref, other_rest, bias_ref, cell_ref, keep_ref
+    )
+    cells = (cell0_ref[32:544, :], cell[32:544])
+    natural = lax.dot_general(
+        hid0_ref[...], choices[0], NN, preferred_element_type=F32
+    ) + lax.dot_general(hid, choices[1], NN, preferred_element_type=F32)
 
     wide[:, 8:40, :] = natural[:576].reshape(18, 32, HID)
     for row in range(18):
@@ -315,13 +334,12 @@
     put(patches, slice(0, 512), 9 * HID, frame_ref[...])
 
     hid, cell = None, None
-    for i in range(2):
+    for i, (first_ref, rest_ref) in enumerate(((own0, own_rest), (other0, other_rest))):
         sums = []
         for pair in range(2):
-            value = None
-            for slot in range(4):
-                part = product(patches[ids_ref[slot]], weights[i][slot], pair)
-                value = part if value is None else value + part
+            value = product(patches[ids_ref[0]], first_ref, pair)
+            for slot in (1, 2, 3):
+                value = value + product(patches[ids_ref[slot]], rest_ref, pair, slot - 1)
             sums.append(value)
         new_hid, new_cell = updated(sums, bias_ref[i], cells[i], keep_ref[32:544, :])
         one = lax.dot_general(new_hid, choices[i], NN, preferred_element_type=F32)
@@ -336,7 +354,7 @@
         flux_out[row : row + 1, :] = flux[0:1, row * 32 : (row + 1) * 32] * keep2_ref[row : row + 1, :]
 
 
-def finished(ids, halves, patches, total, own, other, bias, cell, keep, frame, keep2, proj):
+def finished(ids, halves, *arrays):
     return pl.pallas_call(
         final_kernel,
         out_shape=(
@@ -344,27 +362,28 @@
             jax.ShapeDtypeStruct((512, HID), F32),
             jax.ShapeDtypeStruct((16, 32), F32),
         ),
-        in_specs=[SMEM] * 2 + [VMEM] * 16,
+        in_specs=[SMEM] * 2 + [VMEM] * len(arrays),
         out_specs=(VMEM, VMEM, VMEM),
         scratch_shapes=[pltpu.VMEM((18, 48, HID), F32), pltpu.VMEM((4, 512, CHUNK), BF16)],
         compiler_params=PARAMS,
         cost_estimate=pl.CostEstimate(
             flops=2 * 824 * KPAD * 1024, bytes_accessed=14_000_000, transcendentals=1136 * 1280
         ),
-    )(ids, halves, patches, total, *own, *other, bias, cell, keep, frame, keep2, proj)
-
-
-def compute(ids, halves, own, swapped, prep, land_mask, bias2, proj):
+    )(ids, halves, *arrays)
+
+
+def compute(ids, halves, own0, pieces, swapped, prep, land_mask, bias2, proj):
     rows, cols = land_mask.shape
     patches1, frame2, cell1, keep1 = prep
-    other = [swapped(0, own[0])]
-    total = partial(0, ids, patches1, own[0], other[0])
-    later, total = lax.optimization_barrier((own[1:], total))
-    own = own[:1] + later
-    other += [swapped(slot, own[slot]) for slot in (1, 2, 3)]
+    other0 = swapped(0, own0)
+    total = partial(ids, patches1, own0, other0)
+    pieces, total = lax.optimization_barrier((pieces, total))
+    own_rest = jnp.concatenate(pieces, axis=0)
+    other_rest = swapped(1, own_rest)
+    hid0, cell0 = own_half(ids, halves, patches1, total, own_rest, bias2, cell1, keep1)
     hidden, cell, flux = finished(
-        ids, halves, patches1, total, own, other, bias2, cell1, keep1, frame2,
-        land_mask.astype(F32), proj,
+        ids, halves, patches1, total, own0, own_rest, other0, other_rest, bias2, cell1, keep1,
+        hid0, cell0, frame2, land_mask.astype(F32), proj,
     )
     return hidden.reshape(rows, cols, HID), cell.reshape(rows, cols, HID), flux
 
@@ -404,12 +423,18 @@
     last, first = sides_of(*state, low, high)
     left = shifted(last, ("z", "y"), 1)
     right = shifted(first, ("z", "y"), -1)
-    by_y, left, right = lax.optimization_barrier((by_y, left, right))
-
-    own = [by_y] + [turned(by_y, "x", step) for step in (2, -1, 1)]
+
+    low_half, high_half = by_y[:2], by_y[2:]
+    up_low = turned(low_half, "x", 1)
+    down_high = turned(high_half, "x", -1)
+    up_high = turned(high_half, "x", 1)
+    down_low = turned(low_half, "x", -1)
+    far_low = turned(up_low, "x", 1)
+    far_high = turned(down_high, "x", -1)
+    pieces = [far_low, far_high, down_low, down_high, up_low, up_high]
     prep = prepared(cx, *state, low, high, left, right)
     swapped = lambda slot, piece: turned(piece, "c", 1)
-    return compute(ids, halves, own, swapped, prep, land_mask, bias2, proj)
+    return compute(ids, halves, by_y, pieces, swapped, prep, land_mask, bias2, proj)
 
 
 def solution(mesh):

time: 109 us -> 102 us (0.936)
  the two profiles are of different devices: /device:TPU:27 before, /device:TPU:31 now
where the time goes in v5:
time: 102 us; the launch traced here: 101 us
  starting transfers between devices  55.7 us (55%)
  Pallas kernels  14.8 us (15%)
  waiting for transfers between devices  14.4 us (14%)
  blocking collectives  9.77 us (10%)
  local copies, waits for them, and re-layouts  4.49 us (4%)
  other arithmetic  1.09 us (1%)
  between operations  1.05 us (1%)
    ppermute x8, starting transfers between devices, turned(): lax.ppermute(block, axis, [(i, (i + step) % count) for i in range(count)])  29.3 us
    all_to_all x1, starting transfers between devices, spread(): return lax.all_to_all(copies, axes, 0, 0)  14.9 us
    ppermute x4, starting transfers between devices, shifted(): return lax.ppermute(block, axes, pairs)  11.5 us
    all_to_all x1, blocking collectives, spread(): return lax.all_to_all(copies, axes, 0, 0)  9.77 us
    pallas_call x1, Pallas kernels, finished(): pl.pallas_call(final_kernel, out_shape=(jax.ShapeDtypeStruct((512, HID),...  8.78 us
    ppermute x8, waiting for transfers between devices, turned(): lax.ppermute(block, axis, [(i, (i + step) % count) for i in range(count)])  6.45 us
    all_to_all x1, waiting for transfers between devices, spread(): return lax.all_to_all(copies, axes, 0, 0)  4.38 us
    ppermute x4, waiting for transfers between devices, shifted(): return lax.ppermute(block, axes, pairs)  3.6 us
  transfers between devices with their start and end apart: 13, of which 5 were waited for; matrix products, arithmetic and copies ran while one was open for 3% of the time, Pallas kernels for 6%

profile of v5, /device:TPU:31, one launch (start us, length us, event | category | flops | bytes accessed | tf_op | source)
XLA Modules:
  0.0 101.4 jit_solution(11594802020541605277)
XLA Ops:
  0.7 0.8 slice.17
  1.5 1.0 slice_bitcast_fusion
  2.5 0.1 copy.12
  2.6 0.1 copy.13
  2.7 0.7 broadcast_in_dim.8
  3.4 14.9 %all-to-all-start = ((bf16[16,8,640]{2,1,0:T(8,128)(2,1)}), bf16[16,8,640]{2,1,0:T(8,128)(2,1)S(1)}, u32[]{:S(2)}, u32[]{:S(2)}) async-start(bf16[16,8,640]{2,1,0:T(8,128)(2,1)} %broadcast_in_dim.8), calls=%async_computation | async-start | bytes 327680 | tf_op jit(solution)/shard_map/all_to_all | solution.py:37
  18.3 0.8 fusion.7
  19.1 0.9 copy.20
  20.0 0.1 copy.15
  20.1 0.2 copy.16
  20.3 0.1 fusion.2.aux_ref
  20.5 1.3 %collective-permute-start = (bf16[64,640]{1,0:T(8,128)(2,1)S(1)}, bf16[64,640]{1,0:T(8,128)(2,1)S(1)}, u32[]{:S(2)}, u32[]{:S(2)}) collective-permute-start(bf16[64,640]{1,0:T(8,128)(2,1)S(1)} %get-tuple-element.30), channel_id=1, source_target_pairs={{0,1},{1,2},{2,3},{3,4},{4,5},{5,6},{6,7},{8,9},{9,10},{10,11},{11... | collective-permute-start | bytes 245768 | tf_op jit(solution)/shard_map/ppermute | solution.py:48
  21.8 3.5 %collective-permute-start.1 = (bf16[64,640]{1,0:T(8,128)(2,1)S(1)}, bf16[64,640]{1,0:T(8,128)(2,1)S(1)}, u32[]{:S(2)}, u32[]{:S(2)}) collective-permute-start(bf16[64,640]{1,0:T(8,128)(2,1)S(1)} %get-tuple-element.31), channel_id=1, source_target_pairs={{1,0},{2,1},{3,2},{4,3},{5,4},{6,5},{7,6},{9,8},{10,9},{11,10},{12... | collective-permute-start | bytes 245768 | tf_op jit(solution)/shard_map/ppermute | solution.py:48
  25.3 0.1 reshape.37
  25.5 0.1 reshape.38
  25.6 0.1 pad_add_fusion.half_ref
  25.7 0.1 pad_add_fusion.1.ids_ref
  25.8 0.0 collective-permute-done.low_ref
  25.8 0.4 collective-permute-done.1.high_ref
  26.2 4.4 %all-to-all-done = bf16[16,8,640]{2,1,0:T(8,128)(2,1)S(1)} async-done(((bf16[16,8,640]{2,1,0:T(8,128)(2,1)}), bf16[16,8,640]{2,1,0:T(8,128)(2,1)S(1)}, u32[]{:S(2)}, u32[]{:S(2)}) %all-to-all-start) | async-done | bytes 163872 | tf_op jit(solution)/shard_map/all_to_all | solution.py:37
  30.6 0.1 broadcast_in_dim.11
  30.6 9.8 %all_to_all.10.own_ref.own0 = bf16[4,128,640]{2,1,0:T(8,128)(2,1)S(1)} all-to-all(bf16[4,128,640]{2,1,0:T(8,128)(2,1)S(1)} %broadcast_in_dim.11), channel_id=1, replica_groups=mesh['z'=16,'y'=4,'x'=4,'c'=2] {'y'}, dimensions={0} | all-to-all | bytes 1310720 | tf_op jit(solution)/shard_map/all_to_all | solution.py:37
  40.4 7.7 %collective-permute-start.10 = (bf16[4,128,640]{2,1,0:T(8,128)(2,1)S(1)}, bf16[4,128,640]{2,1,0:T(8,128)(2,1)S(1)}, u32[]{:S(2)}, u32[]{:S(2)}) collective-permute-start(bf16[4,128,640]{2,1,0:T(8,128)(2,1)S(1)} %all_to_all.10.own_ref.own0), channel_id=1, source_target_pairs={{0,1},{1,0},{2,3},{3,2},{4,5},{5,4},{6,7},{7,6},{8,9},{9,8},{10,11... | collective-permute-start | bytes 1966088 | tf_op jit(solution)/shard_map/ppermute | solution.py:42
  48.1 0.1 fusion.6
  48.2 2.5 %collective-permute-start.6 = (bf16[2,128,640]{2,1,0:T(8,128)(2,1)S(1)}, bf16[2,128,640]{2,1,0:T(8,128)(2,1)S(1)}, u32[]{:S(2)}, u32[]{:S(2)}) collective-permute-start(bf16[2,128,640]{2,1,0:T(8,128)(2,1)S(1)} %get-tuple-element.57), channel_id=1, source_target_pairs={{0,6},{2,0},{4,2},{6,4},{1,7},{3,1},{5,3},{7,5},{8,14},{10,8},{12,... | collective-permute-start | bytes 983048 | tf_op jit(solution)/shard_map/ppermute | solution.py:42
  50.6 4.0 %collective-permute-start.4 = (bf16[2,128,640]{2,1,0:T(8,128)(2,1)S(1)}, bf16[2,128,640]{2,1,0:T(8,128)(2,1)S(1)}, u32[]{:S(2)}, u32[]{:S(2)}) collective-permute-start(bf16[2,128,640]{2,1,0:T(8,128)(2,1)S(1)} %get-tuple-element.58), channel_id=1, source_target_pairs={{0,2},{2,4},{4,6},{6,0},{1,3},{3,5},{5,7},{7,1},{8,10},{10,12},{12... | collective-permute-start | bytes 983048 | tf_op jit(solution)/shard_map/ppermute | solution.py:42
  54.7 0.1 shard_map.95
  54.8 4.8 %collective-permute-start.2 = (bf16[48,640]{1,0:T(8,128)(2,1)S(1)}, bf16[48,640]{1,0:T(8,128)(2,1)S(1)}, u32[]{:S(2)}, u32[]{:S(2)}) collective-permute-start(bf16[48,640]{1,0:T(8,128)(2,1)S(1)} %get-tuple-element.36), channel_id=1, source_target_pairs={{0,8},{8,16},{16,24},{24,32},{32,40},{40,48},{48,56},{56,64},{64,7... | collective-permute-start | bytes 184328 | tf_op jit(solution)/shard_map/ppermute | solution.py:48
  59.5 1.9 %collective-permute-start.3 = (bf16[48,640]{1,0:T(8,128)(2,1)S(1)}, bf16[48,640]{1,0:T(8,128)(2,1)S(1)}, u32[]{:S(2)}, u32[]{:S(2)}) collective-permute-start(bf16[48,640]{1,0:T(8,128)(2,1)S(1)} %get-tuple-element.37), channel_id=1, source_target_pairs={{8,0},{16,8},{24,16},{32,24},{40,32},{48,40},{56,48},{64,56},{72,6... | collective-permute-start | bytes 184328 | tf_op jit(solution)/shard_map/ppermute | solution.py:48
  61.5 0.0 collective-permute-done.2.left_ref
  61.5 1.9 %collective-permute-start.9 = (bf16[2,128,640]{2,1,0:T(8,128)(2,1)S(1)}, bf16[2,128,640]{2,1,0:T(8,128)(2,1)S(1)}, u32[]{:S(2)}, u32[]{:S(2)}) collective-permute-start(bf16[2,128,640]{2,1,0:T(8,128)(2,1)S(1)} %get-tuple-element.57), channel_id=1, source_target_pairs={{0,2},{2,4},{4,6},{6,0},{1,3},{3,5},{5,7},{7,1},{8,10},{10,12},{12... | collective-permute-start | bytes 983048 | tf_op jit(solution)/shard_map/ppermute | solution.py:42
  63.4 3.2 %collective-permute-done.3.right_ref = bf16[48,640]{1,0:T(8,128)(2,1)S(1)} collective-permute-done((bf16[48,640]{1,0:T(8,128)(2,1)S(1)}, bf16[48,640]{1,0:T(8,128)(2,1)S(1)}, u32[]{:S(2)}, u32[]{:S(2)}) %collective-permute-start.3) | collective-permute-done | bytes 61472 | tf_op jit(solution)/shard_map/ppermute | solution.py:48
  66.6 1.9 %collective-permute-start.8 = (bf16[2,128,640]{2,1,0:T(8,128)(2,1)S(1)}, bf16[2,128,640]{2,1,0:T(8,128)(2,1)S(1)}, u32[]{:S(2)}, u32[]{:S(2)}) collective-permute-start(bf16[2,128,640]{2,1,0:T(8,128)(2,1)S(1)} %get-tuple-element.58), channel_id=1, source_target_pairs={{0,6},{2,0},{4,2},{6,4},{1,7},{3,1},{5,3},{7,5},{8,14},{10,8},{12,... | collective-permute-start | bytes 983048 | tf_op jit(solution)/shard_map/ppermute | solution.py:42
  68.5 0.0 collective-permute-done.6
  68.5 1.9 %collective-permute-start.7 = (bf16[2,128,640]{2,1,0:T(8,128)(2,1)S(1)}, bf16[2,128,640]{2,1,0:T(8,128)(2,1)S(1)}, u32[]{:S(2)}, u32[]{:S(2)}) collective-permute-start(bf16[2,128,640]{2,1,0:T(8,128)(2,1)S(1)} %collective-permute-done.6), channel_id=1, source_target_pairs={{0,6},{2,0},{4,2},{6,4},{1,7},{3,1},{5,3},{7,5},{8,14},{10,8},{12,... | collective-permute-start | bytes 983048 | tf_op jit(solution)/shard_map/ppermute | solution.py:42
  70.5 0.0 collective-permute-done.4
  70.5 4.6 %collective-permute-start.5 = (bf16[2,128,640]{2,1,0:T(8,128)(2,1)S(1)}, bf16[2,128,640]{2,1,0:T(8,128)(2,1)S(1)}, u32[]{:S(2)}, u32[]{:S(2)}) collective-permute-start(bf16[2,128,640]{2,1,0:T(8,128)(2,1)S(1)} %collective-permute-done.4), channel_id=1, source_target_pairs={{0,2},{2,4},{4,6},{6,0},{1,3},{3,5},{5,7},{7,1},{8,10},{10,12},{12... | collective-permute-start | bytes 983048 | tf_op jit(solution)/shard_map/ppermute | solution.py:42
  75.0 1.7 %shard_map.96 = (bf16[4,624,640]{2,1,0:T(8,128)(2,1)S(1)}, bf16[512,256]{1,0:T(8,128)(2,1)S(1)}, f32[624,256]{1,0:T(8,128)S(1)}, f32[624,128]{1,0:T(8,128)S(1)}) custom-call(bf16[16,32,256]{2,1,0:T(8,128)(2,1)S(1)} %copy-done.1, f32[16,32,256]{2,1,0:T(8,128)S(1)} %copy-done, bf16[16,32,128]{2,1,0:T(8,128)(2,1)S(1)} %fusion.2.aux_ref, ...), custom_call_target="tpu_custom_call" | custom-call | bytes 100000 | tf_op jit(solution)/shard_map/pallas_call | solution.py:180
  76.8 0.0 collective-permute-done.10.other_ref.other0
  76.8 1.7 %shard_map.97.refs_1_.total_ref = f32[2,2,624,256]{3,2,1,0:T(8,128)S(1)} custom-call(s32[4]{0:T(128)S(1)} %pad_add_fusion.1.ids_ref, bf16[4,624,640]{2,1,0:T(8,128)(2,1)S(1)} %get-tuple-element.38.patches_ref.refs_0_, bf16[4,128,640]{2,1,0:T(8,128)(2,1)S(1)} %all_to_all.10.own_ref.own0, bf16[4,128,640]{2,1,0:T(8,128)(2,1)S(1)} %collective-permute-done.10.other_ref.other0), custom_call_target="tpu_custom_call" | custom-call | bytes 100000 | tf_op jit(solution)/shard_map/pallas_call | solution.py:251
  78.5 0.0 collective-permute-done.9
  78.5 0.0 collective-permute-done.8
  78.5 5.4 %collective-permute-done.7 = bf16[2,128,640]{2,1,0:T(8,128)(2,1)S(1)} collective-permute-done((bf16[2,128,640]{2,1,0:T(8,128)(2,1)S(1)}, bf16[2,128,640]{2,1,0:T(8,128)(2,1)S(1)}, u32[]{:S(2)}, u32[]{:S(2)}) %collective-permute-start.7) | collective-permute-done | bytes 327712 | tf_op jit(solution)/shard_map/ppermute | solution.py:42
  83.9 0.0 collective-permute-done.5
  84.2 4.8 %collective-permute-start.11 = (bf16[12,128,640]{2,1,0:T(8,128)(2,1)S(1)}, bf16[12,128,640]{2,1,0:T(8,128)(2,1)S(1)}, u32[]{:S(2)}, u32[]{:S(2)}) collective-permute-start(bf16[12,128,640]{2,1,0:T(8,128)(2,1)S(1)} %constant_dynamic-update-slice_fusion.refs_2_.own_rest), channel_id=1, source_target_pairs={{0,1},{1,0},{2,3},{3,2},{4,5},{5,4},{6,7},{7,6},{8,9},{9,8},{10,11... | collective-permute-start | bytes 5898248 | tf_op jit(solution)/shard_map/ppermute | solution.py:42
  89.0 2.5 %shard_map.98 = (bf16[624,128]{1,0:T(8,128)(2,1)S(1)}, f32[624,128]{1,0:T(8,128)S(1)}) custom-call(s32[4]{0:T(128)S(1)} %pad_add_fusion.1.ids_ref, s32[2]{0:T(128)S(1)} %pad_add_fusion.half_ref, bf16[4,624,640]{2,1,0:T(8,128)(2,1)S(1)} %get-tuple-element.38.patches_ref.refs_0_, f32[2,2,624,256]{3,2,1,0:T(8,128)S(1)} %shard_map.97.refs_1_.total_ref, ...), custom_call_target="tpu_custom_call" | custom-call | flops 1635778560 | bytes 6000000 | tf_op jit(solution)/shard_map/pallas_call | solution.py:279
  91.6 1.1 %collective-permute-done.11.other_rest = bf16[12,128,640]{2,1,0:T(8,128)(2,1)S(1)} collective-permute-done((bf16[12,128,640]{2,1,0:T(8,128)(2,1)S(1)}, bf16[12,128,640]{2,1,0:T(8,128)(2,1)S(1)}, u32[]{:S(2)}, u32[]{:S(2)}) %collective-permute-start.11) | collective-permute-done | bytes 1966112 | tf_op jit(solution)/shard_map/ppermute | solution.py:42
  92.6 8.8 %shard_map.99 = (bf16[512,256]{1,0:T(8,128)(2,1)}, f32[512,256]{1,0:T(8,128)}, f32[16,32]{1,0:T(8,128)}) custom-call(s32[4]{0:T(128)S(1)} %pad_add_fusion.1.ids_ref, s32[2]{0:T(128)S(1)} %pad_add_fusion.half_ref, bf16[4,624,640]{2,1,0:T(8,128)(2,1)S(1)} %get-tuple-element.38.patches_ref.refs_0_, f32[2,2,624,256]{3,2,1,0:T(8,128)S(1)} %shard_map.97.refs_1_.total_ref, ...), custom_call_target="tpu_custom_call" | custom-call | flops 4320133120 | bytes 14000000 | tf_op jit(solution)/shard_map/pallas_call | solution.py:358
  (20 shorter events, 0.3 us)
Async XLA Ops:
  0.6 19.8 %copy-start = (f32[16,32,256]{2,1,0:T(8,128)S(1)}, f32[16,32,256]{2,1,0:T(8,128)}, u32[]{:S(2)}) copy-start(f32[16,32,256]{2,1,0:T(8,128)} %cell_ref.5) | copy-start | bytes 1572868
  0.6 19.8 %copy-start.1 = (bf16[16,32,256]{2,1,0:T(8,128)(2,1)S(1)}, bf16[16,32,256]{2,1,0:T(8,128)(2,1)}, u32[]{:S(2)}) copy-start(bf16[16,32,256]{2,1,0:T(8,128)(2,1)} %hidden_ref.5) | copy-start | bytes 786436
  0.7 24.7 %copy-start.2 = (f32[1024]{0:T(1024)S(1)}, f32[1024]{0:T(1024)}, u32[]{:S(2)}) copy-start(f32[1024]{0:T(1024)} %param.11) | copy-start | bytes 12292
  0.7 29.9 %copy-start.3 = (bf16[256]{0:T(256)(128)(2,1)S(1)}, bf16[256]{0:T(256)(128)(2,1)}, u32[]{:S(2)}) copy-start(bf16[256]{0:T(256)(128)(2,1)} %param.13) | copy-start | bytes 1540
  3.4 27.1 %all-to-all-start = ((bf16[16,8,640]{2,1,0:T(8,128)(2,1)}), bf16[16,8,640]{2,1,0:T(8,128)(2,1)S(1)}, u32[]{:S(2)}, u32[]{:S(2)}) async-start(bf16[16,8,640]{2,1,0:T(8,128)(2,1)} %broadcast_in_dim.8), calls=%async_computation | async-start | bytes 327680 | tf_op jit(solution)/shard_map/all_to_all | solution.py:37
  20.5 5.3 %collective-permute-start = (bf16[64,640]{1,0:T(8,128)(2,1)S(1)}, bf16[64,640]{1,0:T(8,128)(2,1)S(1)}, u32[]{:S(2)}, u32[]{:S(2)}) collective-permute-start(bf16[64,640]{1,0:T(8,128)(2,1)S(1)} %get-tuple-element.30), channel_id=1, source_target_pairs={{0,1},{1,2},{2,3},{3,4},{4,5},{5,6},{6,7},{8,9},{9,10},{10,11},{11... | collective-permute-start | bytes 245768 | tf_op jit(solution)/shard_map/ppermute | solution.py:48
  21.8 4.4 %collective-permute-start.1 = (bf16[64,640]{1,0:T(8,128)(2,1)S(1)}, bf16[64,640]{1,0:T(8,128)(2,1)S(1)}, u32[]{:S(2)}, u32[]{:S(2)}) collective-permute-start(bf16[64,640]{1,0:T(8,128)(2,1)S(1)} %get-tuple-element.31), channel_id=1, source_target_pairs={{1,0},{2,1},{3,2},{4,3},{5,4},{6,5},{7,6},{9,8},{10,9},{11,10},{12... | collective-permute-start | bytes 245768 | tf_op jit(solution)/shard_map/ppermute | solution.py:48
  40.4 36.4 %collective-permute-start.10 = (bf16[4,128,640]{2,1,0:T(8,128)(2,1)S(1)}, bf16[4,128,640]{2,1,0:T(8,128)(2,1)S(1)}, u32[]{:S(2)}, u32[]{:S(2)}) collective-permute-start(bf16[4,128,640]{2,1,0:T(8,128)(2,1)S(1)} %all_to_all.10.own_ref.own0), channel_id=1, source_target_pairs={{0,1},{1,0},{2,3},{3,2},{4,5},{5,4},{6,7},{7,6},{8,9},{9,8},{10,11... | collective-permute-start | bytes 1966088 | tf_op jit(solution)/shard_map/ppermute | solution.py:42
  48.2 20.4 %collective-permute-start.6 = (bf16[2,128,640]{2,1,0:T(8,128)(2,1)S(1)}, bf16[2,128,640]{2,1,0:T(8,128)(2,1)S(1)}, u32[]{:S(2)}, u32[]{:S(2)}) collective-permute-start(bf16[2,128,640]{2,1,0:T(8,128)(2,1)S(1)} %get-tuple-element.57), channel_id=1, source_target_pairs={{0,6},{2,0},{4,2},{6,4},{1,7},{3,1},{5,3},{7,5},{8,14},{10,8},{12,... | collective-permute-start | bytes 983048 | tf_op jit(solution)/shard_map/ppermute | solution.py:42
  50.6 19.8 %collective-permute-start.4 = (bf16[2,128,640]{2,1,0:T(8,128)(2,1)S(1)}, bf16[2,128,640]{2,1,0:T(8,128)(2,1)S(1)}, u32[]{:S(2)}, u32[]{:S(2)}) collective-permute-start(bf16[2,128,640]{2,1,0:T(8,128)(2,1)S(1)} %get-tuple-element.58), channel_id=1, source_target_pairs={{0,2},{2,4},{4,6},{6,0},{1,3},{3,5},{5,7},{7,1},{8,10},{10,12},{12... | collective-permute-start | bytes 983048 | tf_op jit(solution)/shard_map/ppermute | solution.py:42
  54.8 6.7 %collective-permute-start.2 = (bf16[48,640]{1,0:T(8,128)(2,1)S(1)}, bf16[48,640]{1,0:T(8,128)(2,1)S(1)}, u32[]{:S(2)}, u32[]{:S(2)}) collective-permute-start(bf16[48,640]{1,0:T(8,128)(2,1)S(1)} %get-tuple-element.36), channel_id=1, source_target_pairs={{0,8},{8,16},{16,24},{24,32},{32,40},{40,48},{48,56},{56,64},{64,7... | collective-permute-start | bytes 184328 | tf_op jit(solution)/shard_map/ppermute | solution.py:48
  59.5 7.1 %collective-permute-start.3 = (bf16[48,640]{1,0:T(8,128)(2,1)S(1)}, bf16[48,640]{1,0:T(8,128)(2,1)S(1)}, u32[]{:S(2)}, u32[]{:S(2)}) collective-permute-start(bf16[48,640]{1,0:T(8,128)(2,1)S(1)} %get-tuple-element.37), channel_id=1, source_target_pairs={{8,0},{16,8},{24,16},{32,24},{40,32},{48,40},{56,48},{64,56},{72,6... | collective-permute-start | bytes 184328 | tf_op jit(solution)/shard_map/ppermute | solution.py:48
  61.5 17.1 %collective-permute-start.9 = (bf16[2,128,640]{2,1,0:T(8,128)(2,1)S(1)}, bf16[2,128,640]{2,1,0:T(8,128)(2,1)S(1)}, u32[]{:S(2)}, u32[]{:S(2)}) collective-permute-start(bf16[2,128,640]{2,1,0:T(8,128)(2,1)S(1)} %get-tuple-element.57), channel_id=1, source_target_pairs={{0,2},{2,4},{4,6},{6,0},{1,3},{3,5},{5,7},{7,1},{8,10},{10,12},{12... | collective-permute-start | bytes 983048 | tf_op jit(solution)/shard_map/ppermute | solution.py:42
  66.6 11.9 %collective-permute-start.8 = (bf16[2,128,640]{2,1,0:T(8,128)(2,1)S(1)}, bf16[2,128,640]{2,1,0:T(8,128)(2,1)S(1)}, u32[]{:S(2)}, u32[]{:S(2)}) collective-permute-start(bf16[2,128,640]{2,1,0:T(8,128)(2,1)S(1)} %get-tuple-element.58), channel_id=1, source_target_pairs={{0,6},{2,0},{4,2},{6,4},{1,7},{3,1},{5,3},{7,5},{8,14},{10,8},{12,... | collective-permute-start | bytes 983048 | tf_op jit(solution)/shard_map/ppermute | solution.py:42
  68.5 15.4 %collective-permute-start.7 = (bf16[2,128,640]{2,1,0:T(8,128)(2,1)S(1)}, bf16[2,128,640]{2,1,0:T(8,128)(2,1)S(1)}, u32[]{:S(2)}, u32[]{:S(2)}) collective-permute-start(bf16[2,128,640]{2,1,0:T(8,128)(2,1)S(1)} %collective-permute-done.6), channel_id=1, source_target_pairs={{0,6},{2,0},{4,2},{6,4},{1,7},{3,1},{5,3},{7,5},{8,14},{10,8},{12,... | collective-permute-start | bytes 983048 | tf_op jit(solution)/shard_map/ppermute | solution.py:42
  70.5 13.5 %collective-permute-start.5 = (bf16[2,128,640]{2,1,0:T(8,128)(2,1)S(1)}, bf16[2,128,640]{2,1,0:T(8,128)(2,1)S(1)}, u32[]{:S(2)}, u32[]{:S(2)}) collective-permute-start(bf16[2,128,640]{2,1,0:T(8,128)(2,1)S(1)} %collective-permute-done.4), channel_id=1, source_target_pairs={{0,2},{2,4},{4,6},{6,0},{1,3},{3,5},{5,7},{7,1},{8,10},{10,12},{12... | collective-permute-start | bytes 983048 | tf_op jit(solution)/shard_map/ppermute | solution.py:42
  84.2 8.4 %collective-permute-start.11 = (bf16[12,128,640]{2,1,0:T(8,128)(2,1)S(1)}, bf16[12,128,640]{2,1,0:T(8,128)(2,1)S(1)}, u32[]{:S(2)}, u32[]{:S(2)}) collective-permute-start(bf16[12,128,640]{2,1,0:T(8,128)(2,1)S(1)} %constant_dynamic-update-slice_fusion.refs_2_.own_rest), channel_id=1, source_target_pairs={{0,1},{1,0},{2,3},{3,2},{4,5},{5,4},{6,7},{7,6},{8,9},{9,8},{10,11... | collective-permute-start | bytes 5898248 | tf_op jit(solution)/shard_map/ppermute | solution.py:42

commit v6 on v5

--- a/solution.py
+++ b/solution.py
@@ -239,32 +239,19 @@
     return (keep * out_gate * jnp.tanh(cell)).astype(BF16), cell
 
 
-def partial_kernel(ids_ref, patches_ref, own_ref, other_ref, total):
-    patches = patches_ref[ids_ref[0]]
-    for i, weight_ref in enumerate((own_ref, other_ref)):
-        for pair in range(2):
-            total[i, pair] = product(patches, weight_ref, pair)
-
-
-def partial(ids, patches, own, other):
-    count = patches.shape[1]
-    return pl.pallas_call(
-        partial_kernel,
-        out_shape=jax.ShapeDtypeStruct((2, 2, count, HID), F32),
-        in_specs=[SMEM] + [VMEM] * 3,
-        out_specs=VMEM,
-        compiler_params=PARAMS,
-        cost_estimate=pl.CostEstimate(flops=0, bytes_accessed=100_000, transcendentals=0),
-    )(ids, patches, own, other)
-
-
-def first_half(i, half, ids_ref, patches_ref, total_ref, rest_ref, bias_ref, cell_ref, keep_ref):
+def gate_sums(patches_ref, ids_ref, weight_ref):
     sums = []
     for pair in range(2):
-        value = total_ref[i, pair]
-        for slot in (1, 2, 3):
-            value = value + product(patches_ref[ids_ref[slot]], rest_ref, pair, slot - 1)
+        value = None
+        for slot in range(4):
+            part = product(patches_ref[ids_ref[slot]], weight_ref, pair, slot)
+            value = part if value is None else value + part
         sums.append(value)
+    return sums
+
+
+def first_half(i, half, ids_ref, patches_ref, weight_ref, bias_ref, cell_ref, keep_ref):
+    sums = gate_sums(patches_ref, ids_ref, weight_ref)
     cell = moved(cell_ref[...], chooser(half, (HID, 128), 0))
     return updated(sums, bias_ref[i], cell, keep_ref[...])
 
@@ -274,7 +261,7 @@
     hid_out[...], cell_out[...] = first_half(0, half_ref[0], ids_ref, *ins)
 
 
-def own_half(ids, halves, patches, total, rest, bias, cell, keep):
+def own_half(ids, halves, patches, weight, bias, cell, keep):
     count = patches.shape[1]
     return pl.pallas_call(
         own_kernel,
@@ -282,24 +269,21 @@
             jax.ShapeDtypeStruct((count, 128), BF16),
             jax.ShapeDtypeStruct((count, 128), F32),
         ),
-        in_specs=[SMEM] * 2 + [VMEM] * 6,
+        in_specs=[SMEM] * 2 + [VMEM] * 5,
         out_specs=(VMEM, VMEM),
         compiler_params=PARAMS,
         cost_estimate=pl.CostEstimate(
             flops=2 * count * KPAD * 512, bytes_accessed=6_000_000, transcendentals=count * 640
         ),
-    )(ids, halves, patches, total, rest, bias, cell, keep)
+    )(ids, halves, patches, weight, bias, cell, keep)
 
 
 def final_kernel(
     ids_ref,
     half_ref,
     patches_ref,
-    total_ref,
-    own0,
-    own_rest,
-    other0,
-    other_rest,
+    own_ref,
+    other_ref,
     bias_ref,
     cell_ref,
     keep_ref,
@@ -316,7 +300,7 @@
 ):
     choices = [chooser(half_ref[i], (128, HID), 1) for i in range(2)]
     hid, cell = first_half(
-        1, half_ref[1], ids_ref, patches_ref, total_ref, other_rest, bias_ref, cell_ref, keep_ref
+        1, half_ref[1], ids_ref, patches_ref, other_ref, bias_ref, cell_ref, keep_ref
     )
     cells = (cell0_ref[32:544, :], cell[32:544])
     natural = lax.dot_general(
@@ -334,13 +318,8 @@
     put(patches, slice(0, 512), 9 * HID, frame_ref[...])
 
     hid, cell = None, None
-    for i, (first_ref, rest_ref) in enumerate(((own0, own_rest), (other0, other_rest))):
-        sums = []
-        for pair in range(2):
-            value = product(patches[ids_ref[0]], first_ref, pair)
-            for slot in (1, 2, 3):
-                value = value + product(patches[ids_ref[slot]], rest_ref, pair, slot - 1)
-            sums.append(value)
+    for i, weight_ref in enumerate((own_ref, other_ref)):
+        sums = gate_sums(patches, ids_ref, weight_ref)
         new_hid, new_cell = updated(sums, bias_ref[i], cells[i], keep_ref[32:544, :])
         one = lax.dot_general(new_hid, choices[i], NN, preferred_element_type=F32)
         two = moved(new_cell, choices[i])
@@ -372,17 +351,13 @@
     )(ids, halves, *arrays)
 
 
-def compute(ids, halves, own0, pieces, swapped, prep, land_mask, bias2, proj):
+def compute(ids, halves, own, swapped, prep, land_mask, bias2, proj):
     rows, cols = land_mask.shape
     patches1, frame2, cell1, keep1 = prep
-    other0 = swapped(0, own0)
-    total = partial(ids, patches1, own0, other0)
-    pieces, total = lax.optimization_barrier((pieces, total))
-    own_rest = jnp.concatenate(pieces, axis=0)
-    other_rest = swapped(1, own_rest)
-    hid0, cell0 = own_half(ids, halves, patches1, total, own_rest, bias2, cell1, keep1)
+    other = swapped(own)
+    hid0, cell0 = own_half(ids, halves, patches1, own, bias2, cell1, keep1)
     hidden, cell, flux = finished(
-        ids, halves, patches1, total, own0, own_rest, other0, other_rest, bias2, cell1, keep1,
+        ids, halves, patches1, own, other, bias2, cell1, keep1,
         hid0, cell0, frame2, land_mask.astype(F32), proj,
     )
     return hidden.reshape(rows, cols, HID), cell.reshape(rows, cols, HID), flux
@@ -411,30 +386,27 @@
     last, first = ends_of(*state)
     low = shifted(last, ("x", "c"), 1)
     high = shifted(first, ("x", "c"), -1)
+    last, first = sides_of(*state, low, high)
+    left = shifted(last, ("z", "y"), 1)
+    right = shifted(first, ("z", "y"), -1)
     halves = jnp.stack([c, 1 - c]).astype(jnp.int32)
     ids = jnp.stack([x, (x + 2) % 4, (x + 1) % 4, (x + 3) % 4]).astype(jnp.int32)
     proj = jnp.broadcast_to(projection[None], (16, HID))
     bias2 = bias_of(bias, c)
-    by_z, low, high, halves, ids, proj, bias2 = lax.optimization_barrier(
-        (by_z, low, high, halves, ids, proj, bias2)
+    by_z, left, right, halves, ids, proj, bias2 = lax.optimization_barrier(
+        (by_z, left, right, halves, ids, proj, bias2)
     )
 
     by_y = spread(by_z, "y")
-    last, first = sides_of(*state, low, high)
-    left = shifted(last, ("z", "y"), 1)
-    right = shifted(first, ("z", "y"), -1)
-
-    low_half, high_half = by_y[:2], by_y[2:]
-    up_low = turned(low_half, "x", 1)
-    down_high = turned(high_half, "x", -1)
-    up_high = turned(high_half, "x", 1)
-    down_low = turned(low_half, "x", -1)
-    far_low = turned(up_low, "x", 1)
-    far_high = turned(down_high, "x", -1)
-    pieces = [far_low, far_high, down_low, down_high, up_low, up_high]
+    up = turned(by_y, "x", 1)
+    down = turned(by_y, "x", -1)
     prep = prepared(cx, *state, low, high, left, right)
-    swapped = lambda slot, piece: turned(piece, "c", 1)
-    return compute(ids, halves, by_y, pieces, swapped, prep, land_mask, bias2, proj)
+    up, down, prep = lax.optimization_barrier((up, down, prep))
+    far_low = turned(up[:2], "x", 1)
+    far_high = turned(down[2:], "x", -1)
+    own = jnp.concatenate([by_y, far_low, far_high, down, up], axis=0)
+    swapped = lambda piece: turned(piece, "c", 1)
+    return compute(ids, halves, own, swapped, prep, land_mask, bias2, proj)
 
 
 def solution(mesh):

time: 102 us -> 111 us (1.088)
  the two profiles are of different devices: /device:TPU:31 before, /device:TPU:103 now
where the time goes in v6:
time: 111 us; the launch traced here: 110 us
  starting transfers between devices  47 us (42%)
  waiting for transfers between devices  25.5 us (23%)
  blocking collectives  15 us (14%)
  Pallas kernels  14 us (13%)
  local copies, waits for them, and re-layouts  6.58 us (6%)
    ppermute x5, waiting for transfers between devices, turned(): lax.ppermute(block, axis, [(i, (i + step) % count) for i in range(count)])  23.9 us
    ppermute x5, starting transfers between devices, turned(): lax.ppermute(block, axis, [(i, (i + step) % count) for i in range(count)])  20.8 us
    all_to_all x1, blocking collectives, spread(): return lax.all_to_all(copies, axes, 0, 0)  15 us
    all_to_all x1, starting transfers between devices, spread(): return lax.all_to_all(copies, axes, 0, 0)  13.7 us
    ppermute x4, starting transfers between devices, shifted(): return lax.ppermute(block, axes, pairs)  12.5 us
    pallas_call x1, Pallas kernels, finished(): pl.pallas_call(final_kernel, out_shape=(jax.ShapeDtypeStruct((512, HID),...  9.23 us
    unnamed x18, local copies, waits for them, and re-layouts  4.14 us
    pallas_call x1, Pallas kernels, own_half(): pl.pallas_call(own_kernel, out_shape=(jax.ShapeDtypeStruct((count, 128),...  3 us
  transfers between devices with their start and end apart: 10, of which 7 were waited for; matrix products, arithmetic and copies ran while one was open for 2% of the time, Pallas kernels for 4%

profile of v6, /device:TPU:103, one launch (start us, length us, event | category | flops | bytes accessed | tf_op | source)
XLA Modules:
  0.0 110.2 jit_solution(3883664521361273726)
XLA Ops:
  0.6 0.0 copy-start.3
  0.6 0.0 copy-start.1
  0.7 1.1 slice_bitcast_fusion
  1.7 0.8 slice.17
  2.5 0.1 copy.12
  2.6 0.1 copy.13
  2.7 0.7 broadcast_in_dim.8
  3.4 13.7 %all-to-all-start = ((bf16[16,8,640]{2,1,0:T(8,128)(2,1)}), bf16[16,8,640]{2,1,0:T(8,128)(2,1)S(1)}, u32[]{:S(2)}, u32[]{:S(2)}) async-start(bf16[16,8,640]{2,1,0:T(8,128)(2,1)} %broadcast_in_dim.8), calls=%async_computation | async-start | bytes 327680 | tf_op jit(solution)/shard_map/all_to_all | solution.py:37
  17.2 0.8 fusion.6
  17.9 0.2 copy.16
  18.1 0.9 copy.20
  19.0 0.1 copy.15
  19.1 0.1 fusion.2.aux_ref
  19.2 0.0 copy-start
  19.3 1.0 copy-done
  20.3 0.9 copy-done.2
  21.3 1.3 %collective-permute-start = (bf16[64,640]{1,0:T(8,128)(2,1)S(1)}, bf16[64,640]{1,0:T(8,128)(2,1)S(1)}, u32[]{:S(2)}, u32[]{:S(2)}) collective-permute-start(bf16[64,640]{1,0:T(8,128)(2,1)S(1)} %get-tuple-element.29), channel_id=1, source_target_pairs={{0,1},{1,2},{2,3},{3,4},{4,5},{5,6},{6,7},{8,9},{9,10},{10,11},{11... | collective-permute-start | bytes 245768 | tf_op jit(solution)/shard_map/ppermute | solution.py:48
  22.6 3.8 %collective-permute-start.1 = (bf16[64,640]{1,0:T(8,128)(2,1)S(1)}, bf16[64,640]{1,0:T(8,128)(2,1)S(1)}, u32[]{:S(2)}, u32[]{:S(2)}) collective-permute-start(bf16[64,640]{1,0:T(8,128)(2,1)S(1)} %get-tuple-element.30), channel_id=1, source_target_pairs={{1,0},{2,1},{3,2},{4,3},{5,4},{6,5},{7,6},{9,8},{10,9},{11,10},{12... | collective-permute-start | bytes 245768 | tf_op jit(solution)/shard_map/ppermute | solution.py:48
  26.4 0.1 reshape.37
  26.6 0.1 reshape.38
  26.7 0.1 pad_add_fusion.half_ref
  26.8 0.0 collective-permute-done.low_ref
  26.8 0.5 collective-permute-done.1.high_ref
  27.2 0.1 shard_map.95
  27.3 3.2 %collective-permute-start.2 = (bf16[48,640]{1,0:T(8,128)(2,1)S(1)}, bf16[48,640]{1,0:T(8,128)(2,1)S(1)}, u32[]{:S(2)}, u32[]{:S(2)}) collective-permute-start(bf16[48,640]{1,0:T(8,128)(2,1)S(1)} %get-tuple-element.31), channel_id=1, source_target_pairs={{0,8},{8,16},{16,24},{24,32},{32,40},{40,48},{48,56},{56,64},{64,7... | collective-permute-start | bytes 184328 | tf_op jit(solution)/shard_map/ppermute | solution.py:48
  30.5 4.2 %collective-permute-start.3 = (bf16[48,640]{1,0:T(8,128)(2,1)S(1)}, bf16[48,640]{1,0:T(8,128)(2,1)S(1)}, u32[]{:S(2)}, u32[]{:S(2)}) collective-permute-start(bf16[48,640]{1,0:T(8,128)(2,1)S(1)} %get-tuple-element.32), channel_id=1, source_target_pairs={{8,0},{16,8},{24,16},{32,24},{40,32},{48,40},{56,48},{64,56},{72,6... | collective-permute-start | bytes 184328 | tf_op jit(solution)/shard_map/ppermute | solution.py:48
  34.7 0.1 pad_add_fusion.1.ids_ref
  34.8 0.0 collective-permute-done.2.left_ref
  34.8 1.2 %collective-permute-done.3.right_ref = bf16[48,640]{1,0:T(8,128)(2,1)S(1)} collective-permute-done((bf16[48,640]{1,0:T(8,128)(2,1)S(1)}, bf16[48,640]{1,0:T(8,128)(2,1)S(1)}, u32[]{:S(2)}, u32[]{:S(2)}) %collective-permute-start.3) | collective-permute-done | bytes 61472 | tf_op jit(solution)/shard_map/ppermute | solution.py:48
  36.0 0.0 all-to-all-done
  36.0 0.1 broadcast_in_dim.11
  36.1 15.0 %all_to_all.10 = bf16[4,128,640]{2,1,0:T(8,128)(2,1)S(1)} all-to-all(bf16[4,128,640]{2,1,0:T(8,128)(2,1)S(1)} %broadcast_in_dim.11), channel_id=1, replica_groups=mesh['z'=16,'y'=4,'x'=4,'c'=2] {'y'}, dimensions={0} | all-to-all | bytes 1310720 | tf_op jit(solution)/shard_map/all_to_all | solution.py:37
  51.1 9.2 %collective-permute-start.4 = (bf16[4,128,640]{2,1,0:T(8,128)(2,1)S(1)}, bf16[4,128,640]{2,1,0:T(8,128)(2,1)S(1)}, u32[]{:S(2)}, u32[]{:S(2)}) collective-permute-start(bf16[4,128,640]{2,1,0:T(8,128)(2,1)S(1)} %all_to_all.10), channel_id=1, source_target_pairs={{0,2},{2,4},{4,6},{6,0},{1,3},{3,5},{5,7},{7,1},{8,10},{10,12},{12... | collective-permute-start | bytes 1966088 | tf_op jit(solution)/shard_map/ppermute | solution.py:42
  60.3 1.9 %collective-permute-start.5 = (bf16[4,128,640]{2,1,0:T(8,128)(2,1)S(1)}, bf16[4,128,640]{2,1,0:T(8,128)(2,1)S(1)}, u32[]{:S(2)}, u32[]{:S(2)}) collective-permute-start(bf16[4,128,640]{2,1,0:T(8,128)(2,1)S(1)} %all_to_all.10), channel_id=1, source_target_pairs={{0,6},{2,0},{4,2},{6,4},{1,7},{3,1},{5,3},{7,5},{8,14},{10,8},{12,... | collective-permute-start | bytes 1966088 | tf_op jit(solution)/shard_map/ppermute | solution.py:42
  62.3 1.7 %shard_map.96 = (bf16[4,624,640]{2,1,0:T(8,128)(2,1)S(1)}, bf16[512,256]{1,0:T(8,128)(2,1)S(1)}, f32[624,256]{1,0:T(8,128)S(1)}, f32[624,128]{1,0:T(8,128)S(1)}) custom-call(bf16[16,32,256]{2,1,0:T(8,128)(2,1)S(1)} %copy-done.3, f32[16,32,256]{2,1,0:T(8,128)S(1)} %copy-done.1, bf16[16,32,128]{2,1,0:T(8,128)(2,1)S(1)} %fusion.2.aux_ref, ...), custom_call_target="tpu_custom_call" | custom-call | bytes 100000 | tf_op jit(solution)/shard_map/pallas_call | solution.py:180
  64.0 10.1 %collective-permute-done.4 = bf16[4,128,640]{2,1,0:T(8,128)(2,1)S(1)} collective-permute-done((bf16[4,128,640]{2,1,0:T(8,128)(2,1)S(1)}, bf16[4,128,640]{2,1,0:T(8,128)(2,1)S(1)}, u32[]{:S(2)}, u32[]{:S(2)}) %collective-permute-start.4) | collective-permute-done | bytes 655392 | tf_op jit(solution)/shard_map/ppermute | solution.py:42
  74.1 5.0 %collective-permute-done.5 = bf16[4,128,640]{2,1,0:T(8,128)(2,1)S(1)} collective-permute-done((bf16[4,128,640]{2,1,0:T(8,128)(2,1)S(1)}, bf16[4,128,640]{2,1,0:T(8,128)(2,1)S(1)}, u32[]{:S(2)}, u32[]{:S(2)}) %collective-permute-start.5) | collective-permute-done | bytes 655392 | tf_op jit(solution)/shard_map/ppermute | solution.py:42
  79.1 1.9 %collective-permute-start.6 = (bf16[2,128,640]{2,1,0:T(8,128)(2,1)S(1)}, bf16[2,128,640]{2,1,0:T(8,128)(2,1)S(1)}, u32[]{:S(2)}, u32[]{:S(2)}) collective-permute-start(bf16[2,128,640]{2,1,0:T(8,128)(2,1)S(1)} %slice.14), channel_id=1, source_target_pairs={{0,2},{2,4},{4,6},{6,0},{1,3},{3,5},{5,7},{7,1},{8,10},{10,12},{12... | collective-permute-start | bytes 983048 | tf_op jit(solution)/shard_map/ppermute | solution.py:42
  81.1 3.4 %collective-permute-start.7 = (bf16[2,128,640]{2,1,0:T(8,128)(2,1)S(1)}, bf16[2,128,640]{2,1,0:T(8,128)(2,1)S(1)}, u32[]{:S(2)}, u32[]{:S(2)}) collective-permute-start(bf16[2,128,640]{2,1,0:T(8,128)(2,1)S(1)} %slice.15), channel_id=1, source_target_pairs={{0,6},{2,0},{4,2},{6,4},{1,7},{3,1},{5,3},{7,5},{8,14},{10,8},{12,... | collective-permute-start | bytes 983048 | tf_op jit(solution)/shard_map/ppermute | solution.py:42
  84.4 0.1 constant_dynamic-update-slice_fusion.4
  84.5 4.2 %collective-permute-done.6 = bf16[2,128,640]{2,1,0:T(8,128)(2,1)S(1)} collective-permute-done((bf16[2,128,640]{2,1,0:T(8,128)(2,1)S(1)}, bf16[2,128,640]{2,1,0:T(8,128)(2,1)S(1)}, u32[]{:S(2)}, u32[]{:S(2)}) %collective-permute-start.6) | collective-permute-done | bytes 327712 | tf_op jit(solution)/shard_map/ppermute | solution.py:42
  88.7 3.1 %collective-permute-done.7 = bf16[2,128,640]{2,1,0:T(8,128)(2,1)S(1)} collective-permute-done((bf16[2,128,640]{2,1,0:T(8,128)(2,1)S(1)}, bf16[2,128,640]{2,1,0:T(8,128)(2,1)S(1)}, u32[]{:S(2)}, u32[]{:S(2)}) %collective-permute-start.7) | collective-permute-done | bytes 327712 | tf_op jit(solution)/shard_map/ppermute | solution.py:42
  91.9 0.1 constant_dynamic-update-slice_fusion.1
  92.0 0.1 constant_dynamic-update-slice_fusion.refs_1_.own_ref
  92.1 4.3 %collective-permute-start.8 = (bf16[16,128,640]{2,1,0:T(8,128)(2,1)S(1)}, bf16[16,128,640]{2,1,0:T(8,128)(2,1)S(1)}, u32[]{:S(2)}, u32[]{:S(2)}) collective-permute-start(bf16[16,128,640]{2,1,0:T(8,128)(2,1)S(1)} %constant_dynamic-update-slice_fusion.refs_1_.own_ref), channel_id=1, source_target_pairs={{0,1},{1,0},{2,3},{3,2},{4,5},{5,4},{6,7},{7,6},{8,9},{9,8},{10,11... | collective-permute-start | bytes 7864328 | tf_op jit(solution)/shard_map/ppermute | solution.py:42
  96.5 3.0 %shard_map.97 = (bf16[624,128]{1,0:T(8,128)(2,1)S(1)}, f32[624,128]{1,0:T(8,128)S(1)}) custom-call(s32[4]{0:T(128)S(1)} %pad_add_fusion.1.ids_ref, s32[2]{0:T(128)S(1)} %pad_add_fusion.half_ref, bf16[4,624,640]{2,1,0:T(8,128)(2,1)S(1)} %get-tuple-element.42.refs_0_.patches_ref, bf16[16,128,640]{2,1,0:T(8,128)(2,1)S(1)} %constant_dynamic-update-slice_fusion.refs_1_.own_ref, ...), custom_call_target="tpu_custom_call" | custom-call | flops 1635778560 | bytes 6000000 | tf_op jit(solution)/shard_map/pallas_call | solution.py:266
  99.5 1.5 %collective-permute-done.8.other_ref = bf16[16,128,640]{2,1,0:T(8,128)(2,1)S(1)} collective-permute-done((bf16[16,128,640]{2,1,0:T(8,128)(2,1)S(1)}, bf16[16,128,640]{2,1,0:T(8,128)(2,1)S(1)}, u32[]{:S(2)}, u32[]{:S(2)}) %collective-permute-start.8) | collective-permute-done | bytes 2621472 | tf_op jit(solution)/shard_map/ppermute | solution.py:42
  101.0 9.2 %shard_map.98 = (bf16[512,256]{1,0:T(8,128)(2,1)}, f32[512,256]{1,0:T(8,128)}, f32[16,32]{1,0:T(8,128)}) custom-call(s32[4]{0:T(128)S(1)} %pad_add_fusion.1.ids_ref, s32[2]{0:T(128)S(1)} %pad_add_fusion.half_ref, bf16[4,624,640]{2,1,0:T(8,128)(2,1)S(1)} %get-tuple-element.42.refs_0_.patches_ref, ...), custom_call_target="tpu_custom_call" | custom-call | flops 4320133120 | bytes 14000000 | tf_op jit(solution)/shard_map/pallas_call | solution.py:337
  (17 shorter events, 0.2 us)
Async XLA Ops:
  0.6 26.6 %copy-start.3 = (bf16[16,32,256]{2,1,0:T(8,128)(2,1)S(1)}, bf16[16,32,256]{2,1,0:T(8,128)(2,1)}, u32[]{:S(2)}) copy-start(bf16[16,32,256]{2,1,0:T(8,128)(2,1)} %hidden_ref.5) | copy-start | bytes 786436
  0.6 26.6 %copy-start.1 = (f32[16,32,256]{2,1,0:T(8,128)S(1)}, f32[16,32,256]{2,1,0:T(8,128)}, u32[]{:S(2)}) copy-start(f32[16,32,256]{2,1,0:T(8,128)} %cell_ref.5) | copy-start | bytes 1572868
  0.7 25.7 %copy-start.4 = (f32[1024]{0:T(1024)S(1)}, f32[1024]{0:T(1024)}, u32[]{:S(2)}) copy-start(f32[1024]{0:T(1024)} %param.11) | copy-start | bytes 12292
  0.7 35.3 %copy-start.5 = (bf16[256]{0:T(256)(128)(2,1)S(1)}, bf16[256]{0:T(256)(128)(2,1)}, u32[]{:S(2)}) copy-start(bf16[256]{0:T(256)(128)(2,1)} %param.13) | copy-start | bytes 1540
  3.4 32.6 %all-to-all-start = ((bf16[16,8,640]{2,1,0:T(8,128)(2,1)}), bf16[16,8,640]{2,1,0:T(8,128)(2,1)S(1)}, u32[]{:S(2)}, u32[]{:S(2)}) async-start(bf16[16,8,640]{2,1,0:T(8,128)(2,1)} %broadcast_in_dim.8), calls=%async_computation | async-start | bytes 327680 | tf_op jit(solution)/shard_map/all_to_all | solution.py:37
  19.2 1.0 copy-start
  20.3 0.9 copy-start.2
  21.3 5.5 %collective-permute-start = (bf16[64,640]{1,0:T(8,128)(2,1)S(1)}, bf16[64,640]{1,0:T(8,128)(2,1)S(1)}, u32[]{:S(2)}, u32[]{:S(2)}) collective-permute-start(bf16[64,640]{1,0:T(8,128)(2,1)S(1)} %get-tuple-element.29), channel_id=1, source_target_pairs={{0,1},{1,2},{2,3},{3,4},{4,5},{5,6},{6,7},{8,9},{9,10},{10,11},{11... | collective-permute-start | bytes 245768 | tf_op jit(solution)/shard_map/ppermute | solution.py:48
  22.6 4.7 %collective-permute-start.1 = (bf16[64,640]{1,0:T(8,128)(2,1)S(1)}, bf16[64,640]{1,0:T(8,128)(2,1)S(1)}, u32[]{:S(2)}, u32[]{:S(2)}) collective-permute-start(bf16[64,640]{1,0:T(8,128)(2,1)S(1)} %get-tuple-element.30), channel_id=1, source_target_pairs={{1,0},{2,1},{3,2},{4,3},{5,4},{6,5},{7,6},{9,8},{10,9},{11,10},{12... | collective-permute-start | bytes 245768 | tf_op jit(solution)/shard_map/ppermute | solution.py:48
  27.3 7.5 %collective-permute-start.2 = (bf16[48,640]{1,0:T(8,128)(2,1)S(1)}, bf16[48,640]{1,0:T(8,128)(2,1)S(1)}, u32[]{:S(2)}, u32[]{:S(2)}) collective-permute-start(bf16[48,640]{1,0:T(8,128)(2,1)S(1)} %get-tuple-element.31), channel_id=1, source_target_pairs={{0,8},{8,16},{16,24},{24,32},{32,40},{40,48},{48,56},{56,64},{64,7... | collective-permute-start | bytes 184328 | tf_op jit(solution)/shard_map/ppermute | solution.py:48
  30.5 5.5 %collective-permute-start.3 = (bf16[48,640]{1,0:T(8,128)(2,1)S(1)}, bf16[48,640]{1,0:T(8,128)(2,1)S(1)}, u32[]{:S(2)}, u32[]{:S(2)}) collective-permute-start(bf16[48,640]{1,0:T(8,128)(2,1)S(1)} %get-tuple-element.32), channel_id=1, source_target_pairs={{8,0},{16,8},{24,16},{32,24},{40,32},{48,40},{56,48},{64,56},{72,6... | collective-permute-start | bytes 184328 | tf_op jit(solution)/shard_map/ppermute | solution.py:48
  51.1 23.0 %collective-permute-start.4 = (bf16[4,128,640]{2,1,0:T(8,128)(2,1)S(1)}, bf16[4,128,640]{2,1,0:T(8,128)(2,1)S(1)}, u32[]{:S(2)}, u32[]{:S(2)}) collective-permute-start(bf16[4,128,640]{2,1,0:T(8,128)(2,1)S(1)} %all_to_all.10), channel_id=1, source_target_pairs={{0,2},{2,4},{4,6},{6,0},{1,3},{3,5},{5,7},{7,1},{8,10},{10,12},{12... | collective-permute-start | bytes 1966088 | tf_op jit(solution)/shard_map/ppermute | solution.py:42
  60.3 18.7 %collective-permute-start.5 = (bf16[4,128,640]{2,1,0:T(8,128)(2,1)S(1)}, bf16[4,128,640]{2,1,0:T(8,128)(2,1)S(1)}, u32[]{:S(2)}, u32[]{:S(2)}) collective-permute-start(bf16[4,128,640]{2,1,0:T(8,128)(2,1)S(1)} %all_to_all.10), channel_id=1, source_target_pairs={{0,6},{2,0},{4,2},{6,4},{1,7},{3,1},{5,3},{7,5},{8,14},{10,8},{12,... | collective-permute-start | bytes 1966088 | tf_op jit(solution)/shard_map/ppermute | solution.py:42
  79.1 9.6 %collective-permute-start.6 = (bf16[2,128,640]{2,1,0:T(8,128)(2,1)S(1)}, bf16[2,128,640]{2,1,0:T(8,128)(2,1)S(1)}, u32[]{:S(2)}, u32[]{:S(2)}) collective-permute-start(bf16[2,128,640]{2,1,0:T(8,128)(2,1)S(1)} %slice.14), channel_id=1, source_target_pairs={{0,2},{2,4},{4,6},{6,0},{1,3},{3,5},{5,7},{7,1},{8,10},{10,12},{12... | collective-permute-start | bytes 983048 | tf_op jit(solution)/shard_map/ppermute | solution.py:42
  81.1 10.8 %collective-permute-start.7 = (bf16[2,128,640]{2,1,0:T(8,128)(2,1)S(1)}, bf16[2,128,640]{2,1,0:T(8,128)(2,1)S(1)}, u32[]{:S(2)}, u32[]{:S(2)}) collective-permute-start(bf16[2,128,640]{2,1,0:T(8,128)(2,1)S(1)} %slice.15), channel_id=1, source_target_pairs={{0,6},{2,0},{4,2},{6,4},{1,7},{3,1},{5,3},{7,5},{8,14},{10,8},{12,... | collective-permute-start | bytes 983048 | tf_op jit(solution)/shard_map/ppermute | solution.py:42
  92.1 8.9 %collective-permute-start.8 = (bf16[16,128,640]{2,1,0:T(8,128)(2,1)S(1)}, bf16[16,128,640]{2,1,0:T(8,128)(2,1)S(1)}, u32[]{:S(2)}, u32[]{:S(2)}) collective-permute-start(bf16[16,128,640]{2,1,0:T(8,128)(2,1)S(1)} %constant_dynamic-update-slice_fusion.refs_1_.own_ref), channel_id=1, source_target_pairs={{0,1},{1,0},{2,3},{3,2},{4,5},{5,4},{6,7},{7,6},{8,9},{9,8},{10,11... | collective-permute-start | bytes 7864328 | tf_op jit(solution)/shard_map/ppermute | solution.py:42

commit v7 on v6

--- a/solution.py
+++ b/solution.py
@@ -214,10 +214,10 @@
     return dots[0] + (dots[1] + dots[2])
 
 
-def product(patches, weight_ref, pair, chunk=0):
+def product(patches, weight_ref, pair, x):
     rhs = jnp.concatenate(
         [
-            weight_ref[chunk * 4 + y, q * 32 : (q + 1) * 32, :]
+            weight_ref[y * 4 + x, q * 32 : (q + 1) * 32, :]
             for q in (2 * pair, 2 * pair + 1)
             for y in range(4)
         ],
@@ -239,29 +239,29 @@
     return (keep * out_gate * jnp.tanh(cell)).astype(BF16), cell
 
 
-def gate_sums(patches_ref, ids_ref, weight_ref):
+def gate_sums(patches_ref, weight_ref):
     sums = []
     for pair in range(2):
         value = None
-        for slot in range(4):
-            part = product(patches_ref[ids_ref[slot]], weight_ref, pair, slot)
+        for x in range(4):
+            part = product(patches_ref[x], weight_ref, pair, x)
             value = part if value is None else value + part
         sums.append(value)
     return sums
 
 
-def first_half(i, half, ids_ref, patches_ref, weight_ref, bias_ref, cell_ref, keep_ref):
-    sums = gate_sums(patches_ref, ids_ref, weight_ref)
+def first_half(i, half, patches_ref, weight_ref, bias_ref, cell_ref, keep_ref):
+    sums = gate_sums(patches_ref, weight_ref)
     cell = moved(cell_ref[...], chooser(half, (HID, 128), 0))
     return updated(sums, bias_ref[i], cell, keep_ref[...])
 
 
-def own_kernel(ids_ref, half_ref, *refs):
+def own_kernel(half_ref, *refs):
     *ins, hid_out, cell_out = refs
-    hid_out[...], cell_out[...] = first_half(0, half_ref[0], ids_ref, *ins)
-
-
-def own_half(ids, halves, patches, weight, bias, cell, keep):
+    hid_out[...], cell_out[...] = first_half(0, half_ref[0], *ins)
+
+
+def own_half(halves, patches, weight, bias, cell, keep):
     count = patches.shape[1]
     return pl.pallas_call(
         own_kernel,
@@ -269,17 +269,16 @@
             jax.ShapeDtypeStruct((count, 128), BF16),
             jax.ShapeDtypeStruct((count, 128), F32),
         ),
-        in_specs=[SMEM] * 2 + [VMEM] * 5,
+        in_specs=[SMEM] + [VMEM] * 5,
         out_specs=(VMEM, VMEM),
         compiler_params=PARAMS,
         cost_estimate=pl.CostEstimate(
             flops=2 * count * KPAD * 512, bytes_accessed=6_000_000, transcendentals=count * 640
         ),
-    )(ids, halves, patches, weight, bias, cell, keep)
+    )(halves, patches, weight, bias, cell, keep)
 
 
 def final_kernel(
-    ids_ref,
     half_ref,
     patches_ref,
     own_ref,
@@ -300,7 +299,7 @@
 ):
     choices = [chooser(half_ref[i], (128, HID), 1) for i in range(2)]
     hid, cell = first_half(
-        1, half_ref[1], ids_ref, patches_ref, other_ref, bias_ref, cell_ref, keep_ref
+        1, half_ref[1], patches_ref, other_ref, bias_ref, cell_ref, keep_ref
     )
     cells = (cell0_ref[32:544, :], cell[32:544])
     natural = lax.dot_general(
@@ -319,7 +318,7 @@
 
     hid, cell = None, None
     for i, weight_ref in enumerate((own_ref, other_ref)):
-        sums = gate_sums(patches, ids_ref, weight_ref)
+        sums = gate_sums(patches, weight_ref)
         new_hid, new_cell = updated(sums, bias_ref[i], cells[i], keep_ref[32:544, :])
         one = lax.dot_general(new_hid, choices[i], NN, preferred_element_type=F32)
         two = moved(new_cell, choices[i])
@@ -333,7 +332,7 @@
         flux_out[row : row + 1, :] = flux[0:1, row * 32 : (row + 1) * 32] * keep2_ref[row : row + 1, :]
 
 
-def finished(ids, halves, *arrays):
+def finished(halves, *arrays):
     return pl.pallas_call(
         final_kernel,
         out_shape=(
@@ -341,23 +340,23 @@
             jax.ShapeDtypeStruct((512, HID), F32),
             jax.ShapeDtypeStruct((16, 32), F32),
         ),
-        in_specs=[SMEM] * 2 + [VMEM] * len(arrays),
+        in_specs=[SMEM] + [VMEM] * len(arrays),
         out_specs=(VMEM, VMEM, VMEM),
         scratch_shapes=[pltpu.VMEM((18, 48, HID), F32), pltpu.VMEM((4, 512, CHUNK), BF16)],
         compiler_params=PARAMS,
         cost_estimate=pl.CostEstimate(
             flops=2 * 824 * KPAD * 1024, bytes_accessed=14_000_000, transcendentals=1136 * 1280
         ),
-    )(ids, halves, *arrays)
-
-
-def compute(ids, halves, own, swapped, prep, land_mask, bias2, proj):
+    )(halves, *arrays)
+
+
+def compute(halves, own, swapped, prep, land_mask, bias2, proj):
     rows, cols = land_mask.shape
     patches1, frame2, cell1, keep1 = prep
     other = swapped(own)
-    hid0, cell0 = own_half(ids, halves, patches1, own, bias2, cell1, keep1)
+    hid0, cell0 = own_half(halves, patches1, own, bias2, cell1, keep1)
     hidden, cell, flux = finished(
-        ids, halves, patches1, own, other, bias2, cell1, keep1,
+        halves, patches1, own, other, bias2, cell1, keep1,
         hid0, cell0, frame2, land_mask.astype(F32), proj,
     )
     return hidden.reshape(rows, cols, HID), cell.reshape(rows, cols, HID), flux
@@ -390,23 +389,16 @@
     left = shifted(last, ("z", "y"), 1)
     right = shifted(first, ("z", "y"), -1)
     halves = jnp.stack([c, 1 - c]).astype(jnp.int32)
-    ids = jnp.stack([x, (x + 2) % 4, (x + 1) % 4, (x + 3) % 4]).astype(jnp.int32)
     proj = jnp.broadcast_to(projection[None], (16, HID))
     bias2 = bias_of(bias, c)
-    by_z, left, right, halves, ids, proj, bias2 = lax.optimization_barrier(
-        (by_z, left, right, halves, ids, proj, bias2)
+    by_z, left, right, halves, proj, bias2 = lax.optimization_barrier(
+        (by_z, left, right, halves, proj, bias2)
     )
 
-    by_y = spread(by_z, "y")
-    up = turned(by_y, "x", 1)
-    down = turned(by_y, "x", -1)
+    own = spread(by_z, ("y", "x"))
     prep = prepared(cx, *state, low, high, left, right)
-    up, down, prep = lax.optimization_barrier((up, down, prep))
-    far_low = turned(up[:2], "x", 1)
-    far_high = turned(down[2:], "x", -1)
-    own = jnp.concatenate([by_y, far_low, far_high, down, up], axis=0)
     swapped = lambda piece: turned(piece, "c", 1)
-    return compute(ids, halves, own, swapped, prep, land_mask, bias2, proj)
+    return compute(halves, own, swapped, prep, land_mask, bias2, proj)
 
 
 def solution(mesh):

time: 111 us -> 102 us (0.919)
  the two profiles are of different devices: /device:TPU:103 before, /device:TPU:97 now
where the time goes in v7:
time: 102 us; the launch traced here: 101 us
  blocking collectives  43.2 us (42%)
  starting transfers between devices  31 us (30%)
  Pallas kernels  13.8 us (14%)
  local copies, waits for them, and re-layouts  6.43 us (6%)
  waiting for transfers between devices  5 us (5%)
  other arithmetic  1.02 us (1%)
    all_to_all x1, blocking collectives, spread(): return lax.all_to_all(copies, axes, 0, 0)  43.2 us
    all_to_all x1, starting transfers between devices, spread(): return lax.all_to_all(copies, axes, 0, 0)  13.7 us
    ppermute x4, starting transfers between devices, shifted(): return lax.ppermute(block, axes, pairs)  13.6 us
    pallas_call x1, Pallas kernels, finished(): pl.pallas_call(final_kernel, out_shape=(jax.ShapeDtypeStruct((512, HID),...  9 us
    ppermute x4, waiting for transfers between devices, shifted(): return lax.ppermute(block, axes, pairs)  5 us
    unnamed x14, local copies, waits for them, and re-layouts  3.84 us
    ppermute x1, starting transfers between devices, turned(): lax.ppermute(block, axis, [(i, (i + step) % count) for i in range(count)])  3.69 us
    pallas_call x1, Pallas kernels, own_half(): pl.pallas_call(own_kernel, out_shape=(jax.ShapeDtypeStruct((count, 128),...  3.02 us
  transfers between devices with their start and end apart: 6, of which 2 were waited for; matrix products, arithmetic and copies ran while one was open for 2% of the time, Pallas kernels for 5%

profile of v7, /device:TPU:97, one launch (start us, length us, event | category | flops | bytes accessed | tf_op | source)
XLA Modules:
  0.0 101.3 jit_solution(12075521362512422485)
XLA Ops:
  0.6 0.0 copy-start.1
  0.6 0.0 copy-start.3
  0.7 0.0 copy-start.4
  0.7 0.0 copy-start.5
  0.7 0.8 slice.9
  1.5 1.0 slice_bitcast_fusion
  2.5 0.1 copy.12
  2.6 0.1 copy.13
  2.7 0.7 broadcast_in_dim.8
  3.4 13.7 %all-to-all-start = ((bf16[16,8,640]{2,1,0:T(8,128)(2,1)}), bf16[16,8,640]{2,1,0:T(8,128)(2,1)S(1)}, u32[]{:S(2)}, u32[]{:S(2)}) async-start(bf16[16,8,640]{2,1,0:T(8,128)(2,1)} %broadcast_in_dim.8), calls=%async_computation | async-start | bytes 327680 | tf_op jit(solution)/shard_map/all_to_all | solution.py:37
  17.2 0.9 copy.20
  18.0 0.1 copy.15
  18.1 0.8 fusion.6
  18.9 0.2 copy.16
  19.1 0.1 fusion.2.aux_ref
  19.2 0.0 copy-start
  19.3 1.0 %copy-done = f32[16,32,256]{2,1,0:T(8,128)S(1)} copy-done((f32[16,32,256]{2,1,0:T(8,128)S(1)}, f32[16,32,256]{2,1,0:T(8,128)}, u32[]{:S(2)}) %copy-start) | copy-done | bytes 524312
  20.3 0.0 copy-start.2
  20.3 0.9 copy-done.2
  21.3 4.2 %collective-permute-start = (bf16[64,640]{1,0:T(8,128)(2,1)S(1)}, bf16[64,640]{1,0:T(8,128)(2,1)S(1)}, u32[]{:S(2)}, u32[]{:S(2)}) collective-permute-start(bf16[64,640]{1,0:T(8,128)(2,1)S(1)} %get-tuple-element.22), channel_id=1, source_target_pairs={{0,1},{1,2},{2,3},{3,4},{4,5},{5,6},{6,7},{8,9},{9,10},{10,11},{11... | collective-permute-start | bytes 245768 | tf_op jit(solution)/shard_map/ppermute | solution.py:48
  25.5 1.9 %collective-permute-start.1 = (bf16[64,640]{1,0:T(8,128)(2,1)S(1)}, bf16[64,640]{1,0:T(8,128)(2,1)S(1)}, u32[]{:S(2)}, u32[]{:S(2)}) collective-permute-start(bf16[64,640]{1,0:T(8,128)(2,1)S(1)} %get-tuple-element.23), channel_id=1, source_target_pairs={{1,0},{2,1},{3,2},{4,3},{5,4},{6,5},{7,6},{9,8},{10,9},{11,10},{12... | collective-permute-start | bytes 245768 | tf_op jit(solution)/shard_map/ppermute | solution.py:48
  27.4 0.0 copy-done.4
  27.5 0.1 reshape.37
  27.6 0.1 reshape.38
  27.8 0.0 collective-permute-done.low_ref
  27.8 3.8 %collective-permute-done.1.high_ref = bf16[64,640]{1,0:T(8,128)(2,1)S(1)} collective-permute-done((bf16[64,640]{1,0:T(8,128)(2,1)S(1)}, bf16[64,640]{1,0:T(8,128)(2,1)S(1)}, u32[]{:S(2)}, u32[]{:S(2)}) %collective-permute-start.1) | collective-permute-done | bytes 81952 | tf_op jit(solution)/shard_map/ppermute | solution.py:48
  31.6 0.0 copy-done.1
  31.6 0.0 copy-done.3
  31.6 0.1 shard_map.95
  31.7 3.2 %collective-permute-start.2 = (bf16[48,640]{1,0:T(8,128)(2,1)S(1)}, bf16[48,640]{1,0:T(8,128)(2,1)S(1)}, u32[]{:S(2)}, u32[]{:S(2)}) collective-permute-start(bf16[48,640]{1,0:T(8,128)(2,1)S(1)} %get-tuple-element.24), channel_id=1, source_target_pairs={{0,8},{8,16},{16,24},{24,32},{32,40},{40,48},{48,56},{56,64},{64,7... | collective-permute-start | bytes 184328 | tf_op jit(solution)/shard_map/ppermute | solution.py:48
  34.9 4.2 %collective-permute-start.3 = (bf16[48,640]{1,0:T(8,128)(2,1)S(1)}, bf16[48,640]{1,0:T(8,128)(2,1)S(1)}, u32[]{:S(2)}, u32[]{:S(2)}) collective-permute-start(bf16[48,640]{1,0:T(8,128)(2,1)S(1)} %get-tuple-element.25), channel_id=1, source_target_pairs={{8,0},{16,8},{24,16},{32,24},{40,32},{48,40},{56,48},{64,56},{72,6... | collective-permute-start | bytes 184328 | tf_op jit(solution)/shard_map/ppermute | solution.py:48
  39.1 0.1 pad_add_fusion.half_ref
  39.1 0.0 collective-permute-done.2.left_ref
  39.1 1.2 %collective-permute-done.3.right_ref = bf16[48,640]{1,0:T(8,128)(2,1)S(1)} collective-permute-done((bf16[48,640]{1,0:T(8,128)(2,1)S(1)}, bf16[48,640]{1,0:T(8,128)(2,1)S(1)}, u32[]{:S(2)}, u32[]{:S(2)}) %collective-permute-start.3) | collective-permute-done | bytes 61472 | tf_op jit(solution)/shard_map/ppermute | solution.py:48
  40.3 0.0 all-to-all-done
  40.3 0.0 copy-done.5
  40.3 0.3 broadcast_in_dim.11
  40.7 43.2 %all_to_all.10.refs_1_.own_ref = bf16[16,128,640]{2,1,0:T(8,128)(2,1)S(1)} all-to-all(bf16[16,128,640]{2,1,0:T(8,128)(2,1)S(1)} %broadcast_in_dim.11), channel_id=1, replica_groups=mesh['z'=16,'y'=4,'x'=4,'c'=2] {'y','x'}, dimensions={0} | all-to-all | bytes 5242880 | tf_op jit(solution)/shard_map/all_to_all | solution.py:37
  83.9 3.7 %collective-permute-start.4 = (bf16[16,128,640]{2,1,0:T(8,128)(2,1)S(1)}, bf16[16,128,640]{2,1,0:T(8,128)(2,1)S(1)}, u32[]{:S(2)}, u32[]{:S(2)}) collective-permute-start(bf16[16,128,640]{2,1,0:T(8,128)(2,1)S(1)} %all_to_all.10.refs_1_.own_ref), channel_id=1, source_target_pairs={{0,1},{1,0},{2,3},{3,2},{4,5},{5,4},{6,7},{7,6},{8,9},{9,8},{10,11... | collective-permute-start | bytes 7864328 | tf_op jit(solution)/shard_map/ppermute | solution.py:42
  87.6 1.7 %shard_map.96 = (bf16[4,624,640]{2,1,0:T(8,128)(2,1)S(1)}, bf16[512,256]{1,0:T(8,128)(2,1)S(1)}, f32[624,256]{1,0:T(8,128)S(1)}, f32[624,128]{1,0:T(8,128)S(1)}) custom-call(bf16[16,32,256]{2,1,0:T(8,128)(2,1)S(1)} %copy-done.3, f32[16,32,256]{2,1,0:T(8,128)S(1)} %copy-done.1, bf16[16,32,128]{2,1,0:T(8,128)(2,1)S(1)} %fusion.2.aux_ref, ...), custom_call_target="tpu_custom_call" | custom-call | bytes 100000 | tf_op jit(solution)/shard_map/pallas_call | solution.py:180
  89.3 3.0 %shard_map.97 = (bf16[624,128]{1,0:T(8,128)(2,1)S(1)}, f32[624,128]{1,0:T(8,128)S(1)}) custom-call(s32[2]{0:T(128)S(1)} %pad_add_fusion.half_ref, bf16[4,624,640]{2,1,0:T(8,128)(2,1)S(1)} %get-tuple-element.29.refs_0_.patches_ref, bf16[16,128,640]{2,1,0:T(8,128)(2,1)S(1)} %all_to_all.10.refs_1_.own_ref, ...), custom_call_target="tpu_custom_call" | custom-call | flops 1635778560 | bytes 6000000 | tf_op jit(solution)/shard_map/pallas_call | solution.py:266
  92.3 0.0 collective-permute-done.4.other_ref
  92.3 9.0 %shard_map.98 = (bf16[512,256]{1,0:T(8,128)(2,1)}, f32[512,256]{1,0:T(8,128)}, f32[16,32]{1,0:T(8,128)}) custom-call(s32[2]{0:T(128)S(1)} %pad_add_fusion.half_ref, bf16[4,624,640]{2,1,0:T(8,128)(2,1)S(1)} %get-tuple-element.29.refs_0_.patches_ref, bf16[16,128,640]{2,1,0:T(8,128)(2,1)S(1)} %all_to_all.10.refs_1_.own_ref, ...), custom_call_target="tpu_custom_call" | custom-call | flops 4320133120 | bytes 14000000 | tf_op jit(solution)/shard_map/pallas_call | solution.py:336
  (6 shorter events, 0.1 us)
Async XLA Ops:
  0.6 30.9 %copy-start.1 = (f32[16,32,256]{2,1,0:T(8,128)S(1)}, f32[16,32,256]{2,1,0:T(8,128)}, u32[]{:S(2)}) copy-start(f32[16,32,256]{2,1,0:T(8,128)} %cell_ref.5) | copy-start | bytes 1572868
  0.6 30.9 %copy-start.3 = (bf16[16,32,256]{2,1,0:T(8,128)(2,1)S(1)}, bf16[16,32,256]{2,1,0:T(8,128)(2,1)}, u32[]{:S(2)}) copy-start(bf16[16,32,256]{2,1,0:T(8,128)(2,1)} %hidden_ref.5) | copy-start | bytes 786436
  0.7 26.8 %copy-start.4 = (f32[1024]{0:T(1024)S(1)}, f32[1024]{0:T(1024)}, u32[]{:S(2)}) copy-start(f32[1024]{0:T(1024)} %param.11) | copy-start | bytes 12292
  0.7 39.7 %copy-start.5 = (bf16[256]{0:T(256)(128)(2,1)S(1)}, bf16[256]{0:T(256)(128)(2,1)}, u32[]{:S(2)}) copy-start(bf16[256]{0:T(256)(128)(2,1)} %param.13) | copy-start | bytes 1540
  3.4 36.9 %all-to-all-start = ((bf16[16,8,640]{2,1,0:T(8,128)(2,1)}), bf16[16,8,640]{2,1,0:T(8,128)(2,1)S(1)}, u32[]{:S(2)}, u32[]{:S(2)}) async-start(bf16[16,8,640]{2,1,0:T(8,128)(2,1)} %broadcast_in_dim.8), calls=%async_computation | async-start | bytes 327680 | tf_op jit(solution)/shard_map/all_to_all | solution.py:37
  19.2 1.0 %copy-start = (f32[16,32,256]{2,1,0:T(8,128)S(1)}, f32[16,32,256]{2,1,0:T(8,128)}, u32[]{:S(2)}) copy-start(f32[16,32,256]{2,1,0:T(8,128)} %cell_ref.5) | copy-start | bytes 1572868
  20.3 0.9 copy-start.2
  21.3 6.5 %collective-permute-start = (bf16[64,640]{1,0:T(8,128)(2,1)S(1)}, bf16[64,640]{1,0:T(8,128)(2,1)S(1)}, u32[]{:S(2)}, u32[]{:S(2)}) collective-permute-start(bf16[64,640]{1,0:T(8,128)(2,1)S(1)} %get-tuple-element.22), channel_id=1, source_target_pairs={{0,1},{1,2},{2,3},{3,4},{4,5},{5,6},{6,7},{8,9},{9,10},{10,11},{11... | collective-permute-start | bytes 245768 | tf_op jit(solution)/shard_map/ppermute | solution.py:48
  25.5 6.1 %collective-permute-start.1 = (bf16[64,640]{1,0:T(8,128)(2,1)S(1)}, bf16[64,640]{1,0:T(8,128)(2,1)S(1)}, u32[]{:S(2)}, u32[]{:S(2)}) collective-permute-start(bf16[64,640]{1,0:T(8,128)(2,1)S(1)} %get-tuple-element.23), channel_id=1, source_target_pairs={{1,0},{2,1},{3,2},{4,3},{5,4},{6,5},{7,6},{9,8},{10,9},{11,10},{12... | collective-permute-start | bytes 245768 | tf_op jit(solution)/shard_map/ppermute | solution.py:48
  31.7 7.5 %collective-permute-start.2 = (bf16[48,640]{1,0:T(8,128)(2,1)S(1)}, bf16[48,640]{1,0:T(8,128)(2,1)S(1)}, u32[]{:S(2)}, u32[]{:S(2)}) collective-permute-start(bf16[48,640]{1,0:T(8,128)(2,1)S(1)} %get-tuple-element.24), channel_id=1, source_target_pairs={{0,8},{8,16},{16,24},{24,32},{32,40},{40,48},{48,56},{56,64},{64,7... | collective-permute-start | bytes 184328 | tf_op jit(solution)/shard_map/ppermute | solution.py:48
  34.9 5.5 %collective-permute-start.3 = (bf16[48,640]{1,0:T(8,128)(2,1)S(1)}, bf16[48,640]{1,0:T(8,128)(2,1)S(1)}, u32[]{:S(2)}, u32[]{:S(2)}) collective-permute-start(bf16[48,640]{1,0:T(8,128)(2,1)S(1)} %get-tuple-element.25), channel_id=1, source_target_pairs={{8,0},{16,8},{24,16},{32,24},{40,32},{48,40},{56,48},{64,56},{72,6... | collective-permute-start | bytes 184328 | tf_op jit(solution)/shard_map/ppermute | solution.py:48
  83.9 8.5 %collective-permute-start.4 = (bf16[16,128,640]{2,1,0:T(8,128)(2,1)S(1)}, bf16[16,128,640]{2,1,0:T(8,128)(2,1)S(1)}, u32[]{:S(2)}, u32[]{:S(2)}) collective-permute-start(bf16[16,128,640]{2,1,0:T(8,128)(2,1)S(1)} %all_to_all.10.refs_1_.own_ref), channel_id=1, source_target_pairs={{0,1},{1,0},{2,3},{3,2},{4,5},{5,4},{6,7},{7,6},{8,9},{9,8},{10,11... | collective-permute-start | bytes 7864328 | tf_op jit(solution)/shard_map/ppermute | solution.py:42

commit v8 on v7

--- a/solution.py
+++ b/solution.py
@@ -386,16 +386,17 @@
     low = shifted(last, ("x", "c"), 1)
     high = shifted(first, ("x", "c"), -1)
     last, first = sides_of(*state, low, high)
-    left = shifted(last, ("z", "y"), 1)
-    right = shifted(first, ("z", "y"), -1)
     halves = jnp.stack([c, 1 - c]).astype(jnp.int32)
     proj = jnp.broadcast_to(projection[None], (16, HID))
     bias2 = bias_of(bias, c)
-    by_z, left, right, halves, proj, bias2 = lax.optimization_barrier(
-        (by_z, left, right, halves, proj, bias2)
+    by_z, last, first, halves, proj, bias2 = lax.optimization_barrier(
+        (by_z, last, first, halves, proj, bias2)
     )
 
     own = spread(by_z, ("y", "x"))
+    own, last, first = lax.optimization_barrier((own, last, first))
+    left = shifted(last, ("z", "y"), 1)
+    right = shifted(first, ("z", "y"), -1)
     prep = prepared(cx, *state, low, high, left, right)
     swapped = lambda piece: turned(piece, "c", 1)
     return compute(halves, own, swapped, prep, land_mask, bias2, proj)

time: 102 us -> 102 us (level)
  the two profiles are of different devices: /device:TPU:97 before, /device:TPU:120 now
where the time goes in v8:
time: 102 us
  blocking collectives  38.2 us (37%)
  starting transfers between devices  27 us (26%)
  waiting for transfers between devices  14.6 us (14%)
  Pallas kernels  13.8 us (14%)
  local copies, waits for them, and re-layouts  6.43 us (6%)
  other arithmetic  1.02 us (1%)
    all_to_all x1, blocking collectives, spread(): return lax.all_to_all(copies, axes, 0, 0)  38.2 us
    all_to_all x1, starting transfers between devices, spread(): return lax.all_to_all(copies, axes, 0, 0)  14.3 us
    ppermute x4, starting transfers between devices, shifted(): return lax.ppermute(block, axes, pairs)  10.8 us
    ppermute x4, waiting for transfers between devices, shifted(): return lax.ppermute(block, axes, pairs)  10.7 us
    pallas_call x1, Pallas kernels, finished(): pl.pallas_call(final_kernel, out_shape=(jax.ShapeDtypeStruct((512, HID),...  9 us
    all_to_all x1, waiting for transfers between devices, spread(): return lax.all_to_all(copies, axes, 0, 0)  3.89 us
    unnamed x14, local copies, waits for them, and re-layouts  3.84 us
    pallas_call x1, Pallas kernels, own_half(): pl.pallas_call(own_kernel, out_shape=(jax.ShapeDtypeStruct((count, 128),...  3.02 us
  transfers between devices with their start and end apart: 6, of which 3 were waited for; matrix products, arithmetic and copies ran while one was open for 2% of the time, Pallas kernels for 5%

profile of v8, /device:TPU:120, one launch (start us, length us, event | category | flops | bytes accessed | tf_op | source)
XLA Modules:
  0.0 101.9 jit_solution(13890615823288927494)
XLA Ops:
  0.6 0.0 copy-start.1
  0.6 0.0 copy-start.3
  0.7 0.0 copy-start.4
  0.7 0.0 copy-start.5
  0.7 0.8 slice.9
  1.5 1.0 slice_bitcast_fusion
  2.5 0.1 copy.12
  2.6 0.1 copy.13
  2.7 0.7 broadcast_in_dim.8
  3.4 14.3 %all-to-all-start = ((bf16[16,8,640]{2,1,0:T(8,128)(2,1)}), bf16[16,8,640]{2,1,0:T(8,128)(2,1)S(1)}, u32[]{:S(2)}, u32[]{:S(2)}) async-start(bf16[16,8,640]{2,1,0:T(8,128)(2,1)} %broadcast_in_dim.8), calls=%async_computation | async-start | bytes 327680 | tf_op jit(solution)/shard_map/all_to_all | solution.py:37
  17.7 0.9 copy.20
  18.6 0.1 copy.15
  18.7 0.8 fusion.6
  19.5 0.2 copy.16
  19.7 0.1 fusion.2.aux_ref
  19.8 0.0 copy-start
  19.8 1.0 %copy-done = f32[16,32,256]{2,1,0:T(8,128)S(1)} copy-done((f32[16,32,256]{2,1,0:T(8,128)S(1)}, f32[16,32,256]{2,1,0:T(8,128)}, u32[]{:S(2)}) %copy-start) | copy-done | bytes 524312
  20.9 0.0 copy-start.2
  20.9 0.9 copy-done.2
  21.8 1.3 %collective-permute-start = (bf16[64,640]{1,0:T(8,128)(2,1)S(1)}, bf16[64,640]{1,0:T(8,128)(2,1)S(1)}, u32[]{:S(2)}, u32[]{:S(2)}) collective-permute-start(bf16[64,640]{1,0:T(8,128)(2,1)S(1)} %get-tuple-element.25), channel_id=1, source_target_pairs={{0,1},{1,2},{2,3},{3,4},{4,5},{5,6},{6,7},{8,9},{9,10},{10,11},{11... | collective-permute-start | bytes 245768 | tf_op jit(solution)/shard_map/ppermute | solution.py:48
  23.1 1.3 %collective-permute-start.1 = (bf16[64,640]{1,0:T(8,128)(2,1)S(1)}, bf16[64,640]{1,0:T(8,128)(2,1)S(1)}, u32[]{:S(2)}, u32[]{:S(2)}) collective-permute-start(bf16[64,640]{1,0:T(8,128)(2,1)S(1)} %get-tuple-element.26), channel_id=1, source_target_pairs={{1,0},{2,1},{3,2},{4,3},{5,4},{6,5},{7,6},{9,8},{10,9},{11,10},{12... | collective-permute-start | bytes 245768 | tf_op jit(solution)/shard_map/ppermute | solution.py:48
  24.4 0.0 copy-done.4
  24.4 0.1 reshape.37
  24.6 0.1 reshape.38
  24.7 0.1 pad_add_fusion.half_ref
  24.8 0.0 collective-permute-done.low_ref
  24.8 3.2 %collective-permute-done.1.high_ref = bf16[64,640]{1,0:T(8,128)(2,1)S(1)} collective-permute-done((bf16[64,640]{1,0:T(8,128)(2,1)S(1)}, bf16[64,640]{1,0:T(8,128)(2,1)S(1)}, u32[]{:S(2)}, u32[]{:S(2)}) %collective-permute-start.1) | collective-permute-done | bytes 81952 | tf_op jit(solution)/shard_map/ppermute | solution.py:48
  28.0 0.0 copy-done.1
  28.0 0.0 copy-done.3
  28.0 0.1 shard_map.95
  28.1 3.9 %all-to-all-done = bf16[16,8,640]{2,1,0:T(8,128)(2,1)S(1)} async-done(((bf16[16,8,640]{2,1,0:T(8,128)(2,1)}), bf16[16,8,640]{2,1,0:T(8,128)(2,1)S(1)}, u32[]{:S(2)}, u32[]{:S(2)}) %all-to-all-start) | async-done | bytes 163872 | tf_op jit(solution)/shard_map/all_to_all | solution.py:37
  32.0 0.0 copy-done.5
  32.0 0.3 broadcast_in_dim.11
  32.3 38.2 %all_to_all.10.refs_1_.own_ref = bf16[16,128,640]{2,1,0:T(8,128)(2,1)S(1)} all-to-all(bf16[16,128,640]{2,1,0:T(8,128)(2,1)S(1)} %broadcast_in_dim.11), channel_id=1, replica_groups=mesh['z'=16,'y'=4,'x'=4,'c'=2] {'y','x'}, dimensions={0} | all-to-all | bytes 5242880 | tf_op jit(solution)/shard_map/all_to_all | solution.py:37
  70.6 1.9 %collective-permute-start.4 = (bf16[16,128,640]{2,1,0:T(8,128)(2,1)S(1)}, bf16[16,128,640]{2,1,0:T(8,128)(2,1)S(1)}, u32[]{:S(2)}, u32[]{:S(2)}) collective-permute-start(bf16[16,128,640]{2,1,0:T(8,128)(2,1)S(1)} %all_to_all.10.refs_1_.own_ref), channel_id=1, source_target_pairs={{0,1},{1,0},{2,3},{3,2},{4,5},{5,4},{6,7},{7,6},{8,9},{9,8},{10,11... | collective-permute-start | bytes 7864328 | tf_op jit(solution)/shard_map/ppermute | solution.py:42
  72.5 6.3 %collective-permute-start.2 = (bf16[48,640]{1,0:T(8,128)(2,1)S(1)}, bf16[48,640]{1,0:T(8,128)(2,1)S(1)}, u32[]{:S(2)}, u32[]{:S(2)}) collective-permute-start(bf16[48,640]{1,0:T(8,128)(2,1)S(1)} %get-tuple-element.33), channel_id=1, source_target_pairs={{0,8},{8,16},{16,24},{24,32},{32,40},{40,48},{48,56},{56,64},{64,7... | collective-permute-start | bytes 184328 | tf_op jit(solution)/shard_map/ppermute | solution.py:48
  78.7 1.9 %collective-permute-start.3 = (bf16[48,640]{1,0:T(8,128)(2,1)S(1)}, bf16[48,640]{1,0:T(8,128)(2,1)S(1)}, u32[]{:S(2)}, u32[]{:S(2)}) collective-permute-start(bf16[48,640]{1,0:T(8,128)(2,1)S(1)} %get-tuple-element.34), channel_id=1, source_target_pairs={{8,0},{16,8},{24,16},{32,24},{40,32},{48,40},{56,48},{64,56},{72,6... | collective-permute-start | bytes 184328 | tf_op jit(solution)/shard_map/ppermute | solution.py:48
  80.7 0.0 collective-permute-done.2.left_ref
  80.7 7.5 %collective-permute-done.3.right_ref = bf16[48,640]{1,0:T(8,128)(2,1)S(1)} collective-permute-done((bf16[48,640]{1,0:T(8,128)(2,1)S(1)}, bf16[48,640]{1,0:T(8,128)(2,1)S(1)}, u32[]{:S(2)}, u32[]{:S(2)}) %collective-permute-start.3) | collective-permute-done | bytes 61472 | tf_op jit(solution)/shard_map/ppermute | solution.py:48
  88.2 1.7 %shard_map.96 = (bf16[4,624,640]{2,1,0:T(8,128)(2,1)S(1)}, bf16[512,256]{1,0:T(8,128)(2,1)S(1)}, f32[624,256]{1,0:T(8,128)S(1)}, f32[624,128]{1,0:T(8,128)S(1)}) custom-call(bf16[16,32,256]{2,1,0:T(8,128)(2,1)S(1)} %copy-done.3, f32[16,32,256]{2,1,0:T(8,128)S(1)} %copy-done.1, bf16[16,32,128]{2,1,0:T(8,128)(2,1)S(1)} %fusion.2.aux_ref, ...), custom_call_target="tpu_custom_call" | custom-call | bytes 100000 | tf_op jit(solution)/shard_map/pallas_call | solution.py:180
  89.9 3.0 %shard_map.97 = (bf16[624,128]{1,0:T(8,128)(2,1)S(1)}, f32[624,128]{1,0:T(8,128)S(1)}) custom-call(s32[2]{0:T(128)S(1)} %pad_add_fusion.half_ref, bf16[4,624,640]{2,1,0:T(8,128)(2,1)S(1)} %get-tuple-element.35.refs_0_.patches_ref, bf16[16,128,640]{2,1,0:T(8,128)(2,1)S(1)} %all_to_all.10.refs_1_.own_ref, ...), custom_call_target="tpu_custom_call" | custom-call | flops 1635778560 | bytes 6000000 | tf_op jit(solution)/shard_map/pallas_call | solution.py:266
  92.9 0.0 collective-permute-done.4.other_ref
  92.9 9.0 %shard_map.98 = (bf16[512,256]{1,0:T(8,128)(2,1)}, f32[512,256]{1,0:T(8,128)}, f32[16,32]{1,0:T(8,128)}) custom-call(s32[2]{0:T(128)S(1)} %pad_add_fusion.half_ref, bf16[4,624,640]{2,1,0:T(8,128)(2,1)S(1)} %get-tuple-element.35.refs_0_.patches_ref, bf16[16,128,640]{2,1,0:T(8,128)(2,1)S(1)} %all_to_all.10.refs_1_.own_ref, ...), custom_call_target="tpu_custom_call" | custom-call | flops 4320133120 | bytes 14000000 | tf_op jit(solution)/shard_map/pallas_call | solution.py:336
  (6 shorter events, 0.1 us)
Async XLA Ops:
  0.6 27.4 %copy-start.1 = (f32[16,32,256]{2,1,0:T(8,128)S(1)}, f32[16,32,256]{2,1,0:T(8,128)}, u32[]{:S(2)}) copy-start(f32[16,32,256]{2,1,0:T(8,128)} %cell_ref.5) | copy-start | bytes 1572868
  0.6 27.4 %copy-start.3 = (bf16[16,32,256]{2,1,0:T(8,128)(2,1)S(1)}, bf16[16,32,256]{2,1,0:T(8,128)(2,1)}, u32[]{:S(2)}) copy-start(bf16[16,32,256]{2,1,0:T(8,128)(2,1)} %hidden_ref.5) | copy-start | bytes 786436
  0.7 23.8 %copy-start.4 = (f32[1024]{0:T(1024)S(1)}, f32[1024]{0:T(1024)}, u32[]{:S(2)}) copy-start(f32[1024]{0:T(1024)} %param.11) | copy-start | bytes 12292
  0.7 31.3 %copy-start.5 = (bf16[256]{0:T(256)(128)(2,1)S(1)}, bf16[256]{0:T(256)(128)(2,1)}, u32[]{:S(2)}) copy-start(bf16[256]{0:T(256)(128)(2,1)} %param.13) | copy-start | bytes 1540
  3.4 28.6 %all-to-all-start = ((bf16[16,8,640]{2,1,0:T(8,128)(2,1)}), bf16[16,8,640]{2,1,0:T(8,128)(2,1)S(1)}, u32[]{:S(2)}, u32[]{:S(2)}) async-start(bf16[16,8,640]{2,1,0:T(8,128)(2,1)} %broadcast_in_dim.8), calls=%async_computation | async-start | bytes 327680 | tf_op jit(solution)/shard_map/all_to_all | solution.py:37
  19.8 1.0 %copy-start = (f32[16,32,256]{2,1,0:T(8,128)S(1)}, f32[16,32,256]{2,1,0:T(8,128)}, u32[]{:S(2)}) copy-start(f32[16,32,256]{2,1,0:T(8,128)} %cell_ref.5) | copy-start | bytes 1572868
  20.9 0.9 copy-start.2
  21.8 3.0 %collective-permute-start = (bf16[64,640]{1,0:T(8,128)(2,1)S(1)}, bf16[64,640]{1,0:T(8,128)(2,1)S(1)}, u32[]{:S(2)}, u32[]{:S(2)}) collective-permute-start(bf16[64,640]{1,0:T(8,128)(2,1)S(1)} %get-tuple-element.25), channel_id=1, source_target_pairs={{0,1},{1,2},{2,3},{3,4},{4,5},{5,6},{6,7},{8,9},{9,10},{10,11},{11... | collective-permute-start | bytes 245768 | tf_op jit(solution)/shard_map/ppermute | solution.py:48
  23.1 4.9 %collective-permute-start.1 = (bf16[64,640]{1,0:T(8,128)(2,1)S(1)}, bf16[64,640]{1,0:T(8,128)(2,1)S(1)}, u32[]{:S(2)}, u32[]{:S(2)}) collective-permute-start(bf16[64,640]{1,0:T(8,128)(2,1)S(1)} %get-tuple-element.26), channel_id=1, source_target_pairs={{1,0},{2,1},{3,2},{4,3},{5,4},{6,5},{7,6},{9,8},{10,9},{11,10},{12... | collective-permute-start | bytes 245768 | tf_op jit(solution)/shard_map/ppermute | solution.py:48
  70.6 22.4 %collective-permute-start.4 = (bf16[16,128,640]{2,1,0:T(8,128)(2,1)S(1)}, bf16[16,128,640]{2,1,0:T(8,128)(2,1)S(1)}, u32[]{:S(2)}, u32[]{:S(2)}) collective-permute-start(bf16[16,128,640]{2,1,0:T(8,128)(2,1)S(1)} %all_to_all.10.refs_1_.own_ref), channel_id=1, source_target_pairs={{0,1},{1,0},{2,3},{3,2},{4,5},{5,4},{6,7},{7,6},{8,9},{9,8},{10,11... | collective-permute-start | bytes 7864328 | tf_op jit(solution)/shard_map/ppermute | solution.py:42
  72.5 8.2 %collective-permute-start.2 = (bf16[48,640]{1,0:T(8,128)(2,1)S(1)}, bf16[48,640]{1,0:T(8,128)(2,1)S(1)}, u32[]{:S(2)}, u32[]{:S(2)}) collective-permute-start(bf16[48,640]{1,0:T(8,128)(2,1)S(1)} %get-tuple-element.33), channel_id=1, source_target_pairs={{0,8},{8,16},{16,24},{24,32},{32,40},{40,48},{48,56},{56,64},{64,7... | collective-permute-start | bytes 184328 | tf_op jit(solution)/shard_map/ppermute | solution.py:48
  78.7 9.4 %collective-permute-start.3 = (bf16[48,640]{1,0:T(8,128)(2,1)S(1)}, bf16[48,640]{1,0:T(8,128)(2,1)S(1)}, u32[]{:S(2)}, u32[]{:S(2)}) collective-permute-start(bf16[48,640]{1,0:T(8,128)(2,1)S(1)} %get-tuple-element.34), channel_id=1, source_target_pairs={{8,0},{16,8},{24,16},{32,24},{40,32},{48,40},{56,48},{64,56},{72,6... | collective-permute-start | bytes 184328 | tf_op jit(solution)/shard_map/ppermute | solution.py:48

commit v9 on v7

--- a/solution.py
+++ b/solution.py
@@ -48,24 +48,14 @@
     return lax.ppermute(block, axes, pairs)
 
 
-def ends_kernel(hidden_ref, cell_ref, aux_ref, last_out, first_out):
-    for out, start in ((last_out, 14), (first_out, 0)):
-        for j in range(2):
-            rows = slice(j * 32, (j + 1) * 32)
-            out[rows, :HID] = hidden_ref[start + j]
-            out[rows, HID : 2 * HID] = cell_ref[start + j].astype(BF16)
-            out[rows, 2 * HID :] = aux_ref[start + j]
-
-
-def ends_of(hidden, cell, aux):
-    return pl.pallas_call(
-        ends_kernel,
-        out_shape=(jax.ShapeDtypeStruct((64, PACK), BF16),) * 2,
-        in_specs=[VMEM] * 3,
-        out_specs=(VMEM, VMEM),
-        compiler_params=PARAMS,
-        cost_estimate=pl.CostEstimate(flops=0, bytes_accessed=1_000_000, transcendentals=0),
-    )(hidden, cell, aux)
+def ends_of(hidden, cell, frames, land_mask):
+    pick = lambda array, axis: jnp.concatenate(
+        [lax.slice_in_dim(array, 14, 16, axis=axis), lax.slice_in_dim(array, 0, 2, axis=axis)], axis
+    )
+    aux = aux_of(pick(frames, 1), pick(land_mask, 0))
+    packed = jnp.concatenate([pick(hidden, 0), pick(cell, 0).astype(BF16), aux], axis=-1)
+    packed = packed.reshape(128, PACK)
+    return packed[:64], packed[64:]
 
 
 def sides_kernel(hidden_ref, cell_ref, aux_ref, low_ref, high_ref, last_out, first_out, last, first):
@@ -377,26 +367,25 @@
 def body(frames, hidden_init, cell_init, conv_weight, bias, land_mask, projection):
     cx = frames.shape[3]
     x, c = lax.axis_index("x"), lax.axis_index("c")
-    packed = pack_weights(conv_weight)
-    unit = lax.dynamic_slice(packed, (c * 8, x * (KPAD // 4)), (8, KPAD // 4))
-    by_z = spread(unit, "z").reshape(128, KPAD // 4)
-
-    state = (hidden_init, cell_init, aux_of(frames, land_mask))
-    last, first = ends_of(*state)
+    last, first = ends_of(hidden_init, cell_init, frames, land_mask)
     low = shifted(last, ("x", "c"), 1)
     high = shifted(first, ("x", "c"), -1)
+    packed = pack_weights(conv_weight)
+    unit = lax.dynamic_slice(packed, (c * 8, x * CHUNK), (8, CHUNK))
+    unit, low, high = lax.optimization_barrier((unit, low, high))
+    by_z = spread(unit, "z").reshape(128, CHUNK)
+
+    state = (hidden_init, cell_init, aux_of(frames, land_mask))
     last, first = sides_of(*state, low, high)
     left = shifted(last, ("z", "y"), 1)
     right = shifted(first, ("z", "y"), -1)
+    prep = prepared(cx, *state, low, high, left, right)
     halves = jnp.stack([c, 1 - c]).astype(jnp.int32)
     proj = jnp.broadcast_to(projection[None], (16, HID))
     bias2 = bias_of(bias, c)
-    by_z, left, right, halves, proj, bias2 = lax.optimization_barrier(
-        (by_z, left, right, halves, proj, bias2)
-    )
+    by_z, prep, halves, proj, bias2 = lax.optimization_barrier((by_z, prep, halves, proj, bias2))
 
     own = spread(by_z, ("y", "x"))
-    prep = prepared(cx, *state, low, high, left, right)
     swapped = lambda piece: turned(piece, "c", 1)
     return compute(halves, own, swapped, prep, land_mask, bias2, proj)
 

time: 102 us -> 103 us (level)
  other arithmetic: 1.02 us -> 2.14 us
    ppermute x4, waiting for transfers between devices: 5 us -> 3.35 us  [shifted(): return lax.ppermute(block, axes, pairs)]
    slice x0 -> x3, local copies, waits for them, and re-layouts: none -> 1.53 us  [the longest x2 1.51 us: ends_of(): lax.slice_in_dim(array, 14, 16, axis=axis)]
    ppermute x1, waiting for transfers between devices: 0.01 us -> 1.49 us  [turned(): lax.ppermute(block, axis, [(i, (i + step) % count) for i in range(count)])]
    another operation x0 -> x1, other arithmetic: none -> 1.07 us
    unnamed x14 -> x17, local copies, waits for them, and re-layouts: 3.84 us -> 2.79 us
  transfers between devices with their start and end apart: 6 -> 6, of which waited for: 2 -> 3; matrix products, arithmetic and copies ran while one was open for 2% -> 3% of each run, Pallas kernels for 5% -> 5%
where the time goes in v9:
time: 103 us
  blocking collectives  43.7 us (42%)
  starting transfers between devices  30.6 us (30%)
  Pallas kernels  13.8 us (13%)
  local copies, waits for them, and re-layouts  6.87 us (7%)
  waiting for transfers between devices  4.84 us (5%)
  other arithmetic  2.14 us (2%)
    all_to_all x1, blocking collectives, spread(): return lax.all_to_all(copies, axes, 0, 0)  43.7 us
    all_to_all x1, starting transfers between devices, spread(): return lax.all_to_all(copies, axes, 0, 0)  13.7 us
    ppermute x4, starting transfers between devices, shifted(): return lax.ppermute(block, axes, pairs)  13 us
    pallas_call x1, Pallas kernels, finished(): pl.pallas_call(final_kernel, out_shape=(jax.ShapeDtypeStruct((512, HID),...  8.99 us
    ppermute x1, starting transfers between devices, turned(): lax.ppermute(block, axis, [(i, (i + step) % count) for i in range(count)])  3.88 us
    ppermute x4, waiting for transfers between devices, shifted(): return lax.ppermute(block, axes, pairs)  3.35 us
    pallas_call x1, Pallas kernels, own_half(): pl.pallas_call(own_kernel, out_shape=(jax.ShapeDtypeStruct((count, 128),...  3.01 us
    unnamed x17, local copies, waits for them, and re-layouts  2.79 us
  transfers between devices with their start and end apart: 6, of which 3 were waited for; matrix products, arithmetic and copies ran while one was open for 3% of the time, Pallas kernels for 5%

profile of v9, /device:TPU:97, one launch (start us, length us, event | category | flops | bytes accessed | tf_op | source)
XLA Modules:
  0.0 102.9 jit_solution(6938459587645796944)
XLA Ops:
  0.6 0.0 copy-start.4
  0.6 0.0 copy-start
  0.7 0.0 copy-start.3
  0.7 0.0 copy-start.5
  0.7 0.8 fusion.12
  1.5 0.7 fusion.11
  2.3 0.1 copy.25
  2.4 1.1 %convert.14 = bf16[16,32,256]{2,1,0:T(8,128)(2,1)S(1)} convert(f32[16,32,256]{2,1,0:T(8,128)} %cell_ref.3) | non-fusion elementwise | flops 131072 | bytes 786432 | tf_op jit(solution)/shard_map/convert.9
  3.5 0.8 fusion.8
  4.2 0.0 copy-start.6
  4.3 3.7 %collective-permute-start = (bf16[64,640]{1,0:T(8,128)(2,1)S(1)}, bf16[64,640]{1,0:T(8,128)(2,1)S(1)}, u32[]{:S(2)}, u32[]{:S(2)}) collective-permute-start(bf16[64,640]{1,0:T(8,128)(2,1)S(1)} %bitcast.34), channel_id=1, source_target_pairs={{0,1},{1,2},{2,3},{3,4},{4,5},{5,6},{6,7},{8,9},{9,10},{10,11},{11... | collective-permute-start | bytes 245768 | tf_op jit(solution)/shard_map/ppermute | solution.py:48
  8.0 1.9 %collective-permute-start.1 = (bf16[64,640]{1,0:T(8,128)(2,1)S(1)}, bf16[64,640]{1,0:T(8,128)(2,1)S(1)}, u32[]{:S(2)}, u32[]{:S(2)}) collective-permute-start(bf16[64,640]{1,0:T(8,128)(2,1)S(1)} %bitcast.33), channel_id=1, source_target_pairs={{1,0},{2,1},{3,2},{4,3},{5,4},{6,5},{7,6},{9,8},{10,9},{11,10},{12... | collective-permute-start | bytes 245768 | tf_op jit(solution)/shard_map/ppermute | solution.py:48
  9.9 0.8 slice.61
  10.7 1.0 slice_bitcast_fusion
  11.7 0.1 copy.14
  11.8 0.1 copy.15
  11.9 0.0 collective-permute-done.low_ref
  11.9 1.8 %collective-permute-done.1.high_ref = bf16[64,640]{1,0:T(8,128)(2,1)S(1)} collective-permute-done((bf16[64,640]{1,0:T(8,128)(2,1)S(1)}, bf16[64,640]{1,0:T(8,128)(2,1)S(1)}, u32[]{:S(2)}, u32[]{:S(2)}) %collective-permute-start.1) | collective-permute-done | bytes 81952 | tf_op jit(solution)/shard_map/ppermute | solution.py:48
  13.8 0.7 broadcast_in_dim.8
  14.4 13.7 %all-to-all-start = ((bf16[16,8,640]{2,1,0:T(8,128)(2,1)}), bf16[16,8,640]{2,1,0:T(8,128)(2,1)S(1)}, u32[]{:S(2)}, u32[]{:S(2)}) async-start(bf16[16,8,640]{2,1,0:T(8,128)(2,1)} %broadcast_in_dim.8), calls=%async_computation | async-start | bytes 327680 | tf_op jit(solution)/shard_map/all_to_all | solution.py:37
  28.2 0.0 copy-done.4
  28.2 0.0 copy-done.5
  28.2 0.1 reshape.75
  28.4 0.1 reshape.76
  28.5 0.1 copy.22
  28.6 0.2 copy.23
  28.8 0.1 fusion.4.aux_ref
  29.0 0.0 copy-done
  29.0 0.0 copy-done.3
  29.0 0.1 shard_map.94
  29.1 3.2 %collective-permute-start.2 = (bf16[48,640]{1,0:T(8,128)(2,1)S(1)}, bf16[48,640]{1,0:T(8,128)(2,1)S(1)}, u32[]{:S(2)}, u32[]{:S(2)}) collective-permute-start(bf16[48,640]{1,0:T(8,128)(2,1)S(1)} %get-tuple-element.28), channel_id=1, source_target_pairs={{0,8},{8,16},{16,24},{24,32},{32,40},{40,48},{48,56},{56,64},{64,7... | collective-permute-start | bytes 184328 | tf_op jit(solution)/shard_map/ppermute | solution.py:48
  32.3 4.2 %collective-permute-start.3 = (bf16[48,640]{1,0:T(8,128)(2,1)S(1)}, bf16[48,640]{1,0:T(8,128)(2,1)S(1)}, u32[]{:S(2)}, u32[]{:S(2)}) collective-permute-start(bf16[48,640]{1,0:T(8,128)(2,1)S(1)} %get-tuple-element.29), channel_id=1, source_target_pairs={{8,0},{16,8},{24,16},{32,24},{40,32},{48,40},{56,48},{64,56},{72,6... | collective-permute-start | bytes 184328 | tf_op jit(solution)/shard_map/ppermute | solution.py:48
  36.5 0.1 pad_add_fusion.half_ref
  36.6 1.5 %collective-permute-done.2.left_ref = bf16[48,640]{1,0:T(8,128)(2,1)S(1)} collective-permute-done((bf16[48,640]{1,0:T(8,128)(2,1)S(1)}, bf16[48,640]{1,0:T(8,128)(2,1)S(1)}, u32[]{:S(2)}, u32[]{:S(2)}) %collective-permute-start.2) | collective-permute-done | bytes 61472 | tf_op jit(solution)/shard_map/ppermute | solution.py:48
  38.1 0.0 collective-permute-done.3.right_ref
  38.1 1.7 %shard_map.95 = (bf16[4,624,640]{2,1,0:T(8,128)(2,1)S(1)}, bf16[512,256]{1,0:T(8,128)(2,1)S(1)}, f32[624,256]{1,0:T(8,128)S(1)}, f32[624,128]{1,0:T(8,128)S(1)}) custom-call(bf16[16,32,256]{2,1,0:T(8,128)(2,1)S(1)} %copy-done.3, f32[16,32,256]{2,1,0:T(8,128)S(1)} %copy-done, bf16[16,32,128]{2,1,0:T(8,128)(2,1)S(1)} %fusion.4.aux_ref, ...), custom_call_target="tpu_custom_call" | custom-call | bytes 100000 | tf_op jit(solution)/shard_map/pallas_call | solution.py:170
  39.8 0.0 copy-start.1
  39.8 1.6 %copy-done.1 = bf16[4,624,640]{2,1,0:T(8,128)(2,1)} copy-done((bf16[4,624,640]{2,1,0:T(8,128)(2,1)}, bf16[4,624,640]{2,1,0:T(8,128)(2,1)S(1)}, u32[]{:S(2)}) %copy-start.1) | copy-done | bytes 3194904
  41.5 0.0 all-to-all-done
  41.5 0.0 copy-done.6
  41.5 0.3 broadcast_in_dim.11
  41.8 0.0 copy-start.2
  41.8 43.7 %all_to_all.10.refs_1_.own_ref = bf16[16,128,640]{2,1,0:T(8,128)(2,1)S(1)} all-to-all(bf16[16,128,640]{2,1,0:T(8,128)(2,1)S(1)} %broadcast_in_dim.11), channel_id=1, replica_groups=mesh['z'=16,'y'=4,'x'=4,'c'=2] {'y','x'}, dimensions={0} | all-to-all | bytes 5242880 | tf_op jit(solution)/shard_map/all_to_all | solution.py:37
  85.5 3.9 %collective-permute-start.4 = (bf16[16,128,640]{2,1,0:T(8,128)(2,1)S(1)}, bf16[16,128,640]{2,1,0:T(8,128)(2,1)S(1)}, u32[]{:S(2)}, u32[]{:S(2)}) collective-permute-start(bf16[16,128,640]{2,1,0:T(8,128)(2,1)S(1)} %all_to_all.10.refs_1_.own_ref), channel_id=1, source_target_pairs={{0,1},{1,0},{2,3},{3,2},{4,5},{5,4},{6,7},{7,6},{8,9},{9,8},{10,11... | collective-permute-start | bytes 7864328 | tf_op jit(solution)/shard_map/ppermute | solution.py:42
  89.4 0.0 copy-done.2
  89.4 3.0 %shard_map.96 = (bf16[624,128]{1,0:T(8,128)(2,1)S(1)}, f32[624,128]{1,0:T(8,128)S(1)}) custom-call(s32[2]{0:T(128)S(1)} %pad_add_fusion.half_ref, bf16[4,624,640]{2,1,0:T(8,128)(2,1)S(1)} %copy-done.2, bf16[16,128,640]{2,1,0:T(8,128)(2,1)S(1)} %all_to_all.10.refs_1_.own_ref, f32[2,4,128]{2,1,0:T(4,128)S(1)} %reverse_select_fusion.refs_2_.bias_ref, ...), custom_call_target="tpu_custom_call" | custom-call | flops 1635778560 | bytes 6000000 | tf_op jit(solution)/shard_map/pallas_call | solution.py:256
  92.4 1.5 %collective-permute-done.4.other_ref = bf16[16,128,640]{2,1,0:T(8,128)(2,1)S(1)} collective-permute-done((bf16[16,128,640]{2,1,0:T(8,128)(2,1)S(1)}, bf16[16,128,640]{2,1,0:T(8,128)(2,1)S(1)}, u32[]{:S(2)}, u32[]{:S(2)}) %collective-permute-start.4) | collective-permute-done | bytes 2621472 | tf_op jit(solution)/shard_map/ppermute | solution.py:42
  93.9 9.0 %shard_map.97 = (bf16[512,256]{1,0:T(8,128)(2,1)}, f32[512,256]{1,0:T(8,128)}, f32[16,32]{1,0:T(8,128)}) custom-call(s32[2]{0:T(128)S(1)} %pad_add_fusion.half_ref, bf16[4,624,640]{2,1,0:T(8,128)(2,1)S(1)} %copy-done.2, bf16[16,128,640]{2,1,0:T(8,128)(2,1)S(1)} %all_to_all.10.refs_1_.own_ref, bf16[16,128,640]{2,1,0:T(8,128)(2,1)S(1)} %collective-permute-done.4.other_ref, ...), custom_call_target="tpu_custom_call" | custom-call | flops 4320133120 | bytes 14000000 | tf_op jit(solution)/shard_map/pallas_call | solution.py:326
  (13 shorter events, 0.2 us)
Async XLA Ops:
  0.6 27.6 %copy-start.4 = (bf16[2,16,32,8]{2,3,1,0:T(8,128)(2,1)S(1)}, bf16[2,16,32,8]{2,3,1,0:T(8,128)(2,1)}, u32[]{:S(2)}) copy-start(bf16[2,16,32,8]{2,3,1,0:T(8,128)(2,1)} %param.7) | copy-start | bytes 49156
  0.6 28.3 %copy-start = (f32[16,32,256]{2,1,0:T(8,128)S(1)}, f32[16,32,256]{2,1,0:T(8,128)}, u32[]{:S(2)}) copy-start(f32[16,32,256]{2,1,0:T(8,128)} %cell_ref.3) | copy-start | bytes 1572868
  0.7 28.3 %copy-start.3 = (bf16[16,32,256]{2,1,0:T(8,128)(2,1)S(1)}, bf16[16,32,256]{2,1,0:T(8,128)(2,1)}, u32[]{:S(2)}) copy-start(bf16[16,32,256]{2,1,0:T(8,128)(2,1)} %hidden_ref.3) | copy-start | bytes 786436
  0.7 27.5 %copy-start.5 = (f32[1024]{0:T(1024)S(1)}, f32[1024]{0:T(1024)}, u32[]{:S(2)}) copy-start(f32[1024]{0:T(1024)} %param.11) | copy-start | bytes 12292
  4.2 37.2 %copy-start.6 = (bf16[256]{0:T(256)(128)(2,1)S(1)}, bf16[256]{0:T(256)(128)(2,1)}, u32[]{:S(2)}) copy-start(bf16[256]{0:T(256)(128)(2,1)} %param.13) | copy-start | bytes 1540
  4.3 7.6 %collective-permute-start = (bf16[64,640]{1,0:T(8,128)(2,1)S(1)}, bf16[64,640]{1,0:T(8,128)(2,1)S(1)}, u32[]{:S(2)}, u32[]{:S(2)}) collective-permute-start(bf16[64,640]{1,0:T(8,128)(2,1)S(1)} %bitcast.34), channel_id=1, source_target_pairs={{0,1},{1,2},{2,3},{3,4},{4,5},{5,6},{6,7},{8,9},{9,10},{10,11},{11... | collective-permute-start | bytes 245768 | tf_op jit(solution)/shard_map/ppermute | solution.py:48
  8.0 5.8 %collective-permute-start.1 = (bf16[64,640]{1,0:T(8,128)(2,1)S(1)}, bf16[64,640]{1,0:T(8,128)(2,1)S(1)}, u32[]{:S(2)}, u32[]{:S(2)}) collective-permute-start(bf16[64,640]{1,0:T(8,128)(2,1)S(1)} %bitcast.33), channel_id=1, source_target_pairs={{1,0},{2,1},{3,2},{4,3},{5,4},{6,5},{7,6},{9,8},{10,9},{11,10},{12... | collective-permute-start | bytes 245768 | tf_op jit(solution)/shard_map/ppermute | solution.py:48
  14.4 27.0 %all-to-all-start = ((bf16[16,8,640]{2,1,0:T(8,128)(2,1)}), bf16[16,8,640]{2,1,0:T(8,128)(2,1)S(1)}, u32[]{:S(2)}, u32[]{:S(2)}) async-start(bf16[16,8,640]{2,1,0:T(8,128)(2,1)} %broadcast_in_dim.8), calls=%async_computation | async-start | bytes 327680 | tf_op jit(solution)/shard_map/all_to_all | solution.py:37
  29.1 9.0 %collective-permute-start.2 = (bf16[48,640]{1,0:T(8,128)(2,1)S(1)}, bf16[48,640]{1,0:T(8,128)(2,1)S(1)}, u32[]{:S(2)}, u32[]{:S(2)}) collective-permute-start(bf16[48,640]{1,0:T(8,128)(2,1)S(1)} %get-tuple-element.28), channel_id=1, source_target_pairs={{0,8},{8,16},{16,24},{24,32},{32,40},{40,48},{48,56},{56,64},{64,7... | collective-permute-start | bytes 184328 | tf_op jit(solution)/shard_map/ppermute | solution.py:48
  32.3 5.8 %collective-permute-start.3 = (bf16[48,640]{1,0:T(8,128)(2,1)S(1)}, bf16[48,640]{1,0:T(8,128)(2,1)S(1)}, u32[]{:S(2)}, u32[]{:S(2)}) collective-permute-start(bf16[48,640]{1,0:T(8,128)(2,1)S(1)} %get-tuple-element.29), channel_id=1, source_target_pairs={{8,0},{16,8},{24,16},{32,24},{40,32},{48,40},{56,48},{64,56},{72,6... | collective-permute-start | bytes 184328 | tf_op jit(solution)/shard_map/ppermute | solution.py:48
  39.8 1.6 %copy-start.1 = (bf16[4,624,640]{2,1,0:T(8,128)(2,1)}, bf16[4,624,640]{2,1,0:T(8,128)(2,1)S(1)}, u32[]{:S(2)}) copy-start(bf16[4,624,640]{2,1,0:T(8,128)(2,1)S(1)} %get-tuple-element.35.refs_0_.patches_ref) | copy-start | bytes 9584644
  41.8 47.6 %copy-start.2 = (bf16[4,624,640]{2,1,0:T(8,128)(2,1)S(1)}, bf16[4,624,640]{2,1,0:T(8,128)(2,1)}, u32[]{:S(2)}) copy-start(bf16[4,624,640]{2,1,0:T(8,128)(2,1)} %copy-done.1) | copy-start | bytes 9584644
  85.5 8.4 %collective-permute-start.4 = (bf16[16,128,640]{2,1,0:T(8,128)(2,1)S(1)}, bf16[16,128,640]{2,1,0:T(8,128)(2,1)S(1)}, u32[]{:S(2)}, u32[]{:S(2)}) collective-permute-start(bf16[16,128,640]{2,1,0:T(8,128)(2,1)S(1)} %all_to_all.10.refs_1_.own_ref), channel_id=1, source_target_pairs={{0,1},{1,0},{2,3},{3,2},{4,5},{5,4},{6,7},{7,6},{8,9},{9,8},{10,11... | collective-permute-start | bytes 7864328 | tf_op jit(solution)/shard_map/ppermute | solution.py:42

commit v10 on v8

--- a/solution.py
+++ b/solution.py
@@ -102,13 +102,6 @@
     target = lax.broadcasted_iota(jnp.int32, (AUX, AUX), 1)
     hit = (target - source == tap * cx - first) & (source >= first) & (source < first + cx)
     return jnp.where(hit, 1.0, 0.0).astype(BF16)
-
-
-def put(ref, rows, lane, value):
-    for i in range(value.shape[1] // 128):
-        group = lane // 128 + i
-        at = group % 5 * 128
-        ref[group // 5, rows, at : at + 128] = value[:, i * 128 : (i + 1) * 128]
 
 
 def prep_kernel(
@@ -159,8 +152,8 @@
             t = 3 * a + b
             core = cols[a : a + 18].reshape(576, HID + AUX)
             edge = border(b, a)
-            put(patches_out, slice(0, 576), t * HID, core[:, :HID])
-            put(patches_out, slice(576, 624), t * HID, edge[:, :HID])
+            patches_out[:576, t * HID : (t + 1) * HID] = core[:, :HID]
+            patches_out[576:, t * HID : (t + 1) * HID] = edge[:, :HID]
             aux = jnp.concatenate([core[:, HID:], edge[:, HID:]], axis=0)
             first = first + lax.dot_general(aux, placer(t, 0, cx), NN, preferred_element_type=F32)
             second = second + lax.dot_general(
@@ -170,8 +163,8 @@
                 source = lax.broadcasted_iota(jnp.int32, (AUX, AUX), 0)
                 copy = jnp.where(source == 2 * cx, 1.0, 0.0).astype(BF16)
                 keep_out[...] = lax.dot_general(aux, copy, NN, preferred_element_type=F32)
-    put(patches_out, slice(0, 624), 9 * HID, first.astype(BF16))
-    put(patches_out, slice(0, 624), 9 * HID + AUX, jnp.zeros((624, AUX), BF16))
+    patches_out[:, 9 * HID : 9 * HID + AUX] = first.astype(BF16)
+    patches_out[:, 9 * HID + AUX :] = jnp.zeros((624, AUX), BF16)
     frame_out[:, :AUX] = second.astype(BF16)
     frame_out[:, AUX:] = jnp.zeros((512, AUX), BF16)
 
@@ -180,7 +173,7 @@
     return pl.pallas_call(
         functools.partial(prep_kernel, cx),
         out_shape=(
-            jax.ShapeDtypeStruct((4, 624, CHUNK), BF16),
+            jax.ShapeDtypeStruct((624, KPAD), BF16),
             jax.ShapeDtypeStruct((512, HID), BF16),
             jax.ShapeDtypeStruct((624, HID), F32),
             jax.ShapeDtypeStruct((624, 128), F32),
@@ -209,21 +202,15 @@
     return high, middle, (rest - middle.astype(F32)).astype(BF16)
 
 
-def moved(value, choice):
-    dots = [lax.dot_general(p, choice, NN, preferred_element_type=F32) for p in parts_of(value)]
-    return dots[0] + (dots[1] + dots[2])
-
-
-def product(patches, weight_ref, pair, x):
-    rhs = jnp.concatenate(
-        [
-            weight_ref[y * 4 + x, q * 32 : (q + 1) * 32, :]
-            for q in (2 * pair, 2 * pair + 1)
-            for y in range(4)
-        ],
-        axis=0,
-    )
-    return lax.dot_general(patches, rhs, NT, preferred_element_type=F32)
+def moved(values, choices):
+    lhs = jnp.concatenate([part for value in values for part in parts_of(value)], axis=1)
+    rhs = jnp.concatenate([choice for choice in choices for _ in range(3)], axis=0)
+    return lax.dot_general(lhs, rhs, NN, preferred_element_type=F32)
+
+
+def joined(values, choices):
+    lhs, rhs = jnp.concatenate(values, axis=1), jnp.concatenate(choices, axis=0)
+    return lax.dot_general(lhs, rhs, NN, preferred_element_type=F32)
 
 
 def sigmoid(value):
@@ -239,20 +226,30 @@
     return (keep * out_gate * jnp.tanh(cell)).astype(BF16), cell
 
 
-def gate_sums(patches_ref, weight_ref):
+def gate_sums(patches, weight_ref):
     sums = []
     for pair in range(2):
-        value = None
-        for x in range(4):
-            part = product(patches_ref[x], weight_ref, pair, x)
-            value = part if value is None else value + part
-        sums.append(value)
+        rhs = jnp.concatenate(
+            [
+                jnp.concatenate(
+                    [
+                        weight_ref[y * 4 + x, q * 32 : (q + 1) * 32, :]
+                        for q in (2 * pair, 2 * pair + 1)
+                        for y in range(4)
+                    ],
+                    axis=0,
+                )
+                for x in range(4)
+            ],
+            axis=1,
+        )
+        sums.append(lax.dot_general(patches, rhs, NT, preferred_element_type=F32))
     return sums
 
 
 def first_half(i, half, patches_ref, weight_ref, bias_ref, cell_ref, keep_ref):
-    sums = gate_sums(patches_ref, weight_ref)
-    cell = moved(cell_ref[...], chooser(half, (HID, 128), 0))
+    sums = gate_sums(patches_ref[...], weight_ref)
+    cell = moved([cell_ref[...]], [chooser(half, (HID, 128), 0)])
     return updated(sums, bias_ref[i], cell, keep_ref[...])
 
 
@@ -262,7 +259,7 @@
 
 
 def own_half(halves, patches, weight, bias, cell, keep):
-    count = patches.shape[1]
+    count = patches.shape[0]
     return pl.pallas_call(
         own_kernel,
         out_shape=(
@@ -302,9 +299,7 @@
         1, half_ref[1], patches_ref, other_ref, bias_ref, cell_ref, keep_ref
     )
     cells = (cell0_ref[32:544, :], cell[32:544])
-    natural = lax.dot_general(
-        hid0_ref[...], choices[0], NN, preferred_element_type=F32
-    ) + lax.dot_general(hid, choices[1], NN, preferred_element_type=F32)
+    natural = joined([hid0_ref[...], hid], choices)
 
     wide[:, 8:40, :] = natural[:576].reshape(18, 32, HID)
     for row in range(18):
@@ -313,18 +308,18 @@
     for b in range(3):
         moved_rows = wide[:, 7 + b : 39 + b, :].astype(BF16)
         for a in range(3):
-            put(patches, slice(0, 512), (3 * a + b) * HID, moved_rows[a : a + 16].reshape(512, HID))
-    put(patches, slice(0, 512), 9 * HID, frame_ref[...])
-
-    hid, cell = None, None
+            t = 3 * a + b
+            patches[:, t * HID : (t + 1) * HID] = moved_rows[a : a + 16].reshape(512, HID)
+    patches[:, 9 * HID :] = frame_ref[...]
+
+    new_hids, new_cells = [], []
     for i, weight_ref in enumerate((own_ref, other_ref)):
-        sums = gate_sums(patches, weight_ref)
+        sums = gate_sums(patches[...], weight_ref)
         new_hid, new_cell = updated(sums, bias_ref[i], cells[i], keep_ref[32:544, :])
-        one = lax.dot_general(new_hid, choices[i], NN, preferred_element_type=F32)
-        two = moved(new_cell, choices[i])
-        hid = one if hid is None else hid + one
-        cell = two if cell is None else cell + two
-    hid = hid.astype(BF16)
+        new_hids.append(new_hid)
+        new_cells.append(new_cell)
+    hid = joined(new_hids, choices).astype(BF16)
+    cell = moved(new_cells, choices)
     hid_out[...] = hid
     cell_out[...] = cell
     flux = lax.dot_general(proj_ref[...], hid, NT, preferred_element_type=F32)
@@ -342,7 +337,7 @@
         ),
         in_specs=[SMEM] + [VMEM] * len(arrays),
         out_specs=(VMEM, VMEM, VMEM),
-        scratch_shapes=[pltpu.VMEM((18, 48, HID), F32), pltpu.VMEM((4, 512, CHUNK), BF16)],
+        scratch_shapes=[pltpu.VMEM((18, 48, HID), F32), pltpu.VMEM((512, KPAD), BF16)],
         compiler_params=PARAMS,
         cost_estimate=pl.CostEstimate(
             flops=2 * 824 * KPAD * 1024, bytes_accessed=14_000_000, transcendentals=1136 * 1280
@@ -394,9 +389,9 @@
     )
 
     own = spread(by_z, ("y", "x"))
-    own, last, first = lax.optimization_barrier((own, last, first))
     left = shifted(last, ("z", "y"), 1)
     right = shifted(first, ("z", "y"), -1)
+    own, left, right = lax.optimization_barrier((own, left, right))
     prep = prepared(cx, *state, low, high, left, right)
     swapped = lambda piece: turned(piece, "c", 1)
     return compute(halves, own, swapped, prep, land_mask, bias2, proj)

time: 102 us -> 101 us (level)
  the two profiles are of different devices: /device:TPU:120 before, /device:TPU:129 now
where the time goes in v10:
time: 101 us
  starting transfers between devices  36.8 us (36%)
  waiting for transfers between devices  35.7 us (35%)
  local copies, waits for them, and re-layouts  14.5 us (14%)
  Pallas kernels  11.7 us (12%)
  other arithmetic  1.02 us (1%)
    ppermute x4, waiting for transfers between devices, shifted(): return lax.ppermute(block, axes, pairs)  27.4 us
    all_to_all x2, starting transfers between devices, spread(): return lax.all_to_all(copies, axes, 0, 0)  19.7 us
    ppermute x4, starting transfers between devices, shifted(): return lax.ppermute(block, axes, pairs)  14.8 us
    unnamed x36, local copies, waits for them, and re-layouts  9.78 us
    all_to_all x2, waiting for transfers between devices, spread(): return lax.all_to_all(copies, axes, 0, 0)  8.27 us
    pallas_call x1, Pallas kernels, finished(): pl.pallas_call(final_kernel, out_shape=(jax.ShapeDtypeStruct((512, HID),...  7.39 us
    pallas_call x1, Pallas kernels, own_half(): pl.pallas_call(own_kernel, out_shape=(jax.ShapeDtypeStruct((count, 128),...  2.66 us
    broadcast_in_dim x2, local copies, waits for them, and re-layouts, spread(): copies = jnp.broadcast_to(block[None], (count,) + block.shape)  2.5 us
  transfers between devices with their start and end apart: 7, of which 4 were waited for; matrix products, arithmetic and copies ran while one was open for 2% of the time, Pallas kernels for 4%

profile of v10, /device:TPU:129, one launch (start us, length us, event | category | flops | bytes accessed | tf_op | source)
XLA Modules:
  0.0 100.6 jit_solution(8462567780344403439)
XLA Ops:
  0.6 0.0 copy-start.1
  0.6 0.0 copy-start.3
  0.7 0.8 slice.9
  1.5 1.0 slice_bitcast_fusion
  2.5 0.1 copy.12
  2.6 0.1 copy.13
  2.7 0.7 broadcast_in_dim.8
  3.4 13.3 %all-to-all-start = ((bf16[16,8,640]{2,1,0:T(8,128)(2,1)}), bf16[16,8,640]{2,1,0:T(8,128)(2,1)S(1)}, u32[]{:S(2)}, u32[]{:S(2)}) async-start(bf16[16,8,640]{2,1,0:T(8,128)(2,1)} %broadcast_in_dim.8), calls=%async_computation | async-start | bytes 327680 | tf_op jit(solution)/shard_map/all_to_all | solution.py:37
  16.7 0.9 copy.20
  17.6 0.1 copy.15
  17.7 0.8 fusion.6
  18.5 0.2 copy.16
  18.7 0.1 fusion.2.aux_ref
  18.8 0.0 copy-start
  18.8 1.0 %copy-done = f32[16,32,256]{2,1,0:T(8,128)S(1)} copy-done((f32[16,32,256]{2,1,0:T(8,128)S(1)}, f32[16,32,256]{2,1,0:T(8,128)}, u32[]{:S(2)}) %copy-start) | copy-done | bytes 524312
  19.8 0.9 copy-done.2
  20.8 4.2 %collective-permute-start = (bf16[64,640]{1,0:T(8,128)(2,1)S(1)}, bf16[64,640]{1,0:T(8,128)(2,1)S(1)}, u32[]{:S(2)}, u32[]{:S(2)}) collective-permute-start(bf16[64,640]{1,0:T(8,128)(2,1)S(1)} %get-tuple-element.25), channel_id=1, source_target_pairs={{0,1},{1,2},{2,3},{3,4},{4,5},{5,6},{6,7},{8,9},{9,10},{10,11},{11... | collective-permute-start | bytes 245768 | tf_op jit(solution)/shard_map/ppermute | solution.py:48
  25.1 1.9 %collective-permute-start.1 = (bf16[64,640]{1,0:T(8,128)(2,1)S(1)}, bf16[64,640]{1,0:T(8,128)(2,1)S(1)}, u32[]{:S(2)}, u32[]{:S(2)}) collective-permute-start(bf16[64,640]{1,0:T(8,128)(2,1)S(1)} %get-tuple-element.26), channel_id=1, source_target_pairs={{1,0},{2,1},{3,2},{4,3},{5,4},{6,5},{7,6},{9,8},{10,9},{11,10},{12... | collective-permute-start | bytes 245768 | tf_op jit(solution)/shard_map/ppermute | solution.py:48
  27.0 0.1 reshape.37
  27.2 0.1 reshape.38
  27.3 0.1 pad_add_fusion.half_ref
  27.4 0.0 collective-permute-done.low_ref
  27.4 3.4 %collective-permute-done.1.high_ref = bf16[64,640]{1,0:T(8,128)(2,1)S(1)} collective-permute-done((bf16[64,640]{1,0:T(8,128)(2,1)S(1)}, bf16[64,640]{1,0:T(8,128)(2,1)S(1)}, u32[]{:S(2)}, u32[]{:S(2)}) %collective-permute-start.1) | collective-permute-done | bytes 81952 | tf_op jit(solution)/shard_map/ppermute | solution.py:48
  30.8 0.1 shard_map.95
  30.9 0.6 copy-done.13
  31.5 0.6 copy-done.14
  32.2 0.0 all-to-all-done
  32.2 0.6 broadcast_in_dim.10.proj_ref
  32.8 1.8 %broadcast_in_dim.11 = bf16[16,128,640]{2,1,0:T(8,128)(2,1)} broadcast(bf16[128,640]{1,0:T(8,128)(2,1)S(1)} %bitcast.18), dimensions={1,2} | broadcast | bytes 2785280 | tf_op jit(solution)/shard_map/broadcast_in_dim | solution.py:36
  34.6 6.5 %all-to-all-start.1 = ((bf16[16,128,640]{2,1,0:T(8,128)(2,1)}), bf16[16,128,640]{2,1,0:T(8,128)(2,1)S(1)}, u32[]{:S(2)}, u32[]{:S(2)}) async-start(bf16[16,128,640]{2,1,0:T(8,128)(2,1)} %broadcast_in_dim.11), calls=%async_computation.1 | async-start | bytes 5242880 | tf_op jit(solution)/shard_map/all_to_all | solution.py:37
  41.1 3.3 %collective-permute-start.2 = (bf16[48,640]{1,0:T(8,128)(2,1)}, bf16[48,640]{1,0:T(8,128)(2,1)S(1)}, u32[]{:S(2)}, u32[]{:S(2)}) collective-permute-start(bf16[48,640]{1,0:T(8,128)(2,1)} %copy-done.14), channel_id=1, source_target_pairs={{0,8},{8,16},{16,24},{24,32},{32,40},{40,48},{48,56},{56,64},{64,7... | collective-permute-start | bytes 184328 | tf_op jit(solution)/shard_map/ppermute | solution.py:48
  44.3 5.3 %collective-permute-start.3 = (bf16[48,640]{1,0:T(8,128)(2,1)}, bf16[48,640]{1,0:T(8,128)(2,1)S(1)}, u32[]{:S(2)}, u32[]{:S(2)}) collective-permute-start(bf16[48,640]{1,0:T(8,128)(2,1)} %copy-done.13), channel_id=1, source_target_pairs={{8,0},{16,8},{24,16},{32,24},{40,32},{48,40},{56,48},{64,56},{72,6... | collective-permute-start | bytes 184328 | tf_op jit(solution)/shard_map/ppermute | solution.py:48
  49.7 11.8 %collective-permute-done.2.left_ref = bf16[48,640]{1,0:T(8,128)(2,1)S(1)} collective-permute-done((bf16[48,640]{1,0:T(8,128)(2,1)}, bf16[48,640]{1,0:T(8,128)(2,1)S(1)}, u32[]{:S(2)}, u32[]{:S(2)}) %collective-permute-start.2) | collective-permute-done | bytes 61472 | tf_op jit(solution)/shard_map/ppermute | solution.py:48
  61.5 0.6 copy-done.8
  62.1 12.2 %collective-permute-done.3.right_ref = bf16[48,640]{1,0:T(8,128)(2,1)S(1)} collective-permute-done((bf16[48,640]{1,0:T(8,128)(2,1)}, bf16[48,640]{1,0:T(8,128)(2,1)S(1)}, u32[]{:S(2)}, u32[]{:S(2)}) %collective-permute-start.3) | collective-permute-done | bytes 61472 | tf_op jit(solution)/shard_map/ppermute | solution.py:48
  74.3 0.6 copy-done.10
  74.9 8.3 %all-to-all-done.1.refs_1_.own_ref = bf16[16,128,640]{2,1,0:T(8,128)(2,1)S(1)} async-done(((bf16[16,128,640]{2,1,0:T(8,128)(2,1)}), bf16[16,128,640]{2,1,0:T(8,128)(2,1)S(1)}, u32[]{:S(2)}, u32[]{:S(2)}) %all-to-all-start.1) | async-done | bytes 2621472 | tf_op jit(solution)/shard_map/all_to_all | solution.py:37
  83.2 2.3 %collective-permute-start.4 = (bf16[16,128,640]{2,1,0:T(8,128)(2,1)S(1)}, bf16[16,128,640]{2,1,0:T(8,128)(2,1)S(1)}, u32[]{:S(2)}, u32[]{:S(2)}) collective-permute-start(bf16[16,128,640]{2,1,0:T(8,128)(2,1)S(1)} %all-to-all-done.1.refs_1_.own_ref), channel_id=1, source_target_pairs={{0,1},{1,0},{2,3},{3,2},{4,5},{5,4},{6,7},{7,6},{8,9},{9,8},{10,11... | collective-permute-start | bytes 7864328 | tf_op jit(solution)/shard_map/ppermute | solution.py:42
  85.5 0.0 copy-start.5
  85.5 0.9 copy-done.5
  86.4 0.9 copy-done.7
  87.3 0.8 copy-done.9
  88.1 0.8 copy-done.11
  88.9 1.5 %shard_map.96 = (bf16[624,2560]{1,0:T(8,128)(2,1)S(1)}, bf16[512,256]{1,0:T(8,128)(2,1)S(1)}, f32[624,256]{1,0:T(8,128)S(1)}, f32[624,128]{1,0:T(8,128)S(1)}) custom-call(bf16[16,32,256]{2,1,0:T(8,128)(2,1)S(1)} %copy-done.3, f32[16,32,256]{2,1,0:T(8,128)S(1)} %copy-done.1, bf16[16,32,128]{2,1,0:T(8,128)(2,1)S(1)} %fusion.2.aux_ref, ...), custom_call_target="tpu_custom_call" | custom-call | bytes 100000 | tf_op jit(solution)/shard_map/pallas_call | solution.py:173
  90.5 0.0 copy-start.12
  90.5 2.7 %shard_map.97 = (bf16[624,128]{1,0:T(8,128)(2,1)S(1)}, f32[624,128]{1,0:T(8,128)S(1)}) custom-call(s32[2]{0:T(128)S(1)} %pad_add_fusion.half_ref, bf16[624,2560]{1,0:T(8,128)(2,1)S(1)} %get-tuple-element.35.refs_0_.patches_ref, bf16[16,128,640]{2,1,0:T(8,128)(2,1)S(1)} %all-to-all-done.1.refs_1_.own_ref, ...), custom_call_target="tpu_custom_call" | custom-call | flops 1635778560 | bytes 6000000 | tf_op jit(solution)/shard_map/pallas_call | solution.py:263
  93.2 0.0 collective-permute-done.4.other_ref
  93.2 7.4 %shard_map.98 = (bf16[512,256]{1,0:T(8,128)(2,1)}, f32[512,256]{1,0:T(8,128)}, f32[16,32]{1,0:T(8,128)}) custom-call(s32[2]{0:T(128)S(1)} %pad_add_fusion.half_ref, bf16[624,2560]{1,0:T(8,128)(2,1)S(1)} %get-tuple-element.35.refs_0_.patches_ref, bf16[16,128,640]{2,1,0:T(8,128)(2,1)S(1)} %all-to-all-done.1.refs_1_.own_ref, ...), custom_call_target="tpu_custom_call" | custom-call | flops 4320133120 | bytes 14000000 | tf_op jit(solution)/shard_map/pallas_call | solution.py:331
  (24 shorter events, 0.1 us)
Async XLA Ops:
  0.6 30.2 %copy-start.1 = (f32[16,32,256]{2,1,0:T(8,128)S(1)}, f32[16,32,256]{2,1,0:T(8,128)}, u32[]{:S(2)}) copy-start(f32[16,32,256]{2,1,0:T(8,128)} %cell_ref.5) | copy-start | bytes 1572868
  0.6 30.2 %copy-start.3 = (bf16[16,32,256]{2,1,0:T(8,128)(2,1)S(1)}, bf16[16,32,256]{2,1,0:T(8,128)(2,1)}, u32[]{:S(2)}) copy-start(bf16[16,32,256]{2,1,0:T(8,128)(2,1)} %hidden_ref.5) | copy-start | bytes 786436
  0.7 26.3 %copy-start.15 = (f32[1024]{0:T(1024)S(1)}, f32[1024]{0:T(1024)}, u32[]{:S(2)}) copy-start(f32[1024]{0:T(1024)} %param.11) | copy-start | bytes 12292
  0.7 31.5 %copy-start.16 = (bf16[256]{0:T(256)(128)(2,1)S(1)}, bf16[256]{0:T(256)(128)(2,1)}, u32[]{:S(2)}) copy-start(bf16[256]{0:T(256)(128)(2,1)} %param.13) | copy-start | bytes 1540
  3.4 28.7 %all-to-all-start = ((bf16[16,8,640]{2,1,0:T(8,128)(2,1)}), bf16[16,8,640]{2,1,0:T(8,128)(2,1)S(1)}, u32[]{:S(2)}, u32[]{:S(2)}) async-start(bf16[16,8,640]{2,1,0:T(8,128)(2,1)} %broadcast_in_dim.8), calls=%async_computation | async-start | bytes 327680 | tf_op jit(solution)/shard_map/all_to_all | solution.py:37
  18.8 1.0 %copy-start = (f32[16,32,256]{2,1,0:T(8,128)S(1)}, f32[16,32,256]{2,1,0:T(8,128)}, u32[]{:S(2)}) copy-start(f32[16,32,256]{2,1,0:T(8,128)} %cell_ref.5) | copy-start | bytes 1572868
  19.8 0.9 copy-start.2
  20.8 6.6 %collective-permute-start = (bf16[64,640]{1,0:T(8,128)(2,1)S(1)}, bf16[64,640]{1,0:T(8,128)(2,1)S(1)}, u32[]{:S(2)}, u32[]{:S(2)}) collective-permute-start(bf16[64,640]{1,0:T(8,128)(2,1)S(1)} %get-tuple-element.25), channel_id=1, source_target_pairs={{0,1},{1,2},{2,3},{3,4},{4,5},{5,6},{6,7},{8,9},{9,10},{10,11},{11... | collective-permute-start | bytes 245768 | tf_op jit(solution)/shard_map/ppermute | solution.py:48
  25.1 5.8 %collective-permute-start.1 = (bf16[64,640]{1,0:T(8,128)(2,1)S(1)}, bf16[64,640]{1,0:T(8,128)(2,1)S(1)}, u32[]{:S(2)}, u32[]{:S(2)}) collective-permute-start(bf16[64,640]{1,0:T(8,128)(2,1)S(1)} %get-tuple-element.26), channel_id=1, source_target_pairs={{1,0},{2,1},{3,2},{4,3},{5,4},{6,5},{7,6},{9,8},{10,9},{11,10},{12... | collective-permute-start | bytes 245768 | tf_op jit(solution)/shard_map/ppermute | solution.py:48
  27.4 7.2 %copy-start.4 = (bf16[64,640]{1,0:T(8,128)(2,1)}, bf16[64,640]{1,0:T(8,128)(2,1)S(1)}, u32[]{:S(2)}) copy-start(bf16[64,640]{1,0:T(8,128)(2,1)S(1)} %collective-permute-done.low_ref) | copy-start | bytes 245764
  30.8 3.8 %copy-start.6 = (bf16[64,640]{1,0:T(8,128)(2,1)}, bf16[64,640]{1,0:T(8,128)(2,1)S(1)}, u32[]{:S(2)}) copy-start(bf16[64,640]{1,0:T(8,128)(2,1)S(1)} %collective-permute-done.1.high_ref) | copy-start | bytes 245764
  30.9 0.6 copy-start.13
  31.5 0.6 copy-start.14
  34.6 48.6 %all-to-all-start.1 = ((bf16[16,128,640]{2,1,0:T(8,128)(2,1)}), bf16[16,128,640]{2,1,0:T(8,128)(2,1)S(1)}, u32[]{:S(2)}, u32[]{:S(2)}) async-start(bf16[16,128,640]{2,1,0:T(8,128)(2,1)} %broadcast_in_dim.11), calls=%async_computation.1 | async-start | bytes 5242880 | tf_op jit(solution)/shard_map/all_to_all | solution.py:37
  41.1 20.5 %collective-permute-start.2 = (bf16[48,640]{1,0:T(8,128)(2,1)}, bf16[48,640]{1,0:T(8,128)(2,1)S(1)}, u32[]{:S(2)}, u32[]{:S(2)}) collective-permute-start(bf16[48,640]{1,0:T(8,128)(2,1)} %copy-done.14), channel_id=1, source_target_pairs={{0,8},{8,16},{16,24},{24,32},{32,40},{40,48},{48,56},{56,64},{64,7... | collective-permute-start | bytes 184328 | tf_op jit(solution)/shard_map/ppermute | solution.py:48
  44.3 30.0 %collective-permute-start.3 = (bf16[48,640]{1,0:T(8,128)(2,1)}, bf16[48,640]{1,0:T(8,128)(2,1)S(1)}, u32[]{:S(2)}, u32[]{:S(2)}) collective-permute-start(bf16[48,640]{1,0:T(8,128)(2,1)} %copy-done.13), channel_id=1, source_target_pairs={{8,0},{16,8},{24,16},{32,24},{40,32},{48,40},{56,48},{64,56},{72,6... | collective-permute-start | bytes 184328 | tf_op jit(solution)/shard_map/ppermute | solution.py:48
  61.5 0.6 copy-start.8
  74.3 0.6 copy-start.10
  83.2 10.0 %collective-permute-start.4 = (bf16[16,128,640]{2,1,0:T(8,128)(2,1)S(1)}, bf16[16,128,640]{2,1,0:T(8,128)(2,1)S(1)}, u32[]{:S(2)}, u32[]{:S(2)}) collective-permute-start(bf16[16,128,640]{2,1,0:T(8,128)(2,1)S(1)} %all-to-all-done.1.refs_1_.own_ref), channel_id=1, source_target_pairs={{0,1},{1,0},{2,3},{3,2},{4,5},{5,4},{6,7},{7,6},{8,9},{9,8},{10,11... | collective-permute-start | bytes 7864328 | tf_op jit(solution)/shard_map/ppermute | solution.py:42
  85.5 0.9 copy-start.5
  86.4 0.9 copy-start.7
  87.3 0.8 copy-start.9
  88.1 0.8 copy-start.11
  90.5 2.7 %copy-start.12 = (bf16[16,256]{1,0:T(8,128)(2,1)S(1)}, bf16[16,256]{1,0:T(8,128)(2,1)}, u32[]{:S(2)}) copy-start(bf16[16,256]{1,0:T(8,128)(2,1)} %broadcast_in_dim.10.proj_ref) | copy-start | bytes 24580

commit v11 on v10

--- a/solution.py
+++ b/solution.py
@@ -389,9 +389,9 @@
     )
 
     own = spread(by_z, ("y", "x"))
+    own, last, first = lax.optimization_barrier((own, last, first))
     left = shifted(last, ("z", "y"), 1)
     right = shifted(first, ("z", "y"), -1)
-    own, left, right = lax.optimization_barrier((own, left, right))
     prep = prepared(cx, *state, low, high, left, right)
     swapped = lambda piece: turned(piece, "c", 1)
     return compute(halves, own, swapped, prep, land_mask, bias2, proj)

time: 101 us -> 100 us (0.990)
  the two profiles are of different devices: /device:TPU:129 before, /device:TPU:120 now
where the time goes in v11:
time: 100 us; the launch traced here: 99.9 us
  blocking collectives  38.2 us (38%)
  starting transfers between devices  27 us (27%)
  waiting for transfers between devices  14.6 us (15%)
  Pallas kernels  11.8 us (12%)
  local copies, waits for them, and re-layouts  6.43 us (6%)
  other arithmetic  1.02 us (1%)
    all_to_all x1, blocking collectives, spread(): return lax.all_to_all(copies, axes, 0, 0)  38.2 us
    all_to_all x1, starting transfers between devices, spread(): return lax.all_to_all(copies, axes, 0, 0)  14.3 us
    ppermute x4, starting transfers between devices, shifted(): return lax.ppermute(block, axes, pairs)  10.8 us
    ppermute x4, waiting for transfers between devices, shifted(): return lax.ppermute(block, axes, pairs)  10.7 us
    pallas_call x1, Pallas kernels, finished(): pl.pallas_call(final_kernel, out_shape=(jax.ShapeDtypeStruct((512, HID),...  7.4 us
    all_to_all x1, waiting for transfers between devices, spread(): return lax.all_to_all(copies, axes, 0, 0)  3.89 us
    unnamed x14, local copies, waits for them, and re-layouts  3.84 us
    pallas_call x1, Pallas kernels, own_half(): pl.pallas_call(own_kernel, out_shape=(jax.ShapeDtypeStruct((count, 128),...  2.71 us
  transfers between devices with their start and end apart: 6, of which 3 were waited for; matrix products, arithmetic and copies ran while one was open for 2% of the time, Pallas kernels for 4%

profile of v11, /device:TPU:120, one launch (start us, length us, event | category | flops | bytes accessed | tf_op | source)
XLA Modules:
  0.0 99.9 jit_solution(13549026888458611853)
XLA Ops:
  0.6 0.0 copy-start.1
  0.6 0.0 copy-start.3
  0.7 0.0 copy-start.4
  0.7 0.0 copy-start.5
  0.7 0.8 slice.9
  1.5 1.0 slice_bitcast_fusion
  2.5 0.1 copy.12
  2.6 0.1 copy.13
  2.7 0.7 broadcast_in_dim.8
  3.4 14.3 %all-to-all-start = ((bf16[16,8,640]{2,1,0:T(8,128)(2,1)}), bf16[16,8,640]{2,1,0:T(8,128)(2,1)S(1)}, u32[]{:S(2)}, u32[]{:S(2)}) async-start(bf16[16,8,640]{2,1,0:T(8,128)(2,1)} %broadcast_in_dim.8), calls=%async_computation | async-start | bytes 327680 | tf_op jit(solution)/shard_map/all_to_all | solution.py:37
  17.7 0.9 copy.20
  18.6 0.1 copy.15
  18.7 0.8 fusion.6
  19.5 0.2 copy.16
  19.7 0.1 fusion.2.aux_ref
  19.8 0.0 copy-start
  19.8 1.0 %copy-done = f32[16,32,256]{2,1,0:T(8,128)S(1)} copy-done((f32[16,32,256]{2,1,0:T(8,128)S(1)}, f32[16,32,256]{2,1,0:T(8,128)}, u32[]{:S(2)}) %copy-start) | copy-done | bytes 524312
  20.9 0.0 copy-start.2
  20.9 0.9 copy-done.2
  21.8 1.3 %collective-permute-start = (bf16[64,640]{1,0:T(8,128)(2,1)S(1)}, bf16[64,640]{1,0:T(8,128)(2,1)S(1)}, u32[]{:S(2)}, u32[]{:S(2)}) collective-permute-start(bf16[64,640]{1,0:T(8,128)(2,1)S(1)} %get-tuple-element.25), channel_id=1, source_target_pairs={{0,1},{1,2},{2,3},{3,4},{4,5},{5,6},{6,7},{8,9},{9,10},{10,11},{11... | collective-permute-start | bytes 245768 | tf_op jit(solution)/shard_map/ppermute | solution.py:48
  23.1 1.3 %collective-permute-start.1 = (bf16[64,640]{1,0:T(8,128)(2,1)S(1)}, bf16[64,640]{1,0:T(8,128)(2,1)S(1)}, u32[]{:S(2)}, u32[]{:S(2)}) collective-permute-start(bf16[64,640]{1,0:T(8,128)(2,1)S(1)} %get-tuple-element.26), channel_id=1, source_target_pairs={{1,0},{2,1},{3,2},{4,3},{5,4},{6,5},{7,6},{9,8},{10,9},{11,10},{12... | collective-permute-start | bytes 245768 | tf_op jit(solution)/shard_map/ppermute | solution.py:48
  24.4 0.0 copy-done.4
  24.4 0.1 reshape.37
  24.6 0.1 reshape.38
  24.7 0.1 pad_add_fusion.half_ref
  24.8 0.0 collective-permute-done.low_ref
  24.8 3.2 %collective-permute-done.1.high_ref = bf16[64,640]{1,0:T(8,128)(2,1)S(1)} collective-permute-done((bf16[64,640]{1,0:T(8,128)(2,1)S(1)}, bf16[64,640]{1,0:T(8,128)(2,1)S(1)}, u32[]{:S(2)}, u32[]{:S(2)}) %collective-permute-start.1) | collective-permute-done | bytes 81952 | tf_op jit(solution)/shard_map/ppermute | solution.py:48
  28.0 0.0 copy-done.1
  28.0 0.0 copy-done.3
  28.0 0.1 shard_map.95
  28.1 3.9 %all-to-all-done = bf16[16,8,640]{2,1,0:T(8,128)(2,1)S(1)} async-done(((bf16[16,8,640]{2,1,0:T(8,128)(2,1)}), bf16[16,8,640]{2,1,0:T(8,128)(2,1)S(1)}, u32[]{:S(2)}, u32[]{:S(2)}) %all-to-all-start) | async-done | bytes 163872 | tf_op jit(solution)/shard_map/all_to_all | solution.py:37
  32.0 0.0 copy-done.5
  32.0 0.3 broadcast_in_dim.11
  32.3 38.2 %all_to_all.10.refs_1_.own_ref = bf16[16,128,640]{2,1,0:T(8,128)(2,1)S(1)} all-to-all(bf16[16,128,640]{2,1,0:T(8,128)(2,1)S(1)} %broadcast_in_dim.11), channel_id=1, replica_groups=mesh['z'=16,'y'=4,'x'=4,'c'=2] {'y','x'}, dimensions={0} | all-to-all | bytes 5242880 | tf_op jit(solution)/shard_map/all_to_all | solution.py:37
  70.6 1.9 %collective-permute-start.4 = (bf16[16,128,640]{2,1,0:T(8,128)(2,1)S(1)}, bf16[16,128,640]{2,1,0:T(8,128)(2,1)S(1)}, u32[]{:S(2)}, u32[]{:S(2)}) collective-permute-start(bf16[16,128,640]{2,1,0:T(8,128)(2,1)S(1)} %all_to_all.10.refs_1_.own_ref), channel_id=1, source_target_pairs={{0,1},{1,0},{2,3},{3,2},{4,5},{5,4},{6,7},{7,6},{8,9},{9,8},{10,11... | collective-permute-start | bytes 7864328 | tf_op jit(solution)/shard_map/ppermute | solution.py:42
  72.5 6.3 %collective-permute-start.2 = (bf16[48,640]{1,0:T(8,128)(2,1)S(1)}, bf16[48,640]{1,0:T(8,128)(2,1)S(1)}, u32[]{:S(2)}, u32[]{:S(2)}) collective-permute-start(bf16[48,640]{1,0:T(8,128)(2,1)S(1)} %get-tuple-element.33), channel_id=1, source_target_pairs={{0,8},{8,16},{16,24},{24,32},{32,40},{40,48},{48,56},{56,64},{64,7... | collective-permute-start | bytes 184328 | tf_op jit(solution)/shard_map/ppermute | solution.py:48
  78.7 1.9 %collective-permute-start.3 = (bf16[48,640]{1,0:T(8,128)(2,1)S(1)}, bf16[48,640]{1,0:T(8,128)(2,1)S(1)}, u32[]{:S(2)}, u32[]{:S(2)}) collective-permute-start(bf16[48,640]{1,0:T(8,128)(2,1)S(1)} %get-tuple-element.34), channel_id=1, source_target_pairs={{8,0},{16,8},{24,16},{32,24},{40,32},{48,40},{56,48},{64,56},{72,6... | collective-permute-start | bytes 184328 | tf_op jit(solution)/shard_map/ppermute | solution.py:48
  80.7 0.0 collective-permute-done.2.left_ref
  80.7 7.5 %collective-permute-done.3.right_ref = bf16[48,640]{1,0:T(8,128)(2,1)S(1)} collective-permute-done((bf16[48,640]{1,0:T(8,128)(2,1)S(1)}, bf16[48,640]{1,0:T(8,128)(2,1)S(1)}, u32[]{:S(2)}, u32[]{:S(2)}) %collective-permute-start.3) | collective-permute-done | bytes 61472 | tf_op jit(solution)/shard_map/ppermute | solution.py:48
  88.2 1.6 %shard_map.96 = (bf16[624,2560]{1,0:T(8,128)(2,1)S(1)}, bf16[512,256]{1,0:T(8,128)(2,1)S(1)}, f32[624,256]{1,0:T(8,128)S(1)}, f32[624,128]{1,0:T(8,128)S(1)}) custom-call(bf16[16,32,256]{2,1,0:T(8,128)(2,1)S(1)} %copy-done.3, f32[16,32,256]{2,1,0:T(8,128)S(1)} %copy-done.1, bf16[16,32,128]{2,1,0:T(8,128)(2,1)S(1)} %fusion.2.aux_ref, ...), custom_call_target="tpu_custom_call" | custom-call | bytes 100000 | tf_op jit(solution)/shard_map/pallas_call | solution.py:173
  89.7 2.7 %shard_map.97 = (bf16[624,128]{1,0:T(8,128)(2,1)S(1)}, f32[624,128]{1,0:T(8,128)S(1)}) custom-call(s32[2]{0:T(128)S(1)} %pad_add_fusion.half_ref, bf16[624,2560]{1,0:T(8,128)(2,1)S(1)} %get-tuple-element.35.refs_0_.patches_ref, bf16[16,128,640]{2,1,0:T(8,128)(2,1)S(1)} %all_to_all.10.refs_1_.own_ref, f32[2,4,128]{2,1,0:T(4,128)S(1)} %reverse_select_fusion.refs_2_.bias_ref, ...), custom_call_target="tpu_custom_call" | custom-call | flops 1635778560 | bytes 6000000 | tf_op jit(solution)/shard_map/pallas_call | solution.py:263
  92.5 0.0 collective-permute-done.4.other_ref
  92.5 7.4 %shard_map.98 = (bf16[512,256]{1,0:T(8,128)(2,1)}, f32[512,256]{1,0:T(8,128)}, f32[16,32]{1,0:T(8,128)}) custom-call(s32[2]{0:T(128)S(1)} %pad_add_fusion.half_ref, bf16[624,2560]{1,0:T(8,128)(2,1)S(1)} %get-tuple-element.35.refs_0_.patches_ref, bf16[16,128,640]{2,1,0:T(8,128)(2,1)S(1)} %all_to_all.10.refs_1_.own_ref, ...), custom_call_target="tpu_custom_call" | custom-call | flops 4320133120 | bytes 14000000 | tf_op jit(solution)/shard_map/pallas_call | solution.py:331
  (6 shorter events, 0.1 us)
Async XLA Ops:
  0.6 27.4 %copy-start.1 = (f32[16,32,256]{2,1,0:T(8,128)S(1)}, f32[16,32,256]{2,1,0:T(8,128)}, u32[]{:S(2)}) copy-start(f32[16,32,256]{2,1,0:T(8,128)} %cell_ref.5) | copy-start | bytes 1572868
  0.6 27.4 %copy-start.3 = (bf16[16,32,256]{2,1,0:T(8,128)(2,1)S(1)}, bf16[16,32,256]{2,1,0:T(8,128)(2,1)}, u32[]{:S(2)}) copy-start(bf16[16,32,256]{2,1,0:T(8,128)(2,1)} %hidden_ref.5) | copy-start | bytes 786436
  0.7 23.8 %copy-start.4 = (f32[1024]{0:T(1024)S(1)}, f32[1024]{0:T(1024)}, u32[]{:S(2)}) copy-start(f32[1024]{0:T(1024)} %param.11) | copy-start | bytes 12292
  0.7 31.3 %copy-start.5 = (bf16[256]{0:T(256)(128)(2,1)S(1)}, bf16[256]{0:T(256)(128)(2,1)}, u32[]{:S(2)}) copy-start(bf16[256]{0:T(256)(128)(2,1)} %param.13) | copy-start | bytes 1540
  3.4 28.6 %all-to-all-start = ((bf16[16,8,640]{2,1,0:T(8,128)(2,1)}), bf16[16,8,640]{2,1,0:T(8,128)(2,1)S(1)}, u32[]{:S(2)}, u32[]{:S(2)}) async-start(bf16[16,8,640]{2,1,0:T(8,128)(2,1)} %broadcast_in_dim.8), calls=%async_computation | async-start | bytes 327680 | tf_op jit(solution)/shard_map/all_to_all | solution.py:37
  19.8 1.0 %copy-start = (f32[16,32,256]{2,1,0:T(8,128)S(1)}, f32[16,32,256]{2,1,0:T(8,128)}, u32[]{:S(2)}) copy-start(f32[16,32,256]{2,1,0:T(8,128)} %cell_ref.5) | copy-start | bytes 1572868
  20.9 0.9 copy-start.2
  21.8 3.0 %collective-permute-start = (bf16[64,640]{1,0:T(8,128)(2,1)S(1)}, bf16[64,640]{1,0:T(8,128)(2,1)S(1)}, u32[]{:S(2)}, u32[]{:S(2)}) collective-permute-start(bf16[64,640]{1,0:T(8,128)(2,1)S(1)} %get-tuple-element.25), channel_id=1, source_target_pairs={{0,1},{1,2},{2,3},{3,4},{4,5},{5,6},{6,7},{8,9},{9,10},{10,11},{11... | collective-permute-start | bytes 245768 | tf_op jit(solution)/shard_map/ppermute | solution.py:48
  23.1 4.9 %collective-permute-start.1 = (bf16[64,640]{1,0:T(8,128)(2,1)S(1)}, bf16[64,640]{1,0:T(8,128)(2,1)S(1)}, u32[]{:S(2)}, u32[]{:S(2)}) collective-permute-start(bf16[64,640]{1,0:T(8,128)(2,1)S(1)} %get-tuple-element.26), channel_id=1, source_target_pairs={{1,0},{2,1},{3,2},{4,3},{5,4},{6,5},{7,6},{9,8},{10,9},{11,10},{12... | collective-permute-start | bytes 245768 | tf_op jit(solution)/shard_map/ppermute | solution.py:48
  70.6 21.9 %collective-permute-start.4 = (bf16[16,128,640]{2,1,0:T(8,128)(2,1)S(1)}, bf16[16,128,640]{2,1,0:T(8,128)(2,1)S(1)}, u32[]{:S(2)}, u32[]{:S(2)}) collective-permute-start(bf16[16,128,640]{2,1,0:T(8,128)(2,1)S(1)} %all_to_all.10.refs_1_.own_ref), channel_id=1, source_target_pairs={{0,1},{1,0},{2,3},{3,2},{4,5},{5,4},{6,7},{7,6},{8,9},{9,8},{10,11... | collective-permute-start | bytes 7864328 | tf_op jit(solution)/shard_map/ppermute | solution.py:42
  72.5 8.2 %collective-permute-start.2 = (bf16[48,640]{1,0:T(8,128)(2,1)S(1)}, bf16[48,640]{1,0:T(8,128)(2,1)S(1)}, u32[]{:S(2)}, u32[]{:S(2)}) collective-permute-start(bf16[48,640]{1,0:T(8,128)(2,1)S(1)} %get-tuple-element.33), channel_id=1, source_target_pairs={{0,8},{8,16},{16,24},{24,32},{32,40},{40,48},{48,56},{56,64},{64,7... | collective-permute-start | bytes 184328 | tf_op jit(solution)/shard_map/ppermute | solution.py:48
  78.7 9.4 %collective-permute-start.3 = (bf16[48,640]{1,0:T(8,128)(2,1)S(1)}, bf16[48,640]{1,0:T(8,128)(2,1)S(1)}, u32[]{:S(2)}, u32[]{:S(2)}) collective-permute-start(bf16[48,640]{1,0:T(8,128)(2,1)S(1)} %get-tuple-element.34), channel_id=1, source_target_pairs={{8,0},{16,8},{24,16},{32,24},{40,32},{48,40},{56,48},{64,56},{72,6... | collective-permute-start | bytes 184328 | tf_op jit(solution)/shard_map/ppermute | solution.py:48

commit v12 on v11

--- a/solution.py
+++ b/solution.py
@@ -21,14 +21,33 @@
 PARAMS = pltpu.CompilerParams(vmem_limit_bytes=16 * 1024 * 1024)
 
 
-def pack_weights(conv_weight):
-    taps, cin, cols = conv_weight.shape
-    cx = cin - HID
-    flipped = jnp.transpose(conv_weight, (2, 0, 1))
-    hidden = flipped[:, :, cx:].reshape(cols, taps * HID)
-    frame = flipped[:, :, :cx].reshape(cols, taps * cx)
-    packed = jnp.concatenate([hidden, frame], axis=1)
-    return jnp.pad(packed, ((0, 0), (0, KPAD - packed.shape[1])))
+def pack_kernel(place_ref, weight_ref, out, whole):
+    cx = weight_ref.shape[2] - HID
+    frame = jnp.zeros((16, AUX), F32)
+    for t in range(9):
+        block = weight_ref[t]
+        whole[:, t * HID : (t + 1) * HID] = block.astype(F32)[:, cx:]
+        frame = frame + lax.dot_general(
+            block[:, :AUX], placer(t, 0, cx), NN, preferred_element_type=F32
+        )
+    whole[:, 9 * HID : 9 * HID + AUX] = frame
+    whole[:, 9 * HID + AUX :] = jnp.zeros((16, AUX), F32)
+    row = pl.multiple_of(place_ref[0] * 8, 8)
+    lane = pl.multiple_of(place_ref[1] * CHUNK, 128)
+    unit = whole[pl.ds(row, 8), pl.ds(lane, CHUNK)]
+    out[...] = jnp.concatenate([unit] * 16, axis=0).astype(BF16)
+
+
+def packed_unit(place, conv_weight):
+    return pl.pallas_call(
+        pack_kernel,
+        out_shape=jax.ShapeDtypeStruct((128, CHUNK), BF16),
+        in_specs=[SMEM, VMEM],
+        out_specs=VMEM,
+        scratch_shapes=[pltpu.VMEM((16, KPAD), F32)],
+        compiler_params=PARAMS,
+        cost_estimate=pl.CostEstimate(flops=0, bytes_accessed=300_000, transcendentals=0),
+    )(place, jnp.transpose(conv_weight, (0, 2, 1)))
 
 
 def spread(block, axes):
@@ -372,9 +391,8 @@
 def body(frames, hidden_init, cell_init, conv_weight, bias, land_mask, projection):
     cx = frames.shape[3]
     x, c = lax.axis_index("x"), lax.axis_index("c")
-    packed = pack_weights(conv_weight)
-    unit = lax.dynamic_slice(packed, (c * 8, x * (KPAD // 4)), (8, KPAD // 4))
-    by_z = spread(unit, "z").reshape(128, KPAD // 4)
+    copies = packed_unit(jnp.stack([c, x]).astype(jnp.int32), conv_weight)
+    by_z = lax.all_to_all(copies.reshape(16, 8, CHUNK), "z", 0, 0).reshape(128, CHUNK)
 
     state = (hidden_init, cell_init, aux_of(frames, land_mask))
     last, first = ends_of(*state)

time: 100 us -> 100 us (level)
  Pallas kernels: 11.8 us -> 13.1 us
  local copies, waits for them, and re-layouts: 6.43 us -> 5.4 us
    pallas_call x0 -> x1, Pallas kernels: none -> 1.38 us  [packed_unit(): pl.pallas_call(pack_kernel, out_shape=jax.ShapeDtypeStruct((128, CHUNK),...]
    unnamed x14 -> x13, local copies, waits for them, and re-layouts: 3.84 us -> 3.8 us
  transfers between devices with their start and end apart: 6 -> 6, of which waited for: 3 -> 3; matrix products, arithmetic and copies ran while one was open for 2% -> 3% of each run, Pallas kernels for 4% -> 4%
where the time goes in v12:
time: 100 us; the launch traced here: 99.6 us
  blocking collectives  38.2 us (38%)
  starting transfers between devices  27 us (27%)
  waiting for transfers between devices  13.9 us (14%)
  Pallas kernels  13.1 us (13%)
  local copies, waits for them, and re-layouts  5.4 us (5%)
  other arithmetic  1.05 us (1%)
    all_to_all x1, blocking collectives, spread(): return lax.all_to_all(copies, axes, 0, 0)  38.2 us
    all_to_all x1, starting transfers between devices, body(): lax.all_to_all(copies.reshape(16, 8, CHUNK), 'z', 0, 0).reshape(128, CHUNK)  14.3 us
    ppermute x4, starting transfers between devices, shifted(): return lax.ppermute(block, axes, pairs)  10.8 us
    ppermute x4, waiting for transfers between devices, shifted(): return lax.ppermute(block, axes, pairs)  10 us
    pallas_call x1, Pallas kernels, finished(): pl.pallas_call(final_kernel, out_shape=(jax.ShapeDtypeStruct((512, HID),...  7.39 us
    all_to_all x1, waiting for transfers between devices, body(): lax.all_to_all(copies.reshape(16, 8, CHUNK), 'z', 0, 0).reshape(128, CHUNK)  3.89 us
    unnamed x13, local copies, waits for them, and re-layouts  3.8 us
    pallas_call x1, Pallas kernels, own_half(): pl.pallas_call(own_kernel, out_shape=(jax.ShapeDtypeStruct((count, 128),...  2.72 us
  transfers between devices with their start and end apart: 6, of which 3 were waited for; matrix products, arithmetic and copies ran while one was open for 3% of the time, Pallas kernels for 4%

profile of v12, /device:TPU:120, one launch (start us, length us, event | category | flops | bytes accessed | tf_op | source)
XLA Modules:
  0.0 99.6 jit_solution(10888039082252699527)
XLA Ops:
  0.6 0.0 copy-start.1
  0.6 0.0 copy-start.3
  0.7 0.1 pad_add_fusion.place_ref
  0.7 0.0 copy-start.4
  0.7 0.9 copy-done.4
  1.7 0.0 copy-start.5
  1.7 1.4 %shard_map.94 = bf16[128,640]{1,0:T(8,128)(2,1)} custom-call(s32[2]{0:T(128)S(1)} %pad_add_fusion.place_ref, bf16[9,16,264]{2,1,0:T(8,128)(2,1)S(1)} %bitcast.16), custom_call_target="tpu_custom_call" | custom-call | bytes 300000 | tf_op jit(solution)/shard_map/pallas_call | solution.py:42
  3.1 14.3 %all-to-all-start = ((bf16[16,8,640]{2,1,0:T(8,128)(2,1)}), bf16[16,8,640]{2,1,0:T(8,128)(2,1)S(1)}, u32[]{:S(2)}, u32[]{:S(2)}) async-start(bf16[16,8,640]{2,1,0:T(8,128)(2,1)} %bitcast.3), calls=%async_computation | async-start | bytes 327680 | tf_op jit(solution)/shard_map/all_to_all | solution.py:395
  17.4 0.9 copy.16
  18.2 0.1 copy.12
  18.4 0.8 fusion.3
  19.1 0.2 copy.13
  19.3 0.1 fusion.2.aux_ref
  19.5 0.0 copy-start
  19.5 1.0 %copy-done = f32[16,32,256]{2,1,0:T(8,128)S(1)} copy-done((f32[16,32,256]{2,1,0:T(8,128)S(1)}, f32[16,32,256]{2,1,0:T(8,128)}, u32[]{:S(2)}) %copy-start) | copy-done | bytes 524312
  20.5 0.0 copy-start.2
  20.5 0.9 copy-done.2
  21.5 1.3 %collective-permute-start = (bf16[64,640]{1,0:T(8,128)(2,1)S(1)}, bf16[64,640]{1,0:T(8,128)(2,1)S(1)}, u32[]{:S(2)}, u32[]{:S(2)}) collective-permute-start(bf16[64,640]{1,0:T(8,128)(2,1)S(1)} %get-tuple-element.25), channel_id=1, source_target_pairs={{0,1},{1,2},{2,3},{3,4},{4,5},{5,6},{6,7},{8,9},{9,10},{10,11},{11... | collective-permute-start | bytes 245768 | tf_op jit(solution)/shard_map/ppermute | solution.py:67
  22.8 1.3 %collective-permute-start.1 = (bf16[64,640]{1,0:T(8,128)(2,1)S(1)}, bf16[64,640]{1,0:T(8,128)(2,1)S(1)}, u32[]{:S(2)}, u32[]{:S(2)}) collective-permute-start(bf16[64,640]{1,0:T(8,128)(2,1)S(1)} %get-tuple-element.26), channel_id=1, source_target_pairs={{1,0},{2,1},{3,2},{4,3},{5,4},{6,5},{7,6},{9,8},{10,9},{11,10},{12... | collective-permute-start | bytes 245768 | tf_op jit(solution)/shard_map/ppermute | solution.py:67
  24.1 0.8 reshape.32
  24.9 0.1 reshape.33
  25.1 0.1 pad_add_fusion.1.half_ref
  25.1 0.0 collective-permute-done.low_ref
  25.1 2.5 %collective-permute-done.1.high_ref = bf16[64,640]{1,0:T(8,128)(2,1)S(1)} collective-permute-done((bf16[64,640]{1,0:T(8,128)(2,1)S(1)}, bf16[64,640]{1,0:T(8,128)(2,1)S(1)}, u32[]{:S(2)}, u32[]{:S(2)}) %collective-permute-start.1) | collective-permute-done | bytes 81952 | tf_op jit(solution)/shard_map/ppermute | solution.py:67
  27.7 0.0 copy-done.1
  27.7 0.0 copy-done.3
  27.7 0.1 shard_map.96
  27.8 3.9 %all-to-all-done = bf16[16,8,640]{2,1,0:T(8,128)(2,1)S(1)} async-done(((bf16[16,8,640]{2,1,0:T(8,128)(2,1)}), bf16[16,8,640]{2,1,0:T(8,128)(2,1)S(1)}, u32[]{:S(2)}, u32[]{:S(2)}) %all-to-all-start) | async-done | bytes 163872 | tf_op jit(solution)/shard_map/all_to_all | solution.py:395
  31.6 0.0 copy-done.5
  31.6 0.3 broadcast_in_dim.8
  32.0 38.2 %all_to_all.10.refs_1_.own_ref = bf16[16,128,640]{2,1,0:T(8,128)(2,1)S(1)} all-to-all(bf16[16,128,640]{2,1,0:T(8,128)(2,1)S(1)} %broadcast_in_dim.8), channel_id=1, replica_groups=mesh['z'=16,'y'=4,'x'=4,'c'=2] {'y','x'}, dimensions={0} | all-to-all | bytes 5242880 | tf_op jit(solution)/shard_map/all_to_all | solution.py:56
  70.2 1.9 %collective-permute-start.4 = (bf16[16,128,640]{2,1,0:T(8,128)(2,1)S(1)}, bf16[16,128,640]{2,1,0:T(8,128)(2,1)S(1)}, u32[]{:S(2)}, u32[]{:S(2)}) collective-permute-start(bf16[16,128,640]{2,1,0:T(8,128)(2,1)S(1)} %all_to_all.10.refs_1_.own_ref), channel_id=1, source_target_pairs={{0,1},{1,0},{2,3},{3,2},{4,5},{5,4},{6,7},{7,6},{8,9},{9,8},{10,11... | collective-permute-start | bytes 7864328 | tf_op jit(solution)/shard_map/ppermute | solution.py:61
  72.1 6.3 %collective-permute-start.2 = (bf16[48,640]{1,0:T(8,128)(2,1)S(1)}, bf16[48,640]{1,0:T(8,128)(2,1)S(1)}, u32[]{:S(2)}, u32[]{:S(2)}) collective-permute-start(bf16[48,640]{1,0:T(8,128)(2,1)S(1)} %get-tuple-element.33), channel_id=1, source_target_pairs={{0,8},{8,16},{16,24},{24,32},{32,40},{40,48},{48,56},{56,64},{64,7... | collective-permute-start | bytes 184328 | tf_op jit(solution)/shard_map/ppermute | solution.py:67
  78.4 1.9 %collective-permute-start.3 = (bf16[48,640]{1,0:T(8,128)(2,1)S(1)}, bf16[48,640]{1,0:T(8,128)(2,1)S(1)}, u32[]{:S(2)}, u32[]{:S(2)}) collective-permute-start(bf16[48,640]{1,0:T(8,128)(2,1)S(1)} %get-tuple-element.34), channel_id=1, source_target_pairs={{8,0},{16,8},{24,16},{32,24},{40,32},{48,40},{56,48},{64,56},{72,6... | collective-permute-start | bytes 184328 | tf_op jit(solution)/shard_map/ppermute | solution.py:67
  80.4 0.0 collective-permute-done.2.left_ref
  80.4 7.5 %collective-permute-done.3.right_ref = bf16[48,640]{1,0:T(8,128)(2,1)S(1)} collective-permute-done((bf16[48,640]{1,0:T(8,128)(2,1)S(1)}, bf16[48,640]{1,0:T(8,128)(2,1)S(1)}, u32[]{:S(2)}, u32[]{:S(2)}) %collective-permute-start.3) | collective-permute-done | bytes 61472 | tf_op jit(solution)/shard_map/ppermute | solution.py:67
  87.9 1.6 %shard_map.97 = (bf16[624,2560]{1,0:T(8,128)(2,1)S(1)}, bf16[512,256]{1,0:T(8,128)(2,1)S(1)}, f32[624,256]{1,0:T(8,128)S(1)}, f32[624,128]{1,0:T(8,128)S(1)}) custom-call(bf16[16,32,256]{2,1,0:T(8,128)(2,1)S(1)} %copy-done.3, f32[16,32,256]{2,1,0:T(8,128)S(1)} %copy-done.1, bf16[16,32,128]{2,1,0:T(8,128)(2,1)S(1)} %fusion.2.aux_ref, ...), custom_call_target="tpu_custom_call" | custom-call | bytes 100000 | tf_op jit(solution)/shard_map/pallas_call | solution.py:192
  89.4 2.7 %shard_map.98 = (bf16[624,128]{1,0:T(8,128)(2,1)S(1)}, f32[624,128]{1,0:T(8,128)S(1)}) custom-call(s32[2]{0:T(128)S(1)} %pad_add_fusion.1.half_ref, bf16[624,2560]{1,0:T(8,128)(2,1)S(1)} %get-tuple-element.35.refs_0_.patches_ref, bf16[16,128,640]{2,1,0:T(8,128)(2,1)S(1)} %all_to_all.10.refs_1_.own_ref, f32[2,4,128]{2,1,0:T(4,128)S(1)} %reverse_select_fusion.refs_2_.bias_ref, ...), custom_call_target="tpu_custom_call" | custom-call | flops 1635778560 | bytes 6000000 | tf_op jit(solution)/shard_map/pallas_call | solution.py:282
  92.2 0.0 collective-permute-done.4.other_ref
  92.2 7.4 %shard_map.99 = (bf16[512,256]{1,0:T(8,128)(2,1)}, f32[512,256]{1,0:T(8,128)}, f32[16,32]{1,0:T(8,128)}) custom-call(s32[2]{0:T(128)S(1)} %pad_add_fusion.1.half_ref, bf16[624,2560]{1,0:T(8,128)(2,1)S(1)} %get-tuple-element.35.refs_0_.patches_ref, bf16[16,128,640]{2,1,0:T(8,128)(2,1)S(1)} %all_to_all.10.refs_1_.own_ref, ...), custom_call_target="tpu_custom_call" | custom-call | flops 4320133120 | bytes 14000000 | tf_op jit(solution)/shard_map/pallas_call | solution.py:350
  (4 shorter events, 0.0 us)
Async XLA Ops:
  0.6 27.0 %copy-start.1 = (f32[16,32,256]{2,1,0:T(8,128)S(1)}, f32[16,32,256]{2,1,0:T(8,128)}, u32[]{:S(2)}) copy-start(f32[16,32,256]{2,1,0:T(8,128)} %cell_ref.5) | copy-start | bytes 1572868
  0.6 27.0 %copy-start.3 = (bf16[16,32,256]{2,1,0:T(8,128)(2,1)S(1)}, bf16[16,32,256]{2,1,0:T(8,128)(2,1)}, u32[]{:S(2)}) copy-start(bf16[16,32,256]{2,1,0:T(8,128)(2,1)} %hidden_ref.5) | copy-start | bytes 786436
  0.7 1.0 copy-start.4
  1.7 30.0 %copy-start.5 = (bf16[256]{0:T(256)(128)(2,1)S(1)}, bf16[256]{0:T(256)(128)(2,1)}, u32[]{:S(2)}) copy-start(bf16[256]{0:T(256)(128)(2,1)} %param.13) | copy-start | bytes 1540
  3.1 28.6 %all-to-all-start = ((bf16[16,8,640]{2,1,0:T(8,128)(2,1)}), bf16[16,8,640]{2,1,0:T(8,128)(2,1)S(1)}, u32[]{:S(2)}, u32[]{:S(2)}) async-start(bf16[16,8,640]{2,1,0:T(8,128)(2,1)} %bitcast.3), calls=%async_computation | async-start | bytes 327680 | tf_op jit(solution)/shard_map/all_to_all | solution.py:395
  19.5 1.0 %copy-start = (f32[16,32,256]{2,1,0:T(8,128)S(1)}, f32[16,32,256]{2,1,0:T(8,128)}, u32[]{:S(2)}) copy-start(f32[16,32,256]{2,1,0:T(8,128)} %cell_ref.5) | copy-start | bytes 1572868
  20.5 0.9 copy-start.2
  21.5 3.7 %collective-permute-start = (bf16[64,640]{1,0:T(8,128)(2,1)S(1)}, bf16[64,640]{1,0:T(8,128)(2,1)S(1)}, u32[]{:S(2)}, u32[]{:S(2)}) collective-permute-start(bf16[64,640]{1,0:T(8,128)(2,1)S(1)} %get-tuple-element.25), channel_id=1, source_target_pairs={{0,1},{1,2},{2,3},{3,4},{4,5},{5,6},{6,7},{8,9},{9,10},{10,11},{11... | collective-permute-start | bytes 245768 | tf_op jit(solution)/shard_map/ppermute | solution.py:67
  22.8 4.9 %collective-permute-start.1 = (bf16[64,640]{1,0:T(8,128)(2,1)S(1)}, bf16[64,640]{1,0:T(8,128)(2,1)S(1)}, u32[]{:S(2)}, u32[]{:S(2)}) collective-permute-start(bf16[64,640]{1,0:T(8,128)(2,1)S(1)} %get-tuple-element.26), channel_id=1, source_target_pairs={{1,0},{2,1},{3,2},{4,3},{5,4},{6,5},{7,6},{9,8},{10,9},{11,10},{12... | collective-permute-start | bytes 245768 | tf_op jit(solution)/shard_map/ppermute | solution.py:67
  70.2 22.0 %collective-permute-start.4 = (bf16[16,128,640]{2,1,0:T(8,128)(2,1)S(1)}, bf16[16,128,640]{2,1,0:T(8,128)(2,1)S(1)}, u32[]{:S(2)}, u32[]{:S(2)}) collective-permute-start(bf16[16,128,640]{2,1,0:T(8,128)(2,1)S(1)} %all_to_all.10.refs_1_.own_ref), channel_id=1, source_target_pairs={{0,1},{1,0},{2,3},{3,2},{4,5},{5,4},{6,7},{7,6},{8,9},{9,8},{10,11... | collective-permute-start | bytes 7864328 | tf_op jit(solution)/shard_map/ppermute | solution.py:61
  72.1 8.3 %collective-permute-start.2 = (bf16[48,640]{1,0:T(8,128)(2,1)S(1)}, bf16[48,640]{1,0:T(8,128)(2,1)S(1)}, u32[]{:S(2)}, u32[]{:S(2)}) collective-permute-start(bf16[48,640]{1,0:T(8,128)(2,1)S(1)} %get-tuple-element.33), channel_id=1, source_target_pairs={{0,8},{8,16},{16,24},{24,32},{32,40},{40,48},{48,56},{56,64},{64,7... | collective-permute-start | bytes 184328 | tf_op jit(solution)/shard_map/ppermute | solution.py:67
  78.4 9.4 %collective-permute-start.3 = (bf16[48,640]{1,0:T(8,128)(2,1)S(1)}, bf16[48,640]{1,0:T(8,128)(2,1)S(1)}, u32[]{:S(2)}, u32[]{:S(2)}) collective-permute-start(bf16[48,640]{1,0:T(8,128)(2,1)S(1)} %get-tuple-element.34), channel_id=1, source_target_pairs={{8,0},{16,8},{24,16},{32,24},{40,32},{48,40},{56,48},{64,56},{72,6... | collective-permute-start | bytes 184328 | tf_op jit(solution)/shard_map/ppermute | solution.py:67

commit v13 on v12

--- a/solution.py
+++ b/solution.py
@@ -410,6 +410,7 @@
     own, last, first = lax.optimization_barrier((own, last, first))
     left = shifted(last, ("z", "y"), 1)
     right = shifted(first, ("z", "y"), -1)
+    own, left, right = lax.optimization_barrier((own, left, right))
     prep = prepared(cx, *state, low, high, left, right)
     swapped = lambda piece: turned(piece, "c", 1)
     return compute(halves, own, swapped, prep, land_mask, bias2, proj)

time: 100 us -> 101 us (1.010)
  the two profiles are of different devices: /device:TPU:120 before, /device:TPU:121 now
where the time goes in v13:
time: 101 us; the launch traced here: 100 us
  blocking collectives  36.8 us (36%)
  starting transfers between devices  33.6 us (33%)
  Pallas kernels  13.1 us (13%)
  waiting for transfers between devices  9.64 us (10%)
  local copies, waits for them, and re-layouts  5.4 us (5%)
  other arithmetic  1.05 us (1%)
    all_to_all x1, blocking collectives, spread(): return lax.all_to_all(copies, axes, 0, 0)  36.8 us
    ppermute x4, starting transfers between devices, shifted(): return lax.ppermute(block, axes, pairs)  15.9 us
    all_to_all x1, starting transfers between devices, body(): lax.all_to_all(copies.reshape(16, 8, CHUNK), 'z', 0, 0).reshape(128, CHUNK)  13.7 us
    ppermute x4, waiting for transfers between devices, shifted(): return lax.ppermute(block, axes, pairs)  9.41 us
    pallas_call x1, Pallas kernels, finished(): pl.pallas_call(final_kernel, out_shape=(jax.ShapeDtypeStruct((512, HID),...  7.39 us
    ppermute x1, starting transfers between devices, turned(): lax.ppermute(block, axis, [(i, (i + step) % count) for i in range(count)])  4.02 us
    unnamed x13, local copies, waits for them, and re-layouts  3.8 us
    pallas_call x1, Pallas kernels, own_half(): pl.pallas_call(own_kernel, out_shape=(jax.ShapeDtypeStruct((count, 128),...  2.71 us
  transfers between devices with their start and end apart: 6, of which 3 were waited for; matrix products, arithmetic and copies ran while one was open for 3% of the time, Pallas kernels for 4%

profile of v13, /device:TPU:121, one launch (start us, length us, event | category | flops | bytes accessed | tf_op | source)
XLA Modules:
  0.0 100.4 jit_solution(10430094569606809376)
XLA Ops:
  0.6 0.0 copy-start.1
  0.6 0.0 copy-start.3
  0.7 0.1 pad_add_fusion.place_ref
  0.7 0.0 copy-start.4
  0.7 0.9 copy-done.4
  1.7 0.0 copy-start.5
  1.7 1.4 %shard_map.94 = bf16[128,640]{1,0:T(8,128)(2,1)} custom-call(s32[2]{0:T(128)S(1)} %pad_add_fusion.place_ref, bf16[9,16,264]{2,1,0:T(8,128)(2,1)S(1)} %bitcast.16), custom_call_target="tpu_custom_call" | custom-call | bytes 300000 | tf_op jit(solution)/shard_map/pallas_call | solution.py:42
  3.1 13.7 %all-to-all-start = ((bf16[16,8,640]{2,1,0:T(8,128)(2,1)}), bf16[16,8,640]{2,1,0:T(8,128)(2,1)S(1)}, u32[]{:S(2)}, u32[]{:S(2)}) async-start(bf16[16,8,640]{2,1,0:T(8,128)(2,1)} %bitcast.3), calls=%async_computation | async-start | bytes 327680 | tf_op jit(solution)/shard_map/all_to_all | solution.py:395
  16.8 0.9 copy.16
  17.7 0.1 copy.12
  17.8 0.8 fusion.3
  18.6 0.2 copy.13
  18.8 0.1 fusion.2.aux_ref
  18.9 0.0 copy-start
  18.9 1.0 %copy-done = f32[16,32,256]{2,1,0:T(8,128)S(1)} copy-done((f32[16,32,256]{2,1,0:T(8,128)S(1)}, f32[16,32,256]{2,1,0:T(8,128)}, u32[]{:S(2)}) %copy-start) | copy-done | bytes 524312
  19.9 0.0 copy-start.2
  19.9 0.9 copy-done.2
  20.9 4.2 %collective-permute-start = (bf16[64,640]{1,0:T(8,128)(2,1)S(1)}, bf16[64,640]{1,0:T(8,128)(2,1)S(1)}, u32[]{:S(2)}, u32[]{:S(2)}) collective-permute-start(bf16[64,640]{1,0:T(8,128)(2,1)S(1)} %get-tuple-element.28), channel_id=1, source_target_pairs={{0,1},{1,2},{2,3},{3,4},{4,5},{5,6},{6,7},{8,9},{9,10},{10,11},{11... | collective-permute-start | bytes 245768 | tf_op jit(solution)/shard_map/ppermute | solution.py:67
  25.2 1.9 %collective-permute-start.1 = (bf16[64,640]{1,0:T(8,128)(2,1)S(1)}, bf16[64,640]{1,0:T(8,128)(2,1)S(1)}, u32[]{:S(2)}, u32[]{:S(2)}) collective-permute-start(bf16[64,640]{1,0:T(8,128)(2,1)S(1)} %get-tuple-element.29), channel_id=1, source_target_pairs={{1,0},{2,1},{3,2},{4,3},{5,4},{6,5},{7,6},{9,8},{10,9},{11,10},{12... | collective-permute-start | bytes 245768 | tf_op jit(solution)/shard_map/ppermute | solution.py:67
  27.1 0.8 reshape.32
  28.0 0.1 reshape.33
  28.1 0.1 pad_add_fusion.1.half_ref
  28.2 0.0 collective-permute-done.low_ref
  28.2 3.1 %collective-permute-done.1.high_ref = bf16[64,640]{1,0:T(8,128)(2,1)S(1)} collective-permute-done((bf16[64,640]{1,0:T(8,128)(2,1)S(1)}, bf16[64,640]{1,0:T(8,128)(2,1)S(1)}, u32[]{:S(2)}, u32[]{:S(2)}) %collective-permute-start.1) | collective-permute-done | bytes 81952 | tf_op jit(solution)/shard_map/ppermute | solution.py:67
  31.2 0.0 copy-done.1
  31.2 0.0 copy-done.3
  31.2 0.1 shard_map.96
  31.3 0.0 all-to-all-done
  31.3 0.0 copy-done.5
  31.3 0.3 broadcast_in_dim.8
  31.6 36.8 %all_to_all.10.refs_1_.own_ref = bf16[16,128,640]{2,1,0:T(8,128)(2,1)S(1)} all-to-all(bf16[16,128,640]{2,1,0:T(8,128)(2,1)S(1)} %broadcast_in_dim.8), channel_id=1, replica_groups=mesh['z'=16,'y'=4,'x'=4,'c'=2] {'y','x'}, dimensions={0} | all-to-all | bytes 5242880 | tf_op jit(solution)/shard_map/all_to_all | solution.py:56
  68.4 7.8 %collective-permute-start.2 = (bf16[48,640]{1,0:T(8,128)(2,1)S(1)}, bf16[48,640]{1,0:T(8,128)(2,1)S(1)}, u32[]{:S(2)}, u32[]{:S(2)}) collective-permute-start(bf16[48,640]{1,0:T(8,128)(2,1)S(1)} %get-tuple-element.37), channel_id=1, source_target_pairs={{0,8},{8,16},{16,24},{24,32},{32,40},{40,48},{48,56},{56,64},{64,7... | collective-permute-start | bytes 184328 | tf_op jit(solution)/shard_map/ppermute | solution.py:67
  76.2 1.9 %collective-permute-start.3 = (bf16[48,640]{1,0:T(8,128)(2,1)S(1)}, bf16[48,640]{1,0:T(8,128)(2,1)S(1)}, u32[]{:S(2)}, u32[]{:S(2)}) collective-permute-start(bf16[48,640]{1,0:T(8,128)(2,1)S(1)} %get-tuple-element.38), channel_id=1, source_target_pairs={{8,0},{16,8},{24,16},{32,24},{40,32},{48,40},{56,48},{64,56},{72,6... | collective-permute-start | bytes 184328 | tf_op jit(solution)/shard_map/ppermute | solution.py:67
  78.2 0.0 collective-permute-done.2.left_ref
  78.2 6.3 %collective-permute-done.3.right_ref = bf16[48,640]{1,0:T(8,128)(2,1)S(1)} collective-permute-done((bf16[48,640]{1,0:T(8,128)(2,1)S(1)}, bf16[48,640]{1,0:T(8,128)(2,1)S(1)}, u32[]{:S(2)}, u32[]{:S(2)}) %collective-permute-start.3) | collective-permute-done | bytes 61472 | tf_op jit(solution)/shard_map/ppermute | solution.py:67
  84.5 4.0 %collective-permute-start.4 = (bf16[16,128,640]{2,1,0:T(8,128)(2,1)S(1)}, bf16[16,128,640]{2,1,0:T(8,128)(2,1)S(1)}, u32[]{:S(2)}, u32[]{:S(2)}) collective-permute-start(bf16[16,128,640]{2,1,0:T(8,128)(2,1)S(1)} %all_to_all.10.refs_1_.own_ref), channel_id=1, source_target_pairs={{0,1},{1,0},{2,3},{3,2},{4,5},{5,4},{6,7},{7,6},{8,9},{9,8},{10,11... | collective-permute-start | bytes 7864328 | tf_op jit(solution)/shard_map/ppermute | solution.py:61
  88.5 1.6 %shard_map.97 = (bf16[624,2560]{1,0:T(8,128)(2,1)S(1)}, bf16[512,256]{1,0:T(8,128)(2,1)S(1)}, f32[624,256]{1,0:T(8,128)S(1)}, f32[624,128]{1,0:T(8,128)S(1)}) custom-call(bf16[16,32,256]{2,1,0:T(8,128)(2,1)S(1)} %copy-done.3, f32[16,32,256]{2,1,0:T(8,128)S(1)} %copy-done.1, bf16[16,32,128]{2,1,0:T(8,128)(2,1)S(1)} %fusion.2.aux_ref, ...), custom_call_target="tpu_custom_call" | custom-call | bytes 100000 | tf_op jit(solution)/shard_map/pallas_call | solution.py:192
  90.1 2.7 %shard_map.98 = (bf16[624,128]{1,0:T(8,128)(2,1)S(1)}, f32[624,128]{1,0:T(8,128)S(1)}) custom-call(s32[2]{0:T(128)S(1)} %pad_add_fusion.1.half_ref, bf16[624,2560]{1,0:T(8,128)(2,1)S(1)} %get-tuple-element.41.refs_0_.patches_ref, bf16[16,128,640]{2,1,0:T(8,128)(2,1)S(1)} %all_to_all.10.refs_1_.own_ref, f32[2,4,128]{2,1,0:T(4,128)S(1)} %reverse_select_fusion.refs_2_.bias_ref, ...), custom_call_target="tpu_custom_call" | custom-call | flops 1635778560 | bytes 6000000 | tf_op jit(solution)/shard_map/pallas_call | solution.py:282
  92.8 0.2 collective-permute-done.4.other_ref
  93.0 7.4 %shard_map.99 = (bf16[512,256]{1,0:T(8,128)(2,1)}, f32[512,256]{1,0:T(8,128)}, f32[16,32]{1,0:T(8,128)}) custom-call(s32[2]{0:T(128)S(1)} %pad_add_fusion.1.half_ref, bf16[624,2560]{1,0:T(8,128)(2,1)S(1)} %get-tuple-element.41.refs_0_.patches_ref, bf16[16,128,640]{2,1,0:T(8,128)(2,1)S(1)} %all_to_all.10.refs_1_.own_ref, ...), custom_call_target="tpu_custom_call" | custom-call | flops 4320133120 | bytes 14000000 | tf_op jit(solution)/shard_map/pallas_call | solution.py:350
  (4 shorter events, 0.0 us)
Async XLA Ops:
  0.6 30.6 %copy-start.1 = (f32[16,32,256]{2,1,0:T(8,128)S(1)}, f32[16,32,256]{2,1,0:T(8,128)}, u32[]{:S(2)}) copy-start(f32[16,32,256]{2,1,0:T(8,128)} %cell_ref.5) | copy-start | bytes 1572868
  0.6 30.6 %copy-start.3 = (bf16[16,32,256]{2,1,0:T(8,128)(2,1)S(1)}, bf16[16,32,256]{2,1,0:T(8,128)(2,1)}, u32[]{:S(2)}) copy-start(bf16[16,32,256]{2,1,0:T(8,128)(2,1)} %hidden_ref.5) | copy-start | bytes 786436
  0.7 1.0 copy-start.4
  1.7 29.6 %copy-start.5 = (bf16[256]{0:T(256)(128)(2,1)S(1)}, bf16[256]{0:T(256)(128)(2,1)}, u32[]{:S(2)}) copy-start(bf16[256]{0:T(256)(128)(2,1)} %param.13) | copy-start | bytes 1540
  3.1 28.2 %all-to-all-start = ((bf16[16,8,640]{2,1,0:T(8,128)(2,1)}), bf16[16,8,640]{2,1,0:T(8,128)(2,1)S(1)}, u32[]{:S(2)}, u32[]{:S(2)}) async-start(bf16[16,8,640]{2,1,0:T(8,128)(2,1)} %bitcast.3), calls=%async_computation | async-start | bytes 327680 | tf_op jit(solution)/shard_map/all_to_all | solution.py:395
  18.9 1.0 %copy-start = (f32[16,32,256]{2,1,0:T(8,128)S(1)}, f32[16,32,256]{2,1,0:T(8,128)}, u32[]{:S(2)}) copy-start(f32[16,32,256]{2,1,0:T(8,128)} %cell_ref.5) | copy-start | bytes 1572868
  19.9 0.9 copy-start.2
  20.9 7.2 %collective-permute-start = (bf16[64,640]{1,0:T(8,128)(2,1)S(1)}, bf16[64,640]{1,0:T(8,128)(2,1)S(1)}, u32[]{:S(2)}, u32[]{:S(2)}) collective-permute-start(bf16[64,640]{1,0:T(8,128)(2,1)S(1)} %get-tuple-element.28), channel_id=1, source_target_pairs={{0,1},{1,2},{2,3},{3,4},{4,5},{5,6},{6,7},{8,9},{9,10},{10,11},{11... | collective-permute-start | bytes 245768 | tf_op jit(solution)/shard_map/ppermute | solution.py:67
  25.2 6.1 %collective-permute-start.1 = (bf16[64,640]{1,0:T(8,128)(2,1)S(1)}, bf16[64,640]{1,0:T(8,128)(2,1)S(1)}, u32[]{:S(2)}, u32[]{:S(2)}) collective-permute-start(bf16[64,640]{1,0:T(8,128)(2,1)S(1)} %get-tuple-element.29), channel_id=1, source_target_pairs={{1,0},{2,1},{3,2},{4,3},{5,4},{6,5},{7,6},{9,8},{10,9},{11,10},{12... | collective-permute-start | bytes 245768 | tf_op jit(solution)/shard_map/ppermute | solution.py:67
  68.4 9.7 %collective-permute-start.2 = (bf16[48,640]{1,0:T(8,128)(2,1)S(1)}, bf16[48,640]{1,0:T(8,128)(2,1)S(1)}, u32[]{:S(2)}, u32[]{:S(2)}) collective-permute-start(bf16[48,640]{1,0:T(8,128)(2,1)S(1)} %get-tuple-element.37), channel_id=1, source_target_pairs={{0,8},{8,16},{16,24},{24,32},{32,40},{40,48},{48,56},{56,64},{64,7... | collective-permute-start | bytes 184328 | tf_op jit(solution)/shard_map/ppermute | solution.py:67
  76.2 8.3 %collective-permute-start.3 = (bf16[48,640]{1,0:T(8,128)(2,1)S(1)}, bf16[48,640]{1,0:T(8,128)(2,1)S(1)}, u32[]{:S(2)}, u32[]{:S(2)}) collective-permute-start(bf16[48,640]{1,0:T(8,128)(2,1)S(1)} %get-tuple-element.38), channel_id=1, source_target_pairs={{8,0},{16,8},{24,16},{32,24},{40,32},{48,40},{56,48},{64,56},{72,6... | collective-permute-start | bytes 184328 | tf_op jit(solution)/shard_map/ppermute | solution.py:67
  84.5 8.5 %collective-permute-start.4 = (bf16[16,128,640]{2,1,0:T(8,128)(2,1)S(1)}, bf16[16,128,640]{2,1,0:T(8,128)(2,1)S(1)}, u32[]{:S(2)}, u32[]{:S(2)}) collective-permute-start(bf16[16,128,640]{2,1,0:T(8,128)(2,1)S(1)} %all_to_all.10.refs_1_.own_ref), channel_id=1, source_target_pairs={{0,1},{1,0},{2,3},{3,2},{4,5},{5,4},{6,7},{7,6},{8,9},{9,8},{10,11... | collective-permute-start | bytes 7864328 | tf_op jit(solution)/shard_map/ppermute | solution.py:61

commit v14 on v12

--- a/solution.py
+++ b/solution.py
@@ -399,17 +399,16 @@
     low = shifted(last, ("x", "c"), 1)
     high = shifted(first, ("x", "c"), -1)
     last, first = sides_of(*state, low, high)
+    left = shifted(last, ("z", "y"), 1)
+    right = shifted(first, ("z", "y"), -1)
     halves = jnp.stack([c, 1 - c]).astype(jnp.int32)
     proj = jnp.broadcast_to(projection[None], (16, HID))
     bias2 = bias_of(bias, c)
-    by_z, last, first, halves, proj, bias2 = lax.optimization_barrier(
-        (by_z, last, first, halves, proj, bias2)
+    by_z, left, right, halves, proj, bias2 = lax.optimization_barrier(
+        (by_z, left, right, halves, proj, bias2)
     )
 
     own = spread(by_z, ("y", "x"))
-    own, last, first = lax.optimization_barrier((own, last, first))
-    left = shifted(last, ("z", "y"), 1)
-    right = shifted(first, ("z", "y"), -1)
     prep = prepared(cx, *state, low, high, left, right)
     swapped = lambda piece: turned(piece, "c", 1)
     return compute(halves, own, swapped, prep, land_mask, bias2, proj)

time: 100 us -> 99.7 us (level)
  the two profiles are of different devices: /device:TPU:120 before, /device:TPU:97 now
where the time goes in v14:
time: 99.7 us; the launch traced here: 99.1 us
  blocking collectives  43.2 us (43%)
  starting transfers between devices  31 us (31%)
  Pallas kernels  13.1 us (13%)
  local copies, waits for them, and re-layouts  5.4 us (5%)
  waiting for transfers between devices  4.55 us (5%)
  other arithmetic  1.05 us (1%)
    all_to_all x1, blocking collectives, spread(): return lax.all_to_all(copies, axes, 0, 0)  43.2 us
    all_to_all x1, starting transfers between devices, body(): lax.all_to_all(copies.reshape(16, 8, CHUNK), 'z', 0, 0).reshape(128, CHUNK)  13.7 us
    ppermute x4, starting transfers between devices, shifted(): return lax.ppermute(block, axes, pairs)  13.6 us
    pallas_call x1, Pallas kernels, finished(): pl.pallas_call(final_kernel, out_shape=(jax.ShapeDtypeStruct((512, HID),...  7.39 us
    ppermute x4, waiting for transfers between devices, shifted(): return lax.ppermute(block, axes, pairs)  4.32 us
    unnamed x13, local copies, waits for them, and re-layouts  3.8 us
    ppermute x1, starting transfers between devices, turned(): lax.ppermute(block, axis, [(i, (i + step) % count) for i in range(count)])  3.69 us
    pallas_call x1, Pallas kernels, own_half(): pl.pallas_call(own_kernel, out_shape=(jax.ShapeDtypeStruct((count, 128),...  2.72 us
  transfers between devices with their start and end apart: 6, of which 3 were waited for; matrix products, arithmetic and copies ran while one was open for 3% of the time, Pallas kernels for 4%

profile of v14, /device:TPU:97, one launch (start us, length us, event | category | flops | bytes accessed | tf_op | source)
XLA Modules:
  0.0 99.1 jit_solution(16969179974184189920)
XLA Ops:
  0.6 0.0 copy-start.1
  0.6 0.0 copy-start.3
  0.7 0.1 pad_add_fusion.place_ref
  0.7 0.0 copy-start.4
  0.7 0.9 copy-done.4
  1.7 0.0 copy-start.5
  1.7 1.4 %shard_map.94 = bf16[128,640]{1,0:T(8,128)(2,1)} custom-call(s32[2]{0:T(128)S(1)} %pad_add_fusion.place_ref, bf16[9,16,264]{2,1,0:T(8,128)(2,1)S(1)} %bitcast.16), custom_call_target="tpu_custom_call" | custom-call | bytes 300000 | tf_op jit(solution)/shard_map/pallas_call | solution.py:42
  3.1 13.7 %all-to-all-start = ((bf16[16,8,640]{2,1,0:T(8,128)(2,1)}), bf16[16,8,640]{2,1,0:T(8,128)(2,1)S(1)}, u32[]{:S(2)}, u32[]{:S(2)}) async-start(bf16[16,8,640]{2,1,0:T(8,128)(2,1)} %bitcast.3), calls=%async_computation | async-start | bytes 327680 | tf_op jit(solution)/shard_map/all_to_all | solution.py:395
  16.8 0.9 copy.16
  17.7 0.1 copy.12
  17.8 0.8 fusion.3
  18.6 0.2 copy.13
  18.8 0.1 fusion.2.aux_ref
  18.9 0.0 copy-start
  18.9 1.0 %copy-done = f32[16,32,256]{2,1,0:T(8,128)S(1)} copy-done((f32[16,32,256]{2,1,0:T(8,128)S(1)}, f32[16,32,256]{2,1,0:T(8,128)}, u32[]{:S(2)}) %copy-start) | copy-done | bytes 524312
  19.9 0.0 copy-start.2
  19.9 0.9 copy-done.2
  20.9 4.2 %collective-permute-start = (bf16[64,640]{1,0:T(8,128)(2,1)S(1)}, bf16[64,640]{1,0:T(8,128)(2,1)S(1)}, u32[]{:S(2)}, u32[]{:S(2)}) collective-permute-start(bf16[64,640]{1,0:T(8,128)(2,1)S(1)} %get-tuple-element.22), channel_id=1, source_target_pairs={{0,1},{1,2},{2,3},{3,4},{4,5},{5,6},{6,7},{8,9},{9,10},{10,11},{11... | collective-permute-start | bytes 245768 | tf_op jit(solution)/shard_map/ppermute | solution.py:67
  25.2 1.9 %collective-permute-start.1 = (bf16[64,640]{1,0:T(8,128)(2,1)S(1)}, bf16[64,640]{1,0:T(8,128)(2,1)S(1)}, u32[]{:S(2)}, u32[]{:S(2)}) collective-permute-start(bf16[64,640]{1,0:T(8,128)(2,1)S(1)} %get-tuple-element.23), channel_id=1, source_target_pairs={{1,0},{2,1},{3,2},{4,3},{5,4},{6,5},{7,6},{9,8},{10,9},{11,10},{12... | collective-permute-start | bytes 245768 | tf_op jit(solution)/shard_map/ppermute | solution.py:67
  27.1 0.8 reshape.32
  28.0 0.1 reshape.33
  28.1 0.0 collective-permute-done.low_ref
  28.1 3.1 %collective-permute-done.1.high_ref = bf16[64,640]{1,0:T(8,128)(2,1)S(1)} collective-permute-done((bf16[64,640]{1,0:T(8,128)(2,1)S(1)}, bf16[64,640]{1,0:T(8,128)(2,1)S(1)}, u32[]{:S(2)}, u32[]{:S(2)}) %collective-permute-start.1) | collective-permute-done | bytes 81952 | tf_op jit(solution)/shard_map/ppermute | solution.py:67
  31.2 0.0 copy-done.1
  31.2 0.0 copy-done.3
  31.2 0.1 shard_map.96
  31.3 3.2 %collective-permute-start.2 = (bf16[48,640]{1,0:T(8,128)(2,1)S(1)}, bf16[48,640]{1,0:T(8,128)(2,1)S(1)}, u32[]{:S(2)}, u32[]{:S(2)}) collective-permute-start(bf16[48,640]{1,0:T(8,128)(2,1)S(1)} %get-tuple-element.24), channel_id=1, source_target_pairs={{0,8},{8,16},{16,24},{24,32},{32,40},{40,48},{48,56},{56,64},{64,7... | collective-permute-start | bytes 184328 | tf_op jit(solution)/shard_map/ppermute | solution.py:67
  34.5 4.2 %collective-permute-start.3 = (bf16[48,640]{1,0:T(8,128)(2,1)S(1)}, bf16[48,640]{1,0:T(8,128)(2,1)S(1)}, u32[]{:S(2)}, u32[]{:S(2)}) collective-permute-start(bf16[48,640]{1,0:T(8,128)(2,1)S(1)} %get-tuple-element.25), channel_id=1, source_target_pairs={{8,0},{16,8},{24,16},{32,24},{40,32},{48,40},{56,48},{64,56},{72,6... | collective-permute-start | bytes 184328 | tf_op jit(solution)/shard_map/ppermute | solution.py:67
  38.7 0.1 pad_add_fusion.1.half_ref
  38.8 0.0 collective-permute-done.2.left_ref
  38.8 1.2 %collective-permute-done.3.right_ref = bf16[48,640]{1,0:T(8,128)(2,1)S(1)} collective-permute-done((bf16[48,640]{1,0:T(8,128)(2,1)S(1)}, bf16[48,640]{1,0:T(8,128)(2,1)S(1)}, u32[]{:S(2)}, u32[]{:S(2)}) %collective-permute-start.3) | collective-permute-done | bytes 61472 | tf_op jit(solution)/shard_map/ppermute | solution.py:67
  40.0 0.0 all-to-all-done
  40.0 0.0 copy-done.5
  40.0 0.3 broadcast_in_dim.8
  40.3 43.2 %all_to_all.10.refs_1_.own_ref = bf16[16,128,640]{2,1,0:T(8,128)(2,1)S(1)} all-to-all(bf16[16,128,640]{2,1,0:T(8,128)(2,1)S(1)} %broadcast_in_dim.8), channel_id=1, replica_groups=mesh['z'=16,'y'=4,'x'=4,'c'=2] {'y','x'}, dimensions={0} | all-to-all | bytes 5242880 | tf_op jit(solution)/shard_map/all_to_all | solution.py:56
  83.5 3.7 %collective-permute-start.4 = (bf16[16,128,640]{2,1,0:T(8,128)(2,1)S(1)}, bf16[16,128,640]{2,1,0:T(8,128)(2,1)S(1)}, u32[]{:S(2)}, u32[]{:S(2)}) collective-permute-start(bf16[16,128,640]{2,1,0:T(8,128)(2,1)S(1)} %all_to_all.10.refs_1_.own_ref), channel_id=1, source_target_pairs={{0,1},{1,0},{2,3},{3,2},{4,5},{5,4},{6,7},{7,6},{8,9},{9,8},{10,11... | collective-permute-start | bytes 7864328 | tf_op jit(solution)/shard_map/ppermute | solution.py:61
  87.2 1.6 %shard_map.97 = (bf16[624,2560]{1,0:T(8,128)(2,1)S(1)}, bf16[512,256]{1,0:T(8,128)(2,1)S(1)}, f32[624,256]{1,0:T(8,128)S(1)}, f32[624,128]{1,0:T(8,128)S(1)}) custom-call(bf16[16,32,256]{2,1,0:T(8,128)(2,1)S(1)} %copy-done.3, f32[16,32,256]{2,1,0:T(8,128)S(1)} %copy-done.1, bf16[16,32,128]{2,1,0:T(8,128)(2,1)S(1)} %fusion.2.aux_ref, ...), custom_call_target="tpu_custom_call" | custom-call | bytes 100000 | tf_op jit(solution)/shard_map/pallas_call | solution.py:192
  88.8 2.7 %shard_map.98 = (bf16[624,128]{1,0:T(8,128)(2,1)S(1)}, f32[624,128]{1,0:T(8,128)S(1)}) custom-call(s32[2]{0:T(128)S(1)} %pad_add_fusion.1.half_ref, bf16[624,2560]{1,0:T(8,128)(2,1)S(1)} %get-tuple-element.29.refs_0_.patches_ref, bf16[16,128,640]{2,1,0:T(8,128)(2,1)S(1)} %all_to_all.10.refs_1_.own_ref, f32[2,4,128]{2,1,0:T(4,128)S(1)} %reverse_select_fusion.refs_2_.bias_ref, ...), custom_call_target="tpu_custom_call" | custom-call | flops 1635778560 | bytes 6000000 | tf_op jit(solution)/shard_map/pallas_call | solution.py:282
  91.5 0.2 collective-permute-done.4.other_ref
  91.7 7.4 %shard_map.99 = (bf16[512,256]{1,0:T(8,128)(2,1)}, f32[512,256]{1,0:T(8,128)}, f32[16,32]{1,0:T(8,128)}) custom-call(s32[2]{0:T(128)S(1)} %pad_add_fusion.1.half_ref, bf16[624,2560]{1,0:T(8,128)(2,1)S(1)} %get-tuple-element.29.refs_0_.patches_ref, bf16[16,128,640]{2,1,0:T(8,128)(2,1)S(1)} %all_to_all.10.refs_1_.own_ref, ...), custom_call_target="tpu_custom_call" | custom-call | flops 4320133120 | bytes 14000000 | tf_op jit(solution)/shard_map/pallas_call | solution.py:350
  (4 shorter events, 0.0 us)
Async XLA Ops:
  0.6 30.6 %copy-start.1 = (f32[16,32,256]{2,1,0:T(8,128)S(1)}, f32[16,32,256]{2,1,0:T(8,128)}, u32[]{:S(2)}) copy-start(f32[16,32,256]{2,1,0:T(8,128)} %cell_ref.5) | copy-start | bytes 1572868
  0.6 30.6 %copy-start.3 = (bf16[16,32,256]{2,1,0:T(8,128)(2,1)S(1)}, bf16[16,32,256]{2,1,0:T(8,128)(2,1)}, u32[]{:S(2)}) copy-start(bf16[16,32,256]{2,1,0:T(8,128)(2,1)} %hidden_ref.5) | copy-start | bytes 786436
  0.7 1.0 copy-start.4
  1.7 38.3 %copy-start.5 = (bf16[256]{0:T(256)(128)(2,1)S(1)}, bf16[256]{0:T(256)(128)(2,1)}, u32[]{:S(2)}) copy-start(bf16[256]{0:T(256)(128)(2,1)} %param.13) | copy-start | bytes 1540
  3.1 36.9 %all-to-all-start = ((bf16[16,8,640]{2,1,0:T(8,128)(2,1)}), bf16[16,8,640]{2,1,0:T(8,128)(2,1)S(1)}, u32[]{:S(2)}, u32[]{:S(2)}) async-start(bf16[16,8,640]{2,1,0:T(8,128)(2,1)} %bitcast.3), calls=%async_computation | async-start | bytes 327680 | tf_op jit(solution)/shard_map/all_to_all | solution.py:395
  18.9 1.0 %copy-start = (f32[16,32,256]{2,1,0:T(8,128)S(1)}, f32[16,32,256]{2,1,0:T(8,128)}, u32[]{:S(2)}) copy-start(f32[16,32,256]{2,1,0:T(8,128)} %cell_ref.5) | copy-start | bytes 1572868
  19.9 0.9 copy-start.2
  20.9 7.2 %collective-permute-start = (bf16[64,640]{1,0:T(8,128)(2,1)S(1)}, bf16[64,640]{1,0:T(8,128)(2,1)S(1)}, u32[]{:S(2)}, u32[]{:S(2)}) collective-permute-start(bf16[64,640]{1,0:T(8,128)(2,1)S(1)} %get-tuple-element.22), channel_id=1, source_target_pairs={{0,1},{1,2},{2,3},{3,4},{4,5},{5,6},{6,7},{8,9},{9,10},{10,11},{11... | collective-permute-start | bytes 245768 | tf_op jit(solution)/shard_map/ppermute | solution.py:67
  25.2 6.1 %collective-permute-start.1 = (bf16[64,640]{1,0:T(8,128)(2,1)S(1)}, bf16[64,640]{1,0:T(8,128)(2,1)S(1)}, u32[]{:S(2)}, u32[]{:S(2)}) collective-permute-start(bf16[64,640]{1,0:T(8,128)(2,1)S(1)} %get-tuple-element.23), channel_id=1, source_target_pairs={{1,0},{2,1},{3,2},{4,3},{5,4},{6,5},{7,6},{9,8},{10,9},{11,10},{12... | collective-permute-start | bytes 245768 | tf_op jit(solution)/shard_map/ppermute | solution.py:67
  31.3 7.5 %collective-permute-start.2 = (bf16[48,640]{1,0:T(8,128)(2,1)S(1)}, bf16[48,640]{1,0:T(8,128)(2,1)S(1)}, u32[]{:S(2)}, u32[]{:S(2)}) collective-permute-start(bf16[48,640]{1,0:T(8,128)(2,1)S(1)} %get-tuple-element.24), channel_id=1, source_target_pairs={{0,8},{8,16},{16,24},{24,32},{32,40},{40,48},{48,56},{56,64},{64,7... | collective-permute-start | bytes 184328 | tf_op jit(solution)/shard_map/ppermute | solution.py:67
  34.5 5.5 %collective-permute-start.3 = (bf16[48,640]{1,0:T(8,128)(2,1)S(1)}, bf16[48,640]{1,0:T(8,128)(2,1)S(1)}, u32[]{:S(2)}, u32[]{:S(2)}) collective-permute-start(bf16[48,640]{1,0:T(8,128)(2,1)S(1)} %get-tuple-element.25), channel_id=1, source_target_pairs={{8,0},{16,8},{24,16},{32,24},{40,32},{48,40},{56,48},{64,56},{72,6... | collective-permute-start | bytes 184328 | tf_op jit(solution)/shard_map/ppermute | solution.py:67
  83.5 8.2 %collective-permute-start.4 = (bf16[16,128,640]{2,1,0:T(8,128)(2,1)S(1)}, bf16[16,128,640]{2,1,0:T(8,128)(2,1)S(1)}, u32[]{:S(2)}, u32[]{:S(2)}) collective-permute-start(bf16[16,128,640]{2,1,0:T(8,128)(2,1)S(1)} %all_to_all.10.refs_1_.own_ref), channel_id=1, source_target_pairs={{0,1},{1,0},{2,3},{3,2},{4,5},{5,4},{6,7},{7,6},{8,9},{9,8},{10,11... | collective-permute-start | bytes 7864328 | tf_op jit(solution)/shard_map/ppermute | solution.py:61
